TPU v7x, 128 devices: a whole 4x4x4 slice. The times are simulated.
128 devices in a mesh: dx: 16 (over z, y), dy: 8 (over x, core).
Axes of the slice: x: 4, y: 4, z: 4, core: 2. Of those that a mesh axis runs over, the one named last changes fastest.
Arguments:
- charges: bfloat16 [8192, 128, 128], P(('dx', 'dy')), may hold values from -6 to 6
- basis: bfloat16 [8192, 81, 128], P(('dx', 'dy')), may hold values from -0.5 to 0.5
- leaf_count: int32 [8192], P(('dx', 'dy')), may hold values from 64 to 128, as said below
- cotangent: bfloat16 [8192, 128, 128], P(('dx', 'dy')), may hold values from -6 to 6
- m2l_ops: bfloat16 [316, 81, 81], replicated, may hold values from -0.3125 to 0.3125
- fetch_cells: int32 [128, 128, 1], P(('dx', 'dy')), may hold values from 0 to 63
- pair_target: int32 [128, 16, 32], P(('dx', 'dy')), may hold values from 0 to 63
- pair_source: int32 [128, 16, 32], P(('dx', 'dy')), may hold values from 0 to 191
- batch_class: int32 [128, 16], P(('dx', 'dy')), may hold values from 0 to 315
- batch_fill: int32 [128, 16], P(('dx', 'dy')), may hold values from 0 to 32, as said below
Outputs:
- potential: bfloat16 [8192, 128, 128], P(('dx', 'dy'))
- charge_grad: bfloat16 [8192, 128, 128], P(('dx', 'dy'))
Inputs may be any that keep to these rules, and one draw needn't show every extreme that they name: `leaf_count`: in every draw some leaf is full. `batch_fill`: in each domain the batches with a positive count come first, 4 of them or more; the first batch of every domain is full, and on some domain all batches are live.
All inputs are finite; a program needn't handle non-finite values.
Results may differ from a plain program's by a relative error of at most 0.015.
Values may be sent and summed in bfloat16 or wider, within the bound.
No kernel may reach another device: no remote copies, remote signals or barrier semaphores. Data moves between devices by JAX's collectives and lax.ppermute only.
A program may use at most 128 MiB of HBM per device.

v0:
```python
import jax
import jax.numpy as jnp
from jax import lax
from jax.sharding import PartitionSpec as P


def slot_mask(leaf_count, slot_count):
    return (
        lax.broadcasted_iota(jnp.int32, (leaf_count.shape[0], slot_count), 1) < leaf_count[:, None]
    )


def to_moments(basis, values, occupied):
    masked = jnp.where(occupied[:, :, None], values, jnp.zeros((), jnp.bfloat16))
    return jnp.einsum("iks,isc->ikc", basis, masked, preferred_element_type=jnp.float32).astype(
        jnp.bfloat16
    )


def to_atoms(basis, moments, occupied):
    result = jnp.einsum("iks,ikc->isc", basis, moments, preferred_element_type=jnp.float32)
    return jnp.where(occupied[:, :, None], result, jnp.zeros((), jnp.float32)).astype(jnp.bfloat16)


def one_hot_rows(indices, width, keep):
    columns = lax.broadcasted_iota(jnp.int32, (indices.shape[0], width), 1)
    return ((indices[:, None] == columns) & keep[:, None]).astype(jnp.bfloat16)


def select_rows(selector, table):
    return jnp.dot(selector, table, preferred_element_type=jnp.float32).astype(jnp.bfloat16)


def add_into_rows(selector, values):
    high_part = values.astype(jnp.bfloat16)
    low_part = (values - high_part.astype(jnp.float32)).astype(jnp.bfloat16)
    dims = (((0,), (0,)), ((), ()))
    first = lax.dot_general(selector, high_part, dims, preferred_element_type=jnp.float32)
    second = lax.dot_general(selector, low_part, dims, preferred_element_type=jnp.float32)
    return first + second


def local(
    charges,
    basis,
    leaf_count,
    cotangent,
    m2l_ops,
    fetch_cells,
    pair_target,
    pair_source,
    batch_class,
    batch_fill,
):
    cells_dev, coeffs, slot_count = basis.shape
    channels = charges.shape[2]
    slab_count = lax.axis_size("dx")
    column_count = lax.axis_size("dy")
    domains = slab_count * column_count
    per_peer = fetch_cells.shape[2]
    batch_count = pair_target.shape[1]
    batch_size = pair_target.shape[2]
    group_size = 8
    width = coeffs * channels
    occupied = slot_mask(leaf_count, slot_count)
    multipole = to_moments(basis, charges, occupied)
    exp_grad = to_moments(basis, cotangent, occupied)
    multipole_flat = multipole.reshape(cells_dev, width)
    exp_grad_flat = exp_grad.reshape(cells_dev, width)
    asked = lax.all_to_all(fetch_cells[0], ("dx", "dy"), split_axis=0, concat_axis=0, tiled=True)
    asked_rows = asked.reshape(-1)
    every_row = jnp.ones(asked_rows.shape, dtype=jnp.bool_)
    outgoing = select_rows(one_hot_rows(asked_rows, cells_dev, every_row), multipole_flat).reshape(
        domains * per_peer, coeffs, channels
    )
    incoming = lax.all_to_all(outgoing, ("dx", "dy"), split_axis=0, concat_axis=0, tiled=True)
    sources_flat = jnp.concatenate(
        [multipole_flat, incoming.reshape(domains * per_peer, width)], axis=0
    )
    source_total = sources_flat.shape[0]
    active_all = (
        lax.broadcasted_iota(jnp.int32, (batch_count, batch_size), 1) < batch_fill[0][:, None]
    )
    turn_count = batch_count // group_size

    def group_slices(turn_index):
        first_row = turn_index * group_size
        source_rows = lax.dynamic_slice_in_dim(pair_source[0], first_row, group_size, 0).reshape(-1)
        target_rows = lax.dynamic_slice_in_dim(pair_target[0], first_row, group_size, 0).reshape(-1)
        active = lax.dynamic_slice_in_dim(active_all, first_row, group_size, 0).reshape(-1)
        classes = lax.dynamic_slice_in_dim(batch_class[0], first_row, group_size, 0)
        return (source_rows, target_rows, active, m2l_ops[classes])

    def forward_group(turn_index, accumulated):
        source_rows, target_rows, active, chosen = group_slices(turn_index)
        picked = select_rows(one_hot_rows(source_rows, source_total, active), sources_flat)
        picked = picked.reshape(group_size, batch_size, coeffs, channels)
        products = jnp.einsum("gkl,gplc->gpkc", chosen, picked, preferred_element_type=jnp.float32)
        target_hot = one_hot_rows(target_rows, cells_dev, active)
        return accumulated + add_into_rows(target_hot, products.reshape(-1, width))

    local_exp = lax.fori_loop(
        0, turn_count, forward_group, jnp.zeros((cells_dev, width), jnp.float32)
    )
    potential = to_atoms(
        basis, local_exp.astype(jnp.bfloat16).reshape(cells_dev, coeffs, channels), occupied
    )

    def backward_group(turn_index, accumulated):
        source_rows, target_rows, active, chosen = group_slices(turn_index)
        picked = select_rows(one_hot_rows(target_rows, cells_dev, active), exp_grad_flat)
        picked = picked.reshape(group_size, batch_size, coeffs, channels)
        products = jnp.einsum("glk,gplc->gpkc", chosen, picked, preferred_element_type=jnp.float32)
        source_hot = one_hot_rows(source_rows, source_total, active)
        return accumulated + add_into_rows(source_hot, products.reshape(-1, width))

    source_grad = lax.fori_loop(
        0, turn_count, backward_group, jnp.zeros((source_total, width), jnp.float32)
    )
    remote_grads = (
        source_grad[cells_dev:].astype(jnp.bfloat16).reshape(domains * per_peer, coeffs, channels)
    )
    returned = lax.all_to_all(remote_grads, ("dx", "dy"), split_axis=0, concat_axis=0, tiled=True)
    returned = returned.reshape(domains * per_peer, width)
    selector = (asked_rows[None, :] == lax.broadcasted_iota(jnp.int32, (cells_dev, 1), 0)).astype(
        jnp.bfloat16
    )
    collected = jnp.dot(selector, returned, preferred_element_type=jnp.float32)
    mult_grad = (
        (source_grad[:cells_dev] + collected)
        .astype(jnp.bfloat16)
        .reshape(cells_dev, coeffs, channels)
    )
    charge_grad = to_atoms(basis, mult_grad, occupied)
    return (potential, charge_grad)


def solution(mesh):
    in_specs = (
        P(("dx", "dy"), None, None),
        P(("dx", "dy"), None, None),
        P(("dx", "dy")),
        P(("dx", "dy"), None, None),
        P(),
        P(("dx", "dy"), None, None),
        P(("dx", "dy"), None, None),
        P(("dx", "dy"), None, None),
        P(("dx", "dy"), None),
        P(("dx", "dy"), None),
    )
    out_specs = (P(("dx", "dy"), None, None), P(("dx", "dy"), None, None))
    return jax.shard_map(local, mesh=mesh, in_specs=in_specs, out_specs=out_specs, check_vma=False)
```

profile of v0, /device:TPU:1, one launch (start us, length us, event | category | flops | bytes accessed | tf_op | source)
XLA Modules:
  0.0 348.8 jit_solution(2755124276474066206)
XLA Ops:
  0.6 1.5 copy.71
  2.1 11.5 %all-to-all-start = ((s32[128,1,1]{2,1,0:T(1,128)}), s32[128,1,1]{2,1,0:T(1,128)S(1)}, u32[]{:S(2)}, u32[]{:S(2)}) async-start(s32[128,1,1]{2,1,0:T(1,128)} %copy.71), calls=%async_computation | async-start | bytes 131072 | tf_op jit(solution)/shard_map/all_to_all | solution.py:70
  13.7 0.7 iota_compare_fusion.7
  14.4 4.7 %fusion.48 = bf16[64,128,81]{1,2,0:T(8,128)(2,1)S(1)} fusion(bf16[64,128,128]{2,1,0:T(8,128)(2,1)} %param.17, pred[64,128]{1,0:T(8,128)(4,1)S(1)} %iota_compare_fusion.7, bf16[64,81,128]{2,0,1:T(8,128)(2,1)S(1)} %copy-done), kind=kOutput, calls=%fused_computation.70 | convolution fusion | flops 171581440 | bytes 4759552 | tf_op jit(solution)/shard_map/iks,isc->ikc/dot_general | solution.py:15
  19.1 0.2 copy.117
  19.3 11.0 %copy.77 = bf16[316,81,81]{2,1,0:T(8,128)(2,1)} copy(bf16[316,81,81]{0,2,1:T(8,128)(2,1)} %param.18) | data formatting | bytes 8293104
  30.4 96.7 %while.29 = (s32[]{:T(128)}, f32[192,10368]{1,0:T(8,128)}, s32[1,16,32]{2,1,0:T(8,128)S(1)}, pred[16,32]{1,0:T(8,128)(4,1)S(1)}, s32[1,16,32]{2,1,0:T(8,128)S(1)...) while((s32[]{:T(128)}, f32[192,10368]{1,0:T(8,128)}, ...), condition=%wide.region_3.4_spmd.clone, body=%wide.region_2.3_spmd.clone.sunk | while | flops 2827625472 | bytes 86594152 | solution.py:117
  30.5 0.1 and.151
  30.6 3.9 %convolution_convert_fusion.6 = bf16[256,10368]{1,0:T(8,128)(2,1)} fusion(bf16[64,10368]{1,0:T(8,128)(2,1)S(1)} %get-tuple-element.617, s32[256]{0:T(256)S(1)} %eq.223, pred[256]{0:T(512)(128)(4,1)S(1)} %and.151), kind=kOutput, calls=%fused_computation.31.clone.1 | convolution fusion | flops 342425600 | bytes 6636800 | tf_op jit(solution)/shard_map/while/body/eval_jaxpr/dot_general | solution.py:31
  34.4 8.3 %reshape.226 = bf16[8,32,81,128]{3,2,1,0:T(8,128)(2,1)} reshape(bf16[256,10368]{1,0:T(8,128)(2,1)} %convolution_convert_fusion.6) | data formatting | bytes 10616832 | tf_op jit(solution)/shard_map/while/body/eval_jaxpr/reshape | solution.py:112
  42.8 3.6 %gather_fusion.1 = bf16[8,81,81]{2,1,0:T(8,128)(2,1)S(1)} fusion(bf16[316,81,81]{2,1,0:T(8,128)(2,1)} %get-tuple-element.619, s32[1024]{0:T(1024)S(1)} %pad_clamp_fusion.5), kind=kCustom, calls=%fused_computation.1.clone.clone.1 | custom fusion | bytes 209984 | tf_op jit(solution)/shard_map/while/body/eval_jaxpr/gather | solution.py:92
  46.4 8.6 %fusion.112 = f32[8,32,128,81]{2,3,1,0:T(8,128)} fusion(bf16[8,32,81,128]{3,2,1,0:T(8,128)(2,1)} %reshape.226, bf16[8,81,81]{2,1,0:T(8,128)(2,1)S(1)} %gather_fusion.1), kind=kOutput, calls=%fused_computation.38.clone.1 | convolution fusion | flops 429981696 | bytes 16030224 | tf_op jit(solution)/shard_map/while/body/eval_jaxpr/glk,gplc->gpkc/dot_general | solution.py:113
  55.1 9.7 %fusion.113 = f32[192,10368]{1,0:T(8,128)} fusion(f32[32,8,81,128]{3,2,1,0:T(8,128)} %bitcast.112, s32[256]{0:T(256)S(1)} %eq.224, pred[256]{0:T(512)(128)(4,1)S(1)} %and.151), kind=kOutput, calls=%fused_computation.35.clone.1 | convolution fusion | flops 1019314176 | bytes 18580736 | tf_op jit(solution)/shard_map/while/body/eval_jaxpr/dot_general | solution.py:38
  64.8 12.8 %fusion.114 = f32[192,10368]{1,0:T(8,128)} fusion(f32[192,10368]{1,0:T(8,128)} %fusion.113, f32[192,10368]{1,0:T(8,128)} %get-tuple-element.601, f32[32,8,81,128]{3,2,1,0:T(8,128)} %bitcast.113, pred[]{:T(512)S(6)} %compare.7, s32[256]{0:T(256)S(1)} %eq.224, pred[256]{0:T(512)(128)(4,1)S(1)} %and.151), kind=kOutput, calls=%fused_computation.30.clone.1 | convolution fusion | flops 1035902976 | bytes 34505984 | tf_op jit(solution)/shard_map/while/body/eval_jaxpr/dot_general | solution.py:39
  77.6 0.1 eq.223
  77.7 0.1 and.151
  77.8 3.9 %convolution_convert_fusion.6 = bf16[256,10368]{1,0:T(8,128)(2,1)} fusion(bf16[64,10368]{1,0:T(8,128)(2,1)S(1)} %get-tuple-element.617, s32[256]{0:T(256)S(1)} %eq.223, pred[256]{0:T(512)(128)(4,1)S(1)} %and.151), kind=kOutput, calls=%fused_computation.31.clone.1 | convolution fusion | flops 342425600 | bytes 6636800 | tf_op jit(solution)/shard_map/while/body/eval_jaxpr/dot_general | solution.py:31
  81.7 8.3 %reshape.226 = bf16[8,32,81,128]{3,2,1,0:T(8,128)(2,1)} reshape(bf16[256,10368]{1,0:T(8,128)(2,1)} %convolution_convert_fusion.6) | data formatting | bytes 10616832 | tf_op jit(solution)/shard_map/while/body/eval_jaxpr/reshape | solution.py:112
  90.0 3.6 %gather_fusion.1 = bf16[8,81,81]{2,1,0:T(8,128)(2,1)S(1)} fusion(bf16[316,81,81]{2,1,0:T(8,128)(2,1)} %get-tuple-element.619, s32[1024]{0:T(1024)S(1)} %pad_clamp_fusion.5), kind=kCustom, calls=%fused_computation.1.clone.clone.1 | custom fusion | bytes 209984 | tf_op jit(solution)/shard_map/while/body/eval_jaxpr/gather | solution.py:92
  93.6 8.6 %fusion.112 = f32[8,32,128,81]{2,3,1,0:T(8,128)} fusion(bf16[8,32,81,128]{3,2,1,0:T(8,128)(2,1)} %reshape.226, bf16[8,81,81]{2,1,0:T(8,128)(2,1)S(1)} %gather_fusion.1), kind=kOutput, calls=%fused_computation.38.clone.1 | convolution fusion | flops 429981696 | bytes 16030224 | tf_op jit(solution)/shard_map/while/body/eval_jaxpr/glk,gplc->gpkc/dot_general | solution.py:113
  102.3 9.7 %fusion.113 = f32[192,10368]{1,0:T(8,128)} fusion(f32[32,8,81,128]{3,2,1,0:T(8,128)} %bitcast.112, s32[256]{0:T(256)S(1)} %eq.224, pred[256]{0:T(512)(128)(4,1)S(1)} %and.151), kind=kOutput, calls=%fused_computation.35.clone.1 | convolution fusion | flops 1019314176 | bytes 18580736 | tf_op jit(solution)/shard_map/while/body/eval_jaxpr/dot_general | solution.py:38
  112.0 15.1 %fusion.114 = f32[192,10368]{1,0:T(8,128)} fusion(f32[192,10368]{1,0:T(8,128)} %fusion.113, f32[192,10368]{1,0:T(8,128)} %get-tuple-element.601, f32[32,8,81,128]{3,2,1,0:T(8,128)} %bitcast.113, pred[]{:T(512)S(6)} %compare.7, s32[256]{0:T(256)S(1)} %eq.224, pred[256]{0:T(512)(128)(4,1)S(1)} %and.151), kind=kOutput, calls=%fused_computation.30.clone.1 | convolution fusion | flops 1035902976 | bytes 34505984 | tf_op jit(solution)/shard_map/while/body/eval_jaxpr/dot_general | solution.py:39
  127.1 4.3 %slice.16 = bf16[128,10368]{1,0:T(8,128)(2,1)} slice(f32[192,10368]{1,0:T(8,128)} %get-tuple-element.281), slice={[64:192], [0:10368]} | slice | bytes 5308416 | tf_op jit(solution)/shard_map/slice | solution.py:121
  131.4 4.4 %copy.81 = bf16[128,10368]{0,1:T(8,128)(2,1)} copy(bf16[128,10368]{1,0:T(8,128)(2,1)} %slice.16) | data formatting | bytes 5308416 | tf_op jit(solution)/shard_map/slice | solution.py:121
  135.8 4.8 %copy.82 = bf16[128,81,128]{2,1,0:T(8,128)(2,1)} copy(bf16[128,81,128]{0,2,1:T(8,128)(2,1)} %bitcast.119) | data formatting | bytes 5308416 | tf_op jit(solution)/shard_map/reshape | solution.py:121
  140.6 10.1 %all-to-all-start.2 = ((bf16[128,81,128]{2,1,0:T(8,128)(2,1)}), bf16[128,81,128]{2,1,0:T(8,128)(2,1)}, u32[]{:S(2)}, u32[]{:S(2)}) async-start(bf16[128,81,128]{2,1,0:T(8,128)(2,1)} %copy.82), calls=%async_computation.2 | async-start | bytes 5767168 | tf_op jit(solution)/shard_map/all_to_all | solution.py:123
  150.8 4.7 %fusion.45 = bf16[64,128,81]{1,2,0:T(8,128)(2,1)S(1)} fusion(bf16[64,128,128]{2,1,0:T(8,128)(2,1)} %param.14, pred[64,128]{1,0:T(8,128)(4,1)S(1)} %iota_compare_fusion.7, bf16[64,81,128]{2,0,1:T(8,128)(2,1)S(1)} %copy-done), kind=kOutput, calls=%fused_computation.69 | convolution fusion | flops 171581440 | bytes 4759552 | tf_op jit(solution)/shard_map/iks,isc->ikc/dot_general | solution.py:15
  155.4 0.2 copy.118
  155.6 2.4 reduce
  158.0 2.4 convolution_convert_fusion.2
  160.4 4.4 %copy.72 = bf16[128,10368]{0,1:T(8,128)(2,1)} copy(bf16[128,10368]{1,0:T(8,128)(2,1)} %convolution_convert_fusion.2) | data formatting | bytes 5308416 | tf_op jit(solution)/shard_map/convert_element_type | solution.py:31
  164.8 4.8 %copy.73 = bf16[128,81,128]{2,1,0:T(8,128)(2,1)} copy(bf16[128,81,128]{0,2,1:T(8,128)(2,1)} %bitcast.120) | data formatting | bytes 5308416 | tf_op jit(solution)/shard_map/reshape | solution.py:73
  169.6 19.6 %all-to-all-done.2 = bf16[128,81,128]{2,1,0:T(8,128)(2,1)} async-done(((bf16[128,81,128]{2,1,0:T(8,128)(2,1)}), bf16[128,81,128]{2,1,0:T(8,128)(2,1)}, u32[]{:S(2)}, u32[]{:S(2)}) %all-to-all-start.2) | async-done | bytes 2654240 | tf_op jit(solution)/shard_map/all_to_all | solution.py:123
  189.2 5.6 %all-to-all-start.1 = ((bf16[128,81,128]{2,1,0:T(8,128)(2,1)}), bf16[128,81,128]{2,1,0:T(8,128)(2,1)}, u32[]{:S(2)}, u32[]{:S(2)}) async-start(bf16[128,81,128]{2,1,0:T(8,128)(2,1)} %copy.73), calls=%async_computation.1 | async-start | bytes 5767168 | tf_op jit(solution)/shard_map/all_to_all | solution.py:76
  194.8 2.6 copy.75
  197.4 4.8 %copy.83 = bf16[128,81,128]{0,2,1:T(8,128)(2,1)} copy(bf16[128,81,128]{2,1,0:T(8,128)(2,1)} %all-to-all-done.2) | data formatting | bytes 5308416 | tf_op jit(solution)/shard_map/all_to_all | solution.py:123
  202.2 3.6 %fusion.38 = bf16[64,10368]{1,0:T(8,128)(2,1)S(1)} fusion(bf16[128,10368]{0,1:T(8,128)(2,1)} %bitcast.117, f32[192,10368]{1,0:T(8,128)} %get-tuple-element.281, s32[128]{0:T(128)S(1)} %reduce), kind=kOutput, calls=%fused_computation.58 | convolution fusion | flops 171204608 | bytes 6636032 | tf_op jit(solution)/shard_map/dot_general | solution.py:128
  205.8 1.5 reshape.185
  207.3 3.0 fusion.52
  210.3 2.9 copy.86
  213.2 20.1 %all-to-all-done.1 = bf16[128,81,128]{2,1,0:T(8,128)(2,1)} async-done(((bf16[128,81,128]{2,1,0:T(8,128)(2,1)}), bf16[128,81,128]{2,1,0:T(8,128)(2,1)}, u32[]{:S(2)}, u32[]{:S(2)}) %all-to-all-start.1) | async-done | bytes 2654240 | tf_op jit(solution)/shard_map/all_to_all | solution.py:76
  233.4 4.8 %copy.74 = bf16[128,81,128]{0,2,1:T(8,128)(2,1)} copy(bf16[128,81,128]{2,1,0:T(8,128)(2,1)} %all-to-all-done.1) | data formatting | bytes 5308416 | tf_op jit(solution)/shard_map/all_to_all | solution.py:76
  238.2 6.9 %pad_maximum_fusion = bf16[192,10368]{0,1:T(8,128)(2,1)} fusion(bf16[128,10368]{0,1:T(8,128)(2,1)} %bitcast.118, bf16[64,10368]{0,1:T(8,128)(2,1)} %copy.75), kind=kLoop, calls=%fused_computation.60 | loop fusion | flops 7962624 | bytes 7962624 | tf_op jit(solution)/shard_map/concatenate | solution.py:77
  245.0 7.3 %copy.76 = bf16[192,10368]{1,0:T(8,128)(2,1)} copy(bf16[192,10368]{0,1:T(8,128)(2,1)} %pad_maximum_fusion) | data formatting | bytes 7962624
  252.4 87.1 %while.28 = (s32[]{:T(128)}, f32[64,10368]{1,0:T(8,128)}, s32[1,16,32]{2,1,0:T(8,128)S(1)}, pred[16,32]{1,0:T(8,128)(4,1)S(1)}, s32[1,16,32]{2,1,0:T(8,128)S(1)}...) while((s32[]{:T(128)}, f32[64,10368]{1,0:T(8,128)}, ...), condition=%wide.region_1.2_spmd.clone, body=%wide.region_0.1_spmd.clone.sunk | while | flops 2144101376 | bytes 68014696 | solution.py:102
  252.4 0.1 eq.215
  252.5 0.1 and.144
  252.5 6.1 %convolution_convert_fusion.5 = bf16[256,10368]{1,0:T(8,128)(2,1)} fusion(bf16[192,10368]{1,0:T(8,128)(2,1)} %get-tuple-element.581, s32[256]{0:T(256)S(1)} %eq.215, pred[256]{0:T(512)(128)(4,1)S(1)} %and.144), kind=kOutput, calls=%fused_computation.2.clone.1 | convolution fusion | flops 1021968384 | bytes 9291008 | tf_op jit(solution)/shard_map/while/body/eval_jaxpr/dot_general | solution.py:31
  258.6 8.2 %reshape.223 = bf16[8,32,81,128]{3,2,1,0:T(8,128)(2,1)} reshape(bf16[256,10368]{1,0:T(8,128)(2,1)} %convolution_convert_fusion.5) | data formatting | bytes 10616832 | tf_op jit(solution)/shard_map/while/body/eval_jaxpr/reshape | solution.py:97
  266.9 3.6 %gather_fusion = bf16[8,81,81]{2,1,0:T(8,128)(2,1)S(1)} fusion(bf16[316,81,81]{2,1,0:T(8,128)(2,1)} %get-tuple-element.583, s32[1024]{0:T(1024)S(1)} %pad_clamp_fusion.4), kind=kCustom, calls=%fused_computation.clone.clone.1 | custom fusion | bytes 209984 | tf_op jit(solution)/shard_map/while/body/eval_jaxpr/gather | solution.py:92
  270.5 8.5 %fusion.101 = f32[8,32,128,81]{2,3,1,0:T(8,128)} fusion(bf16[8,32,81,128]{3,2,1,0:T(8,128)(2,1)} %reshape.223, bf16[8,81,81]{2,1,0:T(8,128)(2,1)S(1)} %gather_fusion), kind=kOutput, calls=%fused_computation.11.clone.1 | convolution fusion | flops 429981696 | bytes 16030224 | tf_op jit(solution)/shard_map/while/body/eval_jaxpr/gkl,gplc->gpkc/dot_general | solution.py:98
  279.1 7.8 %fusion.102 = f32[64,10368]{1,0:T(8,128)} fusion(f32[32,8,81,128]{3,2,1,0:T(8,128)} %bitcast.110, s32[256]{0:T(256)S(1)} %eq.216, pred[256]{0:T(512)(128)(4,1)S(1)} %and.144), kind=kOutput, calls=%fused_computation.8.clone.1 | convolution fusion | flops 339771392 | bytes 13272320 | tf_op jit(solution)/shard_map/while/body/eval_jaxpr/dot_general | solution.py:38
  286.9 8.6 %fusion.103 = f32[64,10368]{1,0:T(8,128)} fusion(f32[64,10368]{1,0:T(8,128)} %fusion.102, f32[32,8,81,128]{3,2,1,0:T(8,128)} %bitcast.111, f32[64,10368]{1,0:T(8,128)} %get-tuple-element.565, pred[]{:T(512)S(6)} %compare.6, s32[256]{0:T(256)S(1)} %eq.216, pred[256]{0:T(512)(128)(4,1)S(1)} %and.144), kind=kOutput, calls=%fused_computation.4.clone.1 | convolution fusion | flops 352378880 | bytes 18580736 | tf_op jit(solution)/shard_map/while/body/eval_jaxpr/dot_general | solution.py:39
  295.6 0.1 and.144
  295.7 6.1 %convolution_convert_fusion.5 = bf16[256,10368]{1,0:T(8,128)(2,1)} fusion(bf16[192,10368]{1,0:T(8,128)(2,1)} %get-tuple-element.581, s32[256]{0:T(256)S(1)} %eq.215, pred[256]{0:T(512)(128)(4,1)S(1)} %and.144), kind=kOutput, calls=%fused_computation.2.clone.1 | convolution fusion | flops 1021968384 | bytes 9291008 | tf_op jit(solution)/shard_map/while/body/eval_jaxpr/dot_general | solution.py:31
  301.8 8.2 %reshape.223 = bf16[8,32,81,128]{3,2,1,0:T(8,128)(2,1)} reshape(bf16[256,10368]{1,0:T(8,128)(2,1)} %convolution_convert_fusion.5) | data formatting | bytes 10616832 | tf_op jit(solution)/shard_map/while/body/eval_jaxpr/reshape | solution.py:97
  310.1 3.6 %gather_fusion = bf16[8,81,81]{2,1,0:T(8,128)(2,1)S(1)} fusion(bf16[316,81,81]{2,1,0:T(8,128)(2,1)} %get-tuple-element.583, s32[1024]{0:T(1024)S(1)} %pad_clamp_fusion.4), kind=kCustom, calls=%fused_computation.clone.clone.1 | custom fusion | bytes 209984 | tf_op jit(solution)/shard_map/while/body/eval_jaxpr/gather | solution.py:92
  313.7 8.5 %fusion.101 = f32[8,32,128,81]{2,3,1,0:T(8,128)} fusion(bf16[8,32,81,128]{3,2,1,0:T(8,128)(2,1)} %reshape.223, bf16[8,81,81]{2,1,0:T(8,128)(2,1)S(1)} %gather_fusion), kind=kOutput, calls=%fused_computation.11.clone.1 | convolution fusion | flops 429981696 | bytes 16030224 | tf_op jit(solution)/shard_map/while/body/eval_jaxpr/gkl,gplc->gpkc/dot_general | solution.py:98
  322.2 7.8 %fusion.102 = f32[64,10368]{1,0:T(8,128)} fusion(f32[32,8,81,128]{3,2,1,0:T(8,128)} %bitcast.110, s32[256]{0:T(256)S(1)} %eq.216, pred[256]{0:T(512)(128)(4,1)S(1)} %and.144), kind=kOutput, calls=%fused_computation.8.clone.1 | convolution fusion | flops 339771392 | bytes 13272320 | tf_op jit(solution)/shard_map/while/body/eval_jaxpr/dot_general | solution.py:38
  330.0 9.4 %fusion.103 = f32[64,10368]{1,0:T(8,128)} fusion(f32[64,10368]{1,0:T(8,128)} %fusion.102, f32[32,8,81,128]{3,2,1,0:T(8,128)} %bitcast.111, f32[64,10368]{1,0:T(8,128)} %get-tuple-element.565, pred[]{:T(512)S(6)} %compare.6, s32[256]{0:T(256)S(1)} %eq.216, pred[256]{0:T(512)(128)(4,1)S(1)} %and.144), kind=kOutput, calls=%fused_computation.4.clone.1 | convolution fusion | flops 352378880 | bytes 18580736 | tf_op jit(solution)/shard_map/while/body/eval_jaxpr/dot_general | solution.py:39
  339.4 1.9 convert_element_type.107
  341.3 1.5 reshape.181
  342.8 3.0 fusion.51
  345.9 2.9 copy.85
  (36 shorter events, 0.9 us)
Async XLA Ops:
  0.6 13.8 %copy-start = (bf16[64,81,128]{2,0,1:T(8,128)(2,1)S(1)}, bf16[64,81,128]{2,0,1:T(8,128)(2,1)}, u32[]{:S(2)}) copy-start(bf16[64,81,128]{2,0,1:T(8,128)(2,1)} %param.15) | copy-start | bytes 3981316
  2.1 138.5 %all-to-all-start = ((s32[128,1,1]{2,1,0:T(1,128)}), s32[128,1,1]{2,1,0:T(1,128)S(1)}, u32[]{:S(2)}, u32[]{:S(2)}) async-start(s32[128,1,1]{2,1,0:T(1,128)} %copy.71), calls=%async_computation | async-start | bytes 131072 | tf_op jit(solution)/shard_map/all_to_all | solution.py:70
  19.3 11.0 %copy-start.3 = (s32[1,16]{1,0:T(1,128)S(1)}, s32[1,16]{1,0:T(1,128)}, u32[]{:S(2)}) copy-start(s32[1,16]{1,0:T(1,128)} %param.23) | copy-start | bytes 196
  19.3 11.1 %copy-start.1 = (s32[1,16,32]{2,1,0:T(8,128)S(1)}, s32[1,16,32]{2,1,0:T(8,128)}, u32[]{:S(2)}) copy-start(s32[1,16,32]{2,1,0:T(8,128)} %param.20) | copy-start | bytes 6148
  19.3 11.1 %copy-start.2 = (s32[1,16,32]{2,1,0:T(8,128)S(1)}, s32[1,16,32]{2,1,0:T(8,128)}, u32[]{:S(2)}) copy-start(s32[1,16,32]{2,1,0:T(8,128)} %param.21) | copy-start | bytes 6148
  19.3 11.1 %copy-start.4 = (s32[1,16]{1,0:T(1,128)S(1)}, s32[1,16]{1,0:T(1,128)}, u32[]{:S(2)}) copy-start(s32[1,16]{1,0:T(1,128)} %param.22) | copy-start | bytes 196
  140.6 48.6 %all-to-all-start.2 = ((bf16[128,81,128]{2,1,0:T(8,128)(2,1)}), bf16[128,81,128]{2,1,0:T(8,128)(2,1)}, u32[]{:S(2)}, u32[]{:S(2)}) async-start(bf16[128,81,128]{2,1,0:T(8,128)(2,1)} %copy.82), calls=%async_computation.2 | async-start | bytes 5767168 | tf_op jit(solution)/shard_map/all_to_all | solution.py:123
  189.2 44.2 %all-to-all-start.1 = ((bf16[128,81,128]{2,1,0:T(8,128)(2,1)}), bf16[128,81,128]{2,1,0:T(8,128)(2,1)}, u32[]{:S(2)}, u32[]{:S(2)}) async-start(bf16[128,81,128]{2,1,0:T(8,128)(2,1)} %copy.73), calls=%async_computation.1 | async-start | bytes 5767168 | tf_op jit(solution)/shard_map/all_to_all | solution.py:76
where the time goes:
time: 351 us; the launch traced here: 349 us
  matrix products  156 us (44%)
  local copies, waits for them, and re-layouts  112 us (32%)
  waiting for transfers between devices  39.7 us (11%)
  starting transfers between devices  27.2 us (8%)
  other arithmetic  12.3 us (4%)
    dot_general x4, matrix products, add_into_rows(): lax.dot_general(selector, low_part, dims, preferred_element_type=jnp.floa...  46 us
    dot_general x4, matrix products, add_into_rows(): lax.dot_general(selector, high_part, dims, preferred_element_type=jnp.flo...  35 us
    unnamed x16, local copies, waits for them, and re-layouts  24.5 us
    dot_general x5, matrix products, select_rows(): jnp.dot(selector, table, preferred_element_type=jnp.float32)  22.4 us
    all_to_all x1, waiting for transfers between devices, local(): lax.all_to_all(outgoing, ('dx', 'dy'), split_axis=0, concat_axis=0, tiled...  20.1 us
    all_to_all x1, waiting for transfers between devices, local(): lax.all_to_all(remote_grads, ('dx', 'dy'), split_axis=0, concat_axis=0, t...  19.6 us
    dot_general x2, matrix products, backward_group(): jnp.einsum('glk,gplc->gpkc', chosen, picked, preferred_element_type=jnp.f...  17.2 us
    dot_general x2, matrix products, forward_group(): jnp.einsum('gkl,gplc->gpkc', chosen, picked, preferred_element_type=jnp.f...  17 us
  transfers between devices with their start and end apart: 3, of which 2 were waited for; matrix products, arithmetic and copies ran while one was open for 47% of the time, Pallas kernels for 0%

commit v1 on v0

v1 whole, which is shorter than its diff:
```python
import jax
import jax.numpy as jnp
from jax import lax
from jax.experimental import pallas as pl
from jax.experimental.pallas import tpu as pltpu
from jax.sharding import PartitionSpec as P

BF = jnp.bfloat16
F32 = jnp.float32
ROWS = 88
MAIN = 80
PACK = 168
CHUNK = 8


def dot(a, b):
    return lax.dot_general(a, b, (((1,), (0,)), ((), ())), preferred_element_type=F32)


def params(mib):
    return pltpu.CompilerParams(vmem_limit_bytes=mib << 20)


def spread_basis(basis_ref, wide_ref, coeffs, cells):
    def put(k, carry):
        wide_ref[pl.ds(pl.multiple_of(k * cells, cells), cells), :] = basis_ref[k].astype(F32)
        return carry

    lax.fori_loop(0, coeffs, put, 0, unroll=9)
    wide_ref[coeffs * cells : (coeffs + 1) * cells, :] = basis_ref[coeffs - 1].astype(F32)
    rest = ROWS - coeffs - 1
    wide_ref[(coeffs + 1) * cells :, :] = jnp.zeros((rest * cells, wide_ref.shape[1]), F32)


def masked_basis(wide_ref, count_ref, cell, cells):
    tile = wide_ref[pl.ds(cell, ROWS, stride=cells), :]
    lane = lax.broadcasted_iota(jnp.int32, tile.shape, 1)
    return jnp.where(lane < count_ref[cell], tile, 0.0)


def first_kernel(
    count_ref,
    target_ref,
    source_ref,
    fill_ref,
    charges_hbm,
    cotangent_hbm,
    basis_hbm,
    chosen_ref,
    mult_ref,
    back_ref,
    own_hbm,
    forward_op_ref,
    charges_ref,
    cotangent_ref,
    basis_ref,
    wide_ref,
    grad_ref,
    total_ref,
    back_op_ref,
    sems,
):
    cells = charges_ref.shape[0]
    coeffs = basis_ref.shape[0]
    batches = chosen_ref.shape[0]
    remote = back_ref.shape[0]
    parts = 4
    step = cells // parts
    basis_copy = pltpu.make_async_copy(basis_hbm, basis_ref, sems.at[0])
    basis_copy.start()
    copies = []
    for part in range(parts):
        rows = pl.ds(part * step, step)
        pair = (
            pltpu.make_async_copy(cotangent_hbm.at[rows], cotangent_ref.at[rows], sems.at[1 + 2 * part]),
            pltpu.make_async_copy(charges_hbm.at[rows], charges_ref.at[rows], sems.at[2 + 2 * part]),
        )
        for copy in pair:
            copy.start()
        copies.append(pair)

    lane = lax.broadcasted_iota(jnp.int32, (ROWS, 128), 1)

    def prepare(b, carry):
        square = chosen_ref[b].astype(F32)
        wide = jnp.pad(square, ((0, 128 - coeffs), (0, 128 - coeffs)))
        back_op_ref[b] = wide.T[:ROWS].astype(BF)
        top = wide[:ROWS]
        moved = pltpu.roll(top, 1, 1)
        forward_op_ref[b] = jnp.where(lane < MAIN, top, jnp.where(lane == MAIN + 1, moved, 0.0)).astype(BF)
        return carry

    lax.fori_loop(0, batches, prepare, 0)

    def clear(e, carry):
        total_ref[e] = jnp.zeros((ROWS, 128), F32)
        return carry

    lax.fori_loop(0, total_ref.shape[0], clear, 0, unroll=4)

    basis_copy.wait()
    spread_basis(basis_ref, wide_ref, coeffs, cells)

    def moment(i, carry):
        tile = masked_basis(wide_ref, count_ref, i, cells).astype(BF)
        both = jnp.concatenate([cotangent_ref[i], charges_ref[i]], axis=1)
        result = dot(tile, both).astype(BF)
        grad_ref[i] = result[:, :128]
        mult_ref[i] = result[:, 128:]
        return carry

    for part in range(parts):
        for copy in copies[part]:
            copy.wait()
        lax.fori_loop(part * step, (part + 1) * step, moment, 0, unroll=4)

    spare = total_ref.shape[0] - 1

    def batch(b, carry):
        fill = fill_ref[b]
        op = back_op_ref[b][:, :ROWS]

        def chunk(j, inner):
            first = j * CHUNK
            for q in range(0, CHUNK, 2):
                p = first + q
                left = grad_ref[target_ref[b, p]]
                right = grad_ref[target_ref[b, p + 1]]
                result = dot(op, jnp.concatenate([left, right], axis=1))
                e0 = jnp.where(p < fill, source_ref[b, p], spare)
                total_ref[e0] += result[:, :128]
                e1 = jnp.where(p + 1 < fill, source_ref[b, p + 1], spare)
                total_ref[e1] += result[:, 128:]
            return inner

        lax.fori_loop(0, (fill + CHUNK - 1) // CHUNK, chunk, 0)
        return carry

    lax.fori_loop(0, batches, batch, 0)
    own_copy = pltpu.make_async_copy(total_ref.at[pl.ds(0, cells)], own_hbm, sems.at[0])
    own_copy.start()

    def narrow(s, carry):
        back_ref[s] = total_ref[cells + s].astype(BF)
        return carry

    lax.fori_loop(0, remote, narrow, 0, unroll=4)
    own_copy.wait()


def pack_kernel(asked_ref, mult_ref, back_ref, out_ref):
    per_step = out_ref.shape[0]
    first = pl.program_id(0) * per_step
    row = lax.broadcasted_iota(jnp.int32, (8, 128), 0)

    def one(s, carry):
        cell = asked_ref[first + s, 0, 0]
        out_ref[s, :MAIN, :] = mult_ref[cell, :MAIN, :]
        out_ref[s, MAIN : 2 * MAIN, :] = back_ref[s, :MAIN, :]
        tail = jnp.where(
            row == 1, mult_ref[cell, MAIN:ROWS, :].astype(F32), back_ref[s, MAIN:ROWS, :].astype(F32)
        )
        out_ref[s, 2 * MAIN : PACK, :] = tail.astype(BF)
        return carry

    lax.fori_loop(0, per_step, one, 0, unroll=4)


def beside_kernel(
    count_ref,
    target_ref,
    source_ref,
    fill_ref,
    mult_ref,
    basis_ref,
    op_ref,
    local_ref,
    atoms_ref,
    number_ref,
    list_batch_ref,
    list_target_ref,
    list_source_ref,
    wide_ref,
    own_target,
    own_source,
):
    cells = mult_ref.shape[0]
    coeffs = basis_ref.shape[0]
    batches = op_ref.shape[0]

    def clear(i, carry):
        local_ref[i] = jnp.zeros((ROWS, 128), F32)
        return carry

    lax.fori_loop(0, cells + 1, clear, 0)
    spread_basis(basis_ref, wide_ref, coeffs, cells)

    def turn(i, carry):
        tile = masked_basis(wide_ref, count_ref, i, cells)
        full = jnp.pad(tile, ((0, 128 - ROWS), (0, 0)))
        atoms_ref[i] = full.T.astype(BF)
        return carry

    lax.fori_loop(0, cells, turn, 0, unroll=2)

    def batch(b, chunks):
        fill = fill_ref[b]
        base = chunks * CHUNK

        def sort(p, counts):
            own, far = counts
            source = source_ref[b, p]
            target = target_ref[b, p]
            is_own = source < cells

            @pl.when(is_own)
            def _():
                own_target[own] = target
                own_source[own] = source

            @pl.when(jnp.logical_not(is_own))
            def _():
                list_target_ref[base + far] = target
                list_source_ref[base + far] = source - cells

            step = is_own.astype(jnp.int32)
            return own + step, far + 1 - step

        own, far = lax.fori_loop(0, fill, sort, (0, 0))
        for q in range(CHUNK):
            own_target[own + q] = cells
            own_source[own + q] = 0
            list_target_ref[base + far + q] = cells
            list_source_ref[base + far + q] = 0
        far_chunks = (far + CHUNK - 1) // CHUNK

        def mark(j, carry):
            list_batch_ref[chunks + j] = b
            return carry

        lax.fori_loop(0, far_chunks, mark, 0)
        op = op_ref[b][:, :ROWS]

        def chunk(j, carry):
            for q in range(0, CHUNK, 2):
                p = j * CHUNK + q
                both = jnp.concatenate([mult_ref[own_source[p]], mult_ref[own_source[p + 1]]], axis=1)
                result = dot(op, both)
                local_ref[own_target[p]] += result[:, :128]
                local_ref[own_target[p + 1]] += result[:, 128:]
            return carry

        lax.fori_loop(0, (own + CHUNK - 1) // CHUNK, chunk, 0)
        return chunks + far_chunks

    number_ref[0] = lax.fori_loop(0, batches, batch, 0)


def last_kernel(
    asked_ref,
    number_ref,
    list_batch_ref,
    list_target_ref,
    list_source_ref,
    incoming_hbm,
    own_hbm,
    local_hbm,
    atoms_hbm,
    op_ref,
    potential_hbm,
    charge_hbm,
    incoming_ref,
    own_ref,
    local_ref,
    atoms_ref,
    potential_ref,
    charge_ref,
    sems,
    out_sems,
):
    cells = own_ref.shape[0]
    remote = incoming_ref.shape[0]
    parts = 4
    step = remote // parts
    own_copy = pltpu.make_async_copy(own_hbm, own_ref, sems.at[0])
    own_copy.start()
    copies = []
    for part in range(parts):
        rows = pl.ds(part * step, step)
        copy = pltpu.make_async_copy(incoming_hbm.at[rows], incoming_ref.at[rows], sems.at[1 + part])
        copy.start()
        copies.append(copy)
    local_copy = pltpu.make_async_copy(local_hbm, local_ref, sems.at[parts + 1])
    local_copy.start()
    atoms_copy = pltpu.make_async_copy(atoms_hbm, atoms_ref, sems.at[parts + 2])
    atoms_copy.start()
    own_copy.wait()

    def collect(s, carry):
        own_ref[asked_ref[s, 0, 0]] += incoming_ref[s, MAIN:PACK, :].astype(F32)
        return carry

    for part in range(parts):
        copies[part].wait()
        lax.fori_loop(part * step, (part + 1) * step, collect, 0, unroll=4)
    local_copy.wait()

    def pick(e):
        return jnp.concatenate([incoming_ref[e, :MAIN, :], incoming_ref[e, 2 * MAIN : PACK, :]], axis=0)

    def chunk(j, carry):
        op = op_ref[list_batch_ref[j]][:, :ROWS]
        for q in range(0, CHUNK, 2):
            p = j * CHUNK + q
            both = jnp.concatenate([pick(list_source_ref[p]), pick(list_source_ref[p + 1])], axis=1)
            result = dot(op, both)
            local_ref[list_target_ref[p]] += result[:, :128]
            local_ref[list_target_ref[p + 1]] += result[:, 128:]
        return carry

    lax.fori_loop(0, number_ref[0], chunk, 0)
    atoms_copy.wait()
    row = lax.broadcasted_iota(jnp.int32, (ROWS, 128), 0)

    def atoms(i, carry):
        grads = jnp.where(row == MAIN + 1, 0.0, own_ref[i]).astype(BF)
        both = jnp.concatenate([local_ref[i].astype(BF), grads], axis=1)
        result = dot(atoms_ref[i][:, :ROWS], both).astype(BF)
        potential_ref[i] = result[:, :128]
        charge_ref[i] = result[:, 128:]
        return carry

    outs = []
    width = cells // parts
    for part in range(parts):
        lax.fori_loop(part * width, (part + 1) * width, atoms, 0, unroll=4)
        rows = pl.ds(part * width, width)
        for place, (ref, hbm) in enumerate(((potential_ref, potential_hbm), (charge_ref, charge_hbm))):
            copy = pltpu.make_async_copy(ref.at[rows], hbm.at[rows], out_sems.at[2 * part + place])
            copy.start()
            outs.append(copy)
    for copy in outs:
        copy.wait()


SMEM = pl.BlockSpec(memory_space=pltpu.SMEM)
VMEM = pl.BlockSpec(memory_space=pltpu.VMEM)
ANY = pl.BlockSpec(memory_space=pl.ANY)


def local(
    charges,
    basis,
    leaf_count,
    cotangent,
    m2l_ops,
    fetch_cells,
    pair_target,
    pair_source,
    batch_class,
    batch_fill,
):
    cells, coeffs, slots = basis.shape
    channels = charges.shape[2]
    domains = fetch_cells.shape[1]
    _, batches, batch_size = pair_target.shape
    classes = m2l_ops.shape[0]
    Shape = jax.ShapeDtypeStruct
    asked = lax.all_to_all(
        fetch_cells.reshape(domains, 1, 1), ("dx", "dy"), split_axis=0, concat_axis=0, tiled=True
    )
    basis_major = basis.transpose(1, 0, 2)
    hot = (batch_class[0][:, None] == lax.broadcasted_iota(jnp.int32, (1, classes), 1)).astype(BF)
    chosen = jnp.einsum("bn,nkl->bkl", hot, m2l_ops, preferred_element_type=F32).astype(BF)
    targets, sources, fill = pair_target[0], pair_source[0], batch_fill[0]
    mult, back, own, forward_ops = pl.pallas_call(
        first_kernel,
        out_shape=(
            Shape((cells, ROWS, channels), BF),
            Shape((domains, ROWS, channels), BF),
            Shape((cells, ROWS, channels), F32),
            Shape((batches, ROWS, 128), BF),
        ),
        in_specs=[SMEM] * 4 + [ANY] * 3 + [VMEM],
        out_specs=(VMEM, VMEM, ANY, VMEM),
        scratch_shapes=[
            pltpu.VMEM((cells, slots, channels), BF),
            pltpu.VMEM((cells, slots, channels), BF),
            pltpu.VMEM((coeffs, cells, slots), BF),
            pltpu.VMEM((ROWS * cells, slots), F32),
            pltpu.VMEM((cells, ROWS, channels), BF),
            pltpu.VMEM((cells + domains + 1, ROWS, channels), F32),
            pltpu.VMEM((batches, ROWS, 128), BF),
            pltpu.SemaphoreType.DMA((9,)),
        ],
        compiler_params=params(48),
        name="moments_back_pairs",
    )(leaf_count, targets, sources, fill, charges, cotangent, basis_major, chosen)
    per_step = 16
    outgoing = pl.pallas_call(
        pack_kernel,
        out_shape=Shape((domains, PACK, channels), BF),
        grid=(domains // per_step,),
        in_specs=[
            SMEM,
            pl.BlockSpec((cells, ROWS, channels), lambda i: (0, 0, 0)),
            pl.BlockSpec((per_step, ROWS, channels), lambda i: (i, 0, 0)),
        ],
        out_specs=pl.BlockSpec((per_step, PACK, channels), lambda i: (i, 0, 0)),
        compiler_params=params(32),
        name="pack_blocks",
    )(asked, mult, back)
    incoming = lax.all_to_all(outgoing, ("dx", "dy"), split_axis=0, concat_axis=0, tiled=True)
    slots_listed = batches * (batch_size + CHUNK)
    local_part, atoms, number, list_batch, list_target, list_source = pl.pallas_call(
        beside_kernel,
        out_shape=(
            Shape((cells + 1, ROWS, channels), F32),
            Shape((cells, slots, 128), BF),
            Shape((1,), jnp.int32),
            Shape((slots_listed // CHUNK,), jnp.int32),
            Shape((slots_listed,), jnp.int32),
            Shape((slots_listed,), jnp.int32),
        ),
        in_specs=[SMEM] * 4 + [VMEM] * 3,
        out_specs=(VMEM, VMEM, SMEM, SMEM, SMEM, SMEM),
        scratch_shapes=[
            pltpu.VMEM((ROWS * cells, slots), F32),
            pltpu.SMEM((batch_size + CHUNK,), jnp.int32),
            pltpu.SMEM((batch_size + CHUNK,), jnp.int32),
        ],
        compiler_params=params(32),
        cost_estimate=pl.CostEstimate(flops=400_000_000, bytes_accessed=8_000_000, transcendentals=0),
        name="own_pairs",
    )(leaf_count, targets, sources, fill, mult, basis_major, forward_ops)
    return pl.pallas_call(
        last_kernel,
        out_shape=(Shape((cells, slots, channels), BF), Shape((cells, slots, channels), BF)),
        in_specs=[SMEM] * 5 + [ANY] * 4 + [VMEM],
        out_specs=(ANY, ANY),
        scratch_shapes=[
            pltpu.VMEM((domains, PACK, channels), BF),
            pltpu.VMEM((cells, ROWS, channels), F32),
            pltpu.VMEM((cells + 1, ROWS, channels), F32),
            pltpu.VMEM((cells, slots, 128), BF),
            pltpu.VMEM((cells, slots, channels), BF),
            pltpu.VMEM((cells, slots, channels), BF),
            pltpu.SemaphoreType.DMA((8,)),
            pltpu.SemaphoreType.DMA((8,)),
        ],
        compiler_params=params(48),
        name="far_pairs_atoms",
    )(asked, number, list_batch, list_target, list_source, incoming, own, local_part, atoms, forward_ops)


def solution(mesh):
    in_specs = (
        P(("dx", "dy"), None, None),
        P(("dx", "dy"), None, None),
        P(("dx", "dy")),
        P(("dx", "dy"), None, None),
        P(),
        P(("dx", "dy"), None, None),
        P(("dx", "dy"), None, None),
        P(("dx", "dy"), None, None),
        P(("dx", "dy"), None),
        P(("dx", "dy"), None),
    )
    out_specs = (P(("dx", "dy"), None, None), P(("dx", "dy"), None, None))
    return jax.shard_map(local, mesh=mesh, in_specs=in_specs, out_specs=out_specs, check_vma=False)
```

time: 351 us -> 145 us (0.41)
  matrix products: 156 us -> 5.15 us
  local copies, waits for them, and re-layouts: 112 us -> 12.2 us
  Pallas kernels: 0 us -> 41.1 us
  waiting for transfers between devices: 39.7 us -> 53 us
  other arithmetic: 12.3 us -> 0 us
    dot_general x22 -> x1, matrix products: 156 us -> 5.15 us  [local(): jnp.einsum('bn,nkl->bkl', hot, m2l_ops, preferred_element_type=F32)]
    reshape x9 -> x1, local copies, waits for them, and re-layouts: 48.1 us -> 1.39 us  [local(): fetch_cells.reshape(domains, 1, 1)]
    pallas_call x0 -> x4, Pallas kernels: none -> 41.1 us  [the longest x1 14.7 us: local(): pl.pallas_call(first_kernel, out_shape=(Shape((cells, ROWS, channels), BF...]
    all_to_all x1, waiting for transfers between devices: 20.1 us -> 53 us  [local(): lax.all_to_all(outgoing, ('dx', 'dy'), split_axis=0, concat_axis=0, tiled...]
    all_to_all x2 -> x1, waiting for transfers between devices: 19.6 us -> 0.01 us  [local(): lax.all_to_all(fetch_cells.reshape(domains, 1, 1), ('dx', 'dy'), split_ax...]
    gather x4 -> x0, local copies, waits for them, and re-layouts: 14.4 us -> none  [group_slices(): return (source_rows, target_rows, active, m2l_ops[classes])]
    unnamed x16 -> x24, local copies, waits for them, and re-layouts: 24.5 us -> 10.7 us
    all_to_all x1, starting transfers between devices: 5.6 us -> 18.3 us  [local(): lax.all_to_all(outgoing, ('dx', 'dy'), split_axis=0, concat_axis=0, tiled...]
  transfers between devices with their start and end apart: 3 -> 2, of which waited for: 2 -> 1; matrix products, arithmetic and copies ran while one was open for 47% -> 4% of each run, Pallas kernels for 0% -> 18%
where the time goes in v1:
time: 145 us; the launch traced here: 142 us
  waiting for transfers between devices  53 us (37%)
  Pallas kernels  41.1 us (28%)
  starting transfers between devices  29.8 us (21%)
  local copies, waits for them, and re-layouts  12.2 us (8%)
  matrix products  5.15 us (4%)
    all_to_all x1, waiting for transfers between devices, local(): lax.all_to_all(outgoing, ('dx', 'dy'), split_axis=0, concat_axis=0, tiled...  53 us
    all_to_all x1, starting transfers between devices, local(): lax.all_to_all(outgoing, ('dx', 'dy'), split_axis=0, concat_axis=0, tiled...  18.3 us
    pallas_call x1, Pallas kernels, local(): pl.pallas_call(first_kernel, out_shape=(Shape((cells, ROWS, channels), BF...  14.7 us
    pallas_call x1, Pallas kernels, local(): pl.pallas_call(last_kernel, out_shape=(Shape((cells, slots, channels), BF...  13.5 us
    all_to_all x1, starting transfers between devices, local(): lax.all_to_all(fetch_cells.reshape(domains, 1, 1), ('dx', 'dy'), split_ax...  11.5 us
    unnamed x24, local copies, waits for them, and re-layouts  10.7 us
    pallas_call x1, Pallas kernels, local(): pl.pallas_call(beside_kernel, out_shape=(Shape((cells + 1, ROWS, channels...  10.5 us
    dot_general x1, matrix products, local(): jnp.einsum('bn,nkl->bkl', hot, m2l_ops, preferred_element_type=F32)  5.15 us
  transfers between devices with their start and end apart: 2, of which 1 were waited for; matrix products, arithmetic and copies ran while one was open for 4% of the time, Pallas kernels for 18%

profile of v1, /device:TPU:1, one launch (start us, length us, event | category | flops | bytes accessed | tf_op | source)
XLA Modules:
  0.0 141.9 jit_solution(17168537824420392087)
XLA Ops:
  0.6 1.4 copy.14
  2.0 11.5 %all-to-all-start = ((s32[128,1,1]{2,1,0:T(1,128)}), s32[128,1,1]{2,1,0:T(1,128)S(1)}, u32[]{:S(2)}, u32[]{:S(2)}) async-start(s32[128,1,1]{2,1,0:T(1,128)} %copy.14), calls=%async_computation | async-start | bytes 131072 | tf_op jit(solution)/shard_map/all_to_all | solution.py:369
  13.5 0.0 copy-start.1
  13.5 0.0 copy-start.5
  13.5 0.0 copy-start.8
  13.6 0.0 copy-start.9
  13.6 0.0 copy-start.10
  13.6 0.0 copy-start.11
  13.6 5.1 %convolution_convert_fusion = bf16[16,81,81]{2,0,1:T(8,128)(2,1)S(1)} fusion(bf16[316,81,81]{0,2,1:T(8,128)(2,1)} %param.14, s32[16]{0:T(128)} %bitcast.19), kind=kOutput, calls=%fused_computation | convolution fusion | flops 66454864 | bytes 4356568 | tf_op jit(solution)/shard_map/bn,nkl->bkl/dot_general | solution.py:374
  18.7 0.1 copy.15.chosen_ref
  18.9 0.0 copy-done.1
  18.9 0.0 copy-done.5
  18.9 0.0 copy-done.8
  18.9 0.0 copy-done.9
  18.9 0.0 copy-done.10
  18.9 0.0 copy-done.11
  18.9 14.7 %moments_back_pairs.1 = (bf16[64,88,128]{2,1,0:T(8,128)(2,1)S(1)}, bf16[128,88,128]{2,1,0:T(8,128)(2,1)}, f32[64,88,128]{2,1,0:T(8,128)}, bf16[16,88,128]{2,1,0:T(8,128)(2,1)S(1)}) custom-call(s32[64]{0:T(128)S(1)} %copy-done.10, s32[16,32]{1,0:T(8,128)S(1)} %bitcast.12, s32[16,32]{1,0:T(8,128)S(1)} %bitcast.14, s32[16]{0:T(128)S(1)} %bitcast.16, ...), custom_call_target="tpu_custom_call" | custom-call | tf_op jit(solution)/shard_map/moments_back_pairs/pallas_call | solution.py:376
  33.6 0.0 all-to-all-done.asked_ref
  33.6 0.0 copy-start.3
  33.7 1.8 %copy-done.3 = bf16[128,88,128]{2,1,0:T(8,128)(2,1)S(1)} copy-done((bf16[128,88,128]{2,1,0:T(8,128)(2,1)S(1)}, bf16[128,88,128]{2,1,0:T(8,128)(2,1)}, u32[]{:S(2)}) %copy-start.3) | copy-done | bytes 2883608
  35.5 2.3 %pack_blocks.1 = bf16[128,168,128]{2,1,0:T(8,128)(2,1)S(1)} custom-call(s32[128,1,1]{2,1,0:T(1,128)S(1)} %all-to-all-done.asked_ref, bf16[64,88,128]{2,1,0:T(8,128)(2,1)S(1)} %get-tuple-element.12.mult_ref, bf16[128,88,128]{2,1,0:T(8,128)(2,1)S(1)} %copy-done.3), custom_call_target="tpu_custom_call" | custom-call | tf_op jit(solution)/shard_map/pack_blocks/pallas_call | solution.py:400
  37.8 0.0 copy-start
  37.8 2.4 %copy-done = bf16[128,168,128]{2,1,0:T(8,128)(2,1)} copy-done((bf16[128,168,128]{2,1,0:T(8,128)(2,1)}, bf16[128,168,128]{2,1,0:T(8,128)(2,1)S(1)}, u32[]{:S(2)}) %copy-start) | copy-done | bytes 5505048
  40.3 18.3 %all-to-all-start.1 = ((bf16[128,168,128]{2,1,0:T(8,128)(2,1)}), bf16[128,168,128]{2,1,0:T(8,128)(2,1)}, u32[]{:S(2)}, u32[]{:S(2)}) async-start(bf16[128,168,128]{2,1,0:T(8,128)(2,1)} %copy-done), calls=%async_computation.1 | async-start | bytes 11010048 | tf_op jit(solution)/shard_map/all_to_all | solution.py:413
  58.5 10.5 %own_pairs.1 = (f32[65,88,128]{2,1,0:T(8,128)S(1)}, bf16[64,128,128]{2,1,0:T(8,128)(2,1)S(1)}, s32[1]{0:T(128)}, s32[80]{0:T(128)S(1)}, s32[640]{0:T(1024)S(1)}, /*index=5*/s32[640]{0:T(1024)S(1)}) custom-call(s32[64]{0:T(128)S(1)} %copy-done.10, s32[16,32]{1,0:T(8,128)S(1)} %bitcast.13, s32[16,32]{1,0:T(8,128)S(1)} %bitcast.15, s32[16]{0:T(128)S(1)} %bitcast.17, ...), custom_call_target="tpu_custom_call" | custom-call | flops 400000000 | bytes 8000000 | tf_op jit(solution)/shard_map/own_pairs/pallas_call | solution.py:415
  69.1 0.0 copy-start.2
  69.1 1.7 %copy-done.2 = f32[65,88,128]{2,1,0:T(8,128)} copy-done((f32[65,88,128]{2,1,0:T(8,128)}, f32[65,88,128]{2,1,0:T(8,128)S(1)}, u32[]{:S(2)}) %copy-start.2) | copy-done | bytes 2928664
  70.8 0.0 copy-start.6
  70.8 1.3 copy-done.6
  72.1 53.0 %all-to-all-done.1.incoming_hbm = bf16[128,168,128]{2,1,0:T(8,128)(2,1)} async-done(((bf16[128,168,128]{2,1,0:T(8,128)(2,1)}), bf16[128,168,128]{2,1,0:T(8,128)(2,1)}, u32[]{:S(2)}, u32[]{:S(2)}) %all-to-all-start.1) | async-done | bytes 5505056 | tf_op jit(solution)/shard_map/all_to_all | solution.py:413
  125.0 0.0 copy-start.4
  125.0 1.8 %copy-done.4 = f32[64,88,128]{2,1,0:T(8,128)S(1)} copy-done((f32[64,88,128]{2,1,0:T(8,128)S(1)}, f32[64,88,128]{2,1,0:T(8,128)}, u32[]{:S(2)}) %copy-start.4) | copy-done | bytes 2883608
  126.9 0.0 copy-start.7
  126.9 1.6 %copy-done.7 = bf16[64,128,128]{2,1,0:T(8,128)(2,1)S(1)} copy-done((bf16[64,128,128]{2,1,0:T(8,128)(2,1)S(1)}, bf16[64,128,128]{2,1,0:T(8,128)(2,1)}, u32[]{:S(2)}) %copy-start.7) | copy-done | bytes 2097176
  128.4 13.5 %far_pairs_atoms.1 = (bf16[64,128,128]{2,1,0:T(8,128)(2,1)}, bf16[64,128,128]{2,1,0:T(8,128)(2,1)}) custom-call(s32[128,1,1]{2,1,0:T(1,128)S(1)} %all-to-all-done.asked_ref, s32[1]{0:T(128)} %get-tuple-element.14.number_ref, s32[80]{0:T(128)S(1)} %get-tuple-element.15.list_batch_ref, s32[640]{0:T(1024)S(1)} %get-tuple-element.16.list_target_ref, ...), custom_call_target="tpu_custom_call" | custom-call | tf_op jit(solution)/shard_map/far_pairs_atoms/pallas_call | solution.py:436
Async XLA Ops:
  2.0 31.6 %all-to-all-start = ((s32[128,1,1]{2,1,0:T(1,128)}), s32[128,1,1]{2,1,0:T(1,128)S(1)}, u32[]{:S(2)}, u32[]{:S(2)}) async-start(s32[128,1,1]{2,1,0:T(1,128)} %copy.14), calls=%async_computation | async-start | bytes 131072 | tf_op jit(solution)/shard_map/all_to_all | solution.py:369
  13.5 5.3 %copy-start.1 = (bf16[64,81,128]{2,0,1:T(8,128)(2,1)S(1)}, bf16[64,81,128]{2,0,1:T(8,128)(2,1)}, u32[]{:S(2)}) copy-start(bf16[64,81,128]{2,0,1:T(8,128)(2,1)} %param.11) | copy-start | bytes 3981316
  13.5 5.3 %copy-start.5 = (bf16[64,128,128]{2,1,0:T(8,128)(2,1)S(1)}, bf16[64,128,128]{2,1,0:T(8,128)(2,1)}, u32[]{:S(2)}) copy-start(bf16[64,128,128]{2,1,0:T(8,128)(2,1)} %charges_hbm.1) | copy-start | bytes 6291460
  13.5 5.3 %copy-start.8 = (s32[1,16,32]{2,1,0:T(8,128)S(1)}, s32[1,16,32]{2,1,0:T(8,128)}, u32[]{:S(2)}) copy-start(s32[1,16,32]{2,1,0:T(8,128)} %param.16) | copy-start | bytes 6148
  13.6 5.3 %copy-start.9 = (s32[1,16,32]{2,1,0:T(8,128)S(1)}, s32[1,16,32]{2,1,0:T(8,128)}, u32[]{:S(2)}) copy-start(s32[1,16,32]{2,1,0:T(8,128)} %param.17) | copy-start | bytes 6148
  13.6 5.3 %copy-start.10 = (s32[64]{0:T(128)S(1)}, s32[64]{0:T(128)}, u32[]{:S(2)}) copy-start(s32[64]{0:T(128)} %count_ref.3) | copy-start | bytes 772
  13.6 5.3 %copy-start.11 = (s32[1,16]{1,0:T(1,128)S(1)}, s32[1,16]{1,0:T(1,128)}, u32[]{:S(2)}) copy-start(s32[1,16]{1,0:T(1,128)} %param.19) | copy-start | bytes 196
  33.6 1.8 %copy-start.3 = (bf16[128,88,128]{2,1,0:T(8,128)(2,1)S(1)}, bf16[128,88,128]{2,1,0:T(8,128)(2,1)}, u32[]{:S(2)}) copy-start(bf16[128,88,128]{2,1,0:T(8,128)(2,1)} %get-tuple-element.18.back_ref) | copy-start | bytes 8650756
  37.8 2.5 %copy-start = (bf16[128,168,128]{2,1,0:T(8,128)(2,1)}, bf16[128,168,128]{2,1,0:T(8,128)(2,1)S(1)}, u32[]{:S(2)}) copy-start(bf16[128,168,128]{2,1,0:T(8,128)(2,1)S(1)} %pack_blocks.1) | copy-start | bytes 16515076
  40.3 84.8 %all-to-all-start.1 = ((bf16[128,168,128]{2,1,0:T(8,128)(2,1)}), bf16[128,168,128]{2,1,0:T(8,128)(2,1)}, u32[]{:S(2)}, u32[]{:S(2)}) async-start(bf16[128,168,128]{2,1,0:T(8,128)(2,1)} %copy-done), calls=%async_computation.1 | async-start | bytes 11010048 | tf_op jit(solution)/shard_map/all_to_all | solution.py:413
  69.1 1.7 %copy-start.2 = (f32[65,88,128]{2,1,0:T(8,128)}, f32[65,88,128]{2,1,0:T(8,128)S(1)}, u32[]{:S(2)}) copy-start(f32[65,88,128]{2,1,0:T(8,128)S(1)} %get-tuple-element.20.local_hbm) | copy-start | bytes 8785924
  70.8 1.3 copy-start.6
  125.0 1.8 %copy-start.4 = (f32[64,88,128]{2,1,0:T(8,128)S(1)}, f32[64,88,128]{2,1,0:T(8,128)}, u32[]{:S(2)}) copy-start(f32[64,88,128]{2,1,0:T(8,128)} %get-tuple-element.19.own_hbm) | copy-start | bytes 8650756
  126.9 1.6 %copy-start.7 = (bf16[64,128,128]{2,1,0:T(8,128)(2,1)S(1)}, bf16[64,128,128]{2,1,0:T(8,128)(2,1)}, u32[]{:S(2)}) copy-start(bf16[64,128,128]{2,1,0:T(8,128)(2,1)} %copy-done.6) | copy-start | bytes 6291460

commit v2 on v0

v2 whole, which is shorter than its diff:
```python
import jax
import jax.numpy as jnp
from jax import lax
from jax.experimental import pallas as pl
from jax.experimental.pallas import tpu as pltpu
from jax.sharding import PartitionSpec as P

BF = jnp.bfloat16
F32 = jnp.float32
I32 = jnp.int32
ROWS = 88
MAIN = 80
UNROLL = 16
LIMIT = 62


def dot(a, b):
    return lax.dot_general(a, b, (((1,), (0,)), ((), ())), preferred_element_type=F32)


def params(mib):
    return pltpu.CompilerParams(vmem_limit_bytes=mib << 20)


def spread_basis(basis_ref, wide_ref):
    coeffs, cells, slots = basis_ref.shape

    def put(k, carry):
        wide_ref[pl.ds(pl.multiple_of(k * cells, cells), cells), :] = basis_ref[k].astype(F32)
        return carry

    lax.fori_loop(0, coeffs, put, 0, unroll=9)
    wide_ref[coeffs * cells :, :] = jnp.zeros(((ROWS - coeffs) * cells, slots), F32)


def masked_basis(wide_ref, count_ref, cell, cells):
    tile = wide_ref[pl.ds(cell, ROWS, stride=cells), :]
    lane = lax.broadcasted_iota(I32, tile.shape, 1)
    return jnp.where(lane < count_ref[cell], tile, 0.0)


def clear(ref, count):
    def one(e, carry):
        ref[e] = jnp.zeros(ref.shape[1:], ref.dtype)
        return carry

    lax.fori_loop(0, count, one, 0, unroll=8)


def list_doubles(fill_ref, list_ref, batches):
    def batch(b, count):
        fill = fill_ref[b]

        def double(j, carry):
            live = jnp.where(2 * j + 1 < fill, 3 << 16, 1 << 16)
            list_ref[count + j] = live + b * 64 + 2 * j
            return carry

        doubles = (fill + 1) // 2
        lax.fori_loop(0, doubles, double, 0)
        return count + doubles

    count = lax.fori_loop(0, batches, batch, 0)
    for q in range(UNROLL):
        list_ref[count + q] = 0
    return (count + UNROLL - 1) // UNROLL


def back_kernel(
    count_ref,
    target_ref,
    source_ref,
    fill_ref,
    fetch_ref,
    cotangent_hbm,
    basis_hbm,
    chosen_ref,
    back_hbm,
    own_hbm,
    forward_op_ref,
    cotangent_ref,
    basis_ref,
    wide_ref,
    grad_ref,
    total_ref,
    back_ref,
    back_op_ref,
    list_ref,
    sems,
    out_sems,
):
    cells = cotangent_ref.shape[0]
    coeffs = basis_ref.shape[0]
    batches = chosen_ref.shape[0]
    remote = back_ref.shape[0]
    parts = 4
    step = cells // parts
    basis_copy = pltpu.make_async_copy(basis_hbm, basis_ref, sems.at[0])
    basis_copy.start()
    copies = []
    for part in range(parts):
        rows = pl.ds(part * step, step)
        copy = pltpu.make_async_copy(cotangent_hbm.at[rows], cotangent_ref.at[rows], sems.at[1 + part])
        copy.start()
        copies.append(copy)

    lane = lax.broadcasted_iota(I32, (ROWS, 128), 1)

    def prepare(b, carry):
        square = chosen_ref[b].astype(F32)
        wide = jnp.pad(square, ((0, 128 - coeffs), (0, 128 - coeffs)))
        back_op_ref[b] = wide.T[:ROWS].astype(BF)
        forward_op_ref[b] = wide[:ROWS].astype(BF)
        return carry

    lax.fori_loop(0, batches, prepare, 0, unroll=2)
    turns = list_doubles(fill_ref, list_ref, batches)
    clear(total_ref, cells + remote)
    basis_copy.wait()
    spread_basis(basis_ref, wide_ref)

    def moment(i, carry):
        tile = masked_basis(wide_ref, count_ref, i, cells).astype(BF)
        grad_ref[i] = dot(tile, cotangent_ref[i]).astype(BF)
        return carry

    for part in range(parts):
        copies[part].wait()
        lax.fori_loop(part * step, (part + 1) * step, moment, 0, unroll=8)

    spare = total_ref.shape[0] - 1

    def turn(j, carry):
        for q in range(UNROLL):
            entry = list_ref[j * UNROLL + q]
            b = (entry & 0xFFFF) >> 6
            p = entry & 63
            both = jnp.concatenate([grad_ref[target_ref[b, p]], grad_ref[target_ref[b, p + 1]]], axis=1)
            result = dot(back_op_ref[b][:, :ROWS], both)
            e0 = jnp.where((entry & (1 << 16)) != 0, source_ref[b, p], spare)
            total_ref[e0] += result[:, :128]
            e1 = jnp.where((entry & (1 << 17)) != 0, source_ref[b, p + 1], spare)
            total_ref[e1] += result[:, 128:]
        return carry

    lax.fori_loop(0, turns, turn, 0)
    own_copy = pltpu.make_async_copy(total_ref.at[pl.ds(0, cells)], own_hbm, sems.at[0])
    own_copy.start()
    row = lax.broadcasted_iota(I32, (ROWS - MAIN, 128), 0)

    def narrow(s, carry):
        back_ref[s, :MAIN, :] = total_ref[cells + s, :MAIN, :].astype(BF)
        wish = fetch_ref[0, s].astype(F32)
        back_ref[s, MAIN:, :] = jnp.where(row == 1, wish, total_ref[cells + s, MAIN:, :]).astype(BF)
        return carry

    outs = []
    width = remote // parts
    for part in range(parts):
        lax.fori_loop(part * width, (part + 1) * width, narrow, 0, unroll=8)
        rows = pl.ds(part * width, width)
        copy = pltpu.make_async_copy(back_ref.at[rows], back_hbm.at[rows], out_sems.at[part])
        copy.start()
        outs.append(copy)
    for copy in outs:
        copy.wait()
    own_copy.wait()


def beside_kernel(
    count_ref,
    target_ref,
    source_ref,
    fill_ref,
    charges_hbm,
    basis_hbm,
    op_ref,
    mult_ref,
    local_ref,
    atoms_ref,
    number_ref,
    list_batch_ref,
    list_target_ref,
    list_source_ref,
    charges_ref,
    basis_ref,
    wide_ref,
    own_target,
    own_source,
    sems,
):
    cells = mult_ref.shape[0]
    batches = op_ref.shape[0]
    basis_copy = pltpu.make_async_copy(basis_hbm, basis_ref, sems.at[0])
    basis_copy.start()
    charges_copy = pltpu.make_async_copy(charges_hbm, charges_ref, sems.at[1])
    charges_copy.start()
    clear(local_ref, cells)
    basis_copy.wait()
    spread_basis(basis_ref, wide_ref)
    charges_copy.wait()

    def turn(i, carry):
        tile = masked_basis(wide_ref, count_ref, i, cells)
        mult_ref[i] = dot(tile.astype(BF), charges_ref[i]).astype(BF)
        atoms_ref[i] = jnp.pad(tile, ((0, 128 - ROWS), (0, 0))).T.astype(BF)
        return carry

    lax.fori_loop(0, cells, turn, 0, unroll=4)

    def batch(b, count):
        fill = fill_ref[b]
        base = 2 * count

        def sort(p, counts):
            own, far = counts
            source = source_ref[b, p]
            target = target_ref[b, p]
            is_own = source < cells

            @pl.when(is_own)
            def _():
                own_target[own] = target
                own_source[own] = source

            @pl.when(jnp.logical_not(is_own))
            def _():
                list_target_ref[base + far] = target
                list_source_ref[base + far] = source - cells

            step = is_own.astype(I32)
            return own + step, far + 1 - step

        own, far = lax.fori_loop(0, fill, sort, (0, 0))
        for q in range(8):
            own_target[own + q] = cells
            own_source[own + q] = 0
        list_target_ref[base + far] = cells
        list_source_ref[base + far] = 0
        doubles = (far + 1) // 2

        def mark(j, carry):
            list_batch_ref[count + j] = b
            return carry

        lax.fori_loop(0, doubles, mark, 0)
        op = op_ref[b][:, :ROWS]

        def chunk(j, carry):
            for q in range(0, 8, 2):
                p = j * 8 + q
                both = jnp.concatenate([mult_ref[own_source[p]], mult_ref[own_source[p + 1]]], axis=1)
                result = dot(op, both)
                local_ref[own_target[p]] += result[:, :128]
                local_ref[own_target[p + 1]] += result[:, 128:]
            return carry

        lax.fori_loop(0, (own + 7) // 8, chunk, 0)
        return count + doubles

    count = lax.fori_loop(0, batches, batch, 0)
    for q in range(UNROLL):
        list_batch_ref[count + q] = 0
        for side in range(2):
            list_target_ref[2 * (count + q) + side] = cells
            list_source_ref[2 * (count + q) + side] = 0
    number_ref[0] = (count + UNROLL - 1) // UNROLL


def pack_kernel(mult_hbm, back_hbm, out_hbm, asked_ref, mult_ref, back_ref, out_ref, wish_ref, sems, out_sems):
    remote = back_ref.shape[0]
    parts = 4
    step = remote // parts
    copies = []
    for part in range(parts):
        rows = pl.ds(part * step, step)
        copy = pltpu.make_async_copy(back_hbm.at[rows], back_ref.at[rows], sems.at[2 + part])
        copy.start()
        copies.append(copy)
    mult_copy = pltpu.make_async_copy(mult_hbm, mult_ref, sems.at[0])
    mult_copy.start()
    row = lax.broadcasted_iota(I32, (ROWS - MAIN, 128), 0)
    lane = lax.broadcasted_iota(I32, (ROWS - MAIN, 128), 1)

    def read(s, wish):
        tail = back_ref[s, MAIN:, :].astype(F32)
        return jnp.where((lane == s) & (row == 1), tail, wish)

    wish = jnp.zeros(row.shape, F32)
    for part in range(parts):
        copies[part].wait()
        wish = lax.fori_loop(part * step, (part + 1) * step, read, wish, unroll=16)
    wish_ref[...] = jnp.sum(wish, axis=0, keepdims=True).astype(I32)
    wish_copy = pltpu.make_async_copy(wish_ref, asked_ref, sems.at[1])
    wish_copy.start()
    mult_copy.wait()
    wish_copy.wait()

    def one(s, carry):
        out_ref[s] = mult_ref[asked_ref[0, s]]
        return carry

    outs = []
    for part in range(parts):
        lax.fori_loop(part * step, (part + 1) * step, one, 0, unroll=8)
        rows = pl.ds(part * step, step)
        copy = pltpu.make_async_copy(out_ref.at[rows], out_hbm.at[rows], out_sems.at[part])
        copy.start()
        outs.append(copy)
    for copy in outs:
        copy.wait()


def charge_kernel(asked_ref, returned_hbm, own_hbm, atoms_hbm, charge_hbm, returned_ref, own_ref, atoms_ref, charge_ref, sems):
    cells = own_ref.shape[0]
    remote = returned_ref.shape[0]
    copies = [
        pltpu.make_async_copy(src, dst, sems.at[k])
        for k, (src, dst) in enumerate(((own_hbm, own_ref), (returned_hbm, returned_ref), (atoms_hbm, atoms_ref)))
    ]
    for copy in copies:
        copy.start()
    for copy in copies:
        copy.wait()

    def collect(s, carry):
        own_ref[asked_ref[0, s]] += returned_ref[s].astype(F32)
        return carry

    lax.fori_loop(0, remote, collect, 0, unroll=4)

    row = lax.broadcasted_iota(I32, (ROWS, 128), 0)

    def atoms(i, carry):
        grads = jnp.where(row > MAIN, 0.0, own_ref[i]).astype(BF)
        charge_ref[i] = dot(atoms_ref[i][:, :ROWS], grads).astype(BF)
        return carry

    lax.fori_loop(0, cells, atoms, 0, unroll=4)
    out = pltpu.make_async_copy(charge_ref, charge_hbm, sems.at[0])
    out.start()
    out.wait()


def far_kernel(
    number_ref,
    list_batch_ref,
    list_target_ref,
    list_source_ref,
    incoming_hbm,
    local_hbm,
    atoms_hbm,
    op_hbm,
    potential_hbm,
    incoming_ref,
    local_ref,
    atoms_ref,
    op_ref,
    potential_ref,
    sems,
    out_sems,
):
    cells = atoms_ref.shape[0]
    copies = [
        pltpu.make_async_copy(src, dst, sems.at[k])
        for k, (src, dst) in enumerate(
            ((op_hbm, op_ref), (incoming_hbm, incoming_ref), (local_hbm, local_ref), (atoms_hbm, atoms_ref))
        )
    ]
    for copy in copies:
        copy.start()
    for copy in copies[:3]:
        copy.wait()

    def turn(j, carry):
        for q in range(UNROLL):
            d = j * UNROLL + q
            both = jnp.concatenate(
                [incoming_ref[list_source_ref[2 * d]], incoming_ref[list_source_ref[2 * d + 1]]], axis=1
            )
            result = dot(op_ref[list_batch_ref[d]][:, :ROWS], both)
            local_ref[list_target_ref[2 * d]] += result[:, :128]
            local_ref[list_target_ref[2 * d + 1]] += result[:, 128:]
        return carry

    lax.fori_loop(0, number_ref[0], turn, 0)
    copies[3].wait()

    def atoms(i, carry):
        potential_ref[i] = dot(atoms_ref[i][:, :ROWS], local_ref[i].astype(BF)).astype(BF)
        return carry

    outs = []
    parts = 4
    width = cells // parts
    for part in range(parts):
        lax.fori_loop(part * width, (part + 1) * width, atoms, 0, unroll=8)
        rows = pl.ds(part * width, width)
        copy = pltpu.make_async_copy(potential_ref.at[rows], potential_hbm.at[rows], out_sems.at[part])
        copy.start()
        outs.append(copy)
    for copy in outs:
        copy.wait()


SMEM = pl.BlockSpec(memory_space=pltpu.SMEM)
VMEM = pl.BlockSpec(memory_space=pltpu.VMEM)
ANY = pl.BlockSpec(memory_space=pl.ANY)
Shape = jax.ShapeDtypeStruct


def call_back(leaf_count, targets, sources, fill, wishes, cotangent, basis_major, chosen):
    coeffs, cells, slots = basis_major.shape
    domains = wishes.shape[1]
    batches, batch_size = targets.shape
    channels = cotangent.shape[2]
    return pl.pallas_call(
        back_kernel,
        out_shape=(
            Shape((domains, ROWS, channels), BF),
            Shape((cells, ROWS, channels), F32),
            Shape((batches, ROWS, 128), BF),
        ),
        in_specs=[SMEM] * 5 + [ANY] * 2 + [VMEM],
        out_specs=(ANY, ANY, VMEM),
        scratch_shapes=[
            pltpu.VMEM((cells, slots, channels), BF),
            pltpu.VMEM((coeffs, cells, slots), BF),
            pltpu.VMEM((ROWS * cells, slots), F32),
            pltpu.VMEM((cells, ROWS, channels), BF),
            pltpu.VMEM((cells + domains + 1, ROWS, channels), F32),
            pltpu.VMEM((domains, ROWS, channels), BF),
            pltpu.VMEM((batches, ROWS, 128), BF),
            pltpu.SMEM((batches * batch_size // 2 + UNROLL,), I32),
            pltpu.SemaphoreType.DMA((5,)),
            pltpu.SemaphoreType.DMA((4,)),
        ],
        compiler_params=params(LIMIT),
        name="back_pairs",
    )(leaf_count, targets, sources, fill, wishes, cotangent, basis_major, chosen)


def call_beside(leaf_count, targets, sources, fill, charges, basis_major, ops):
    coeffs, cells, slots = basis_major.shape
    batches, batch_size = targets.shape
    channels = charges.shape[2]
    doubles = batches * (batch_size // 2) + UNROLL
    return pl.pallas_call(
        beside_kernel,
        out_shape=(
            Shape((cells, ROWS, channels), BF),
            Shape((cells + 1, ROWS, channels), F32),
            Shape((cells, slots, 128), BF),
            Shape((1,), I32),
            Shape((doubles,), I32),
            Shape((2 * doubles,), I32),
            Shape((2 * doubles,), I32),
        ),
        in_specs=[SMEM] * 4 + [ANY] * 2 + [VMEM],
        out_specs=(VMEM, VMEM, VMEM, SMEM, SMEM, SMEM, SMEM),
        scratch_shapes=[
            pltpu.VMEM((cells, slots, channels), BF),
            pltpu.VMEM((coeffs, cells, slots), BF),
            pltpu.VMEM((ROWS * cells, slots), F32),
            pltpu.SMEM((batch_size + 8,), I32),
            pltpu.SMEM((batch_size + 8,), I32),
            pltpu.SemaphoreType.DMA((2,)),
        ],
        compiler_params=params(LIMIT),
        cost_estimate=pl.CostEstimate(flops=400_000_000, bytes_accessed=8_000_000, transcendentals=0),
        name="own_pairs",
    )(leaf_count, targets, sources, fill, charges, basis_major, ops)


def call_pack(mult, returned):
    cells, _, channels = mult.shape
    domains = returned.shape[0]
    return pl.pallas_call(
        pack_kernel,
        out_shape=(Shape((domains, ROWS, channels), BF), Shape((1, domains), I32)),
        in_specs=[ANY] * 2,
        out_specs=(ANY, SMEM),
        scratch_shapes=[
            pltpu.VMEM((cells, ROWS, channels), BF),
            pltpu.VMEM((domains, ROWS, channels), BF),
            pltpu.VMEM((domains, ROWS, channels), BF),
            pltpu.VMEM((1, domains), I32),
            pltpu.SemaphoreType.DMA((6,)),
            pltpu.SemaphoreType.DMA((4,)),
        ],
        compiler_params=params(LIMIT),
        name="pack_blocks",
    )(mult, returned)


def call_charge(asked, returned, own, atoms):
    cells, slots, _ = atoms.shape
    domains, _, channels = returned.shape
    return pl.pallas_call(
        charge_kernel,
        out_shape=Shape((cells, slots, channels), BF),
        in_specs=[SMEM] + [ANY] * 3,
        out_specs=ANY,
        scratch_shapes=[
            pltpu.VMEM((domains, ROWS, channels), BF),
            pltpu.VMEM((cells, ROWS, channels), F32),
            pltpu.VMEM((cells, slots, 128), BF),
            pltpu.VMEM((cells, slots, channels), BF),
            pltpu.SemaphoreType.DMA((3,)),
        ],
        compiler_params=params(LIMIT),
        cost_estimate=pl.CostEstimate(flops=200_000_000, bytes_accessed=8_000_000, transcendentals=0),
        name="charge_atoms",
    )(asked, returned, own, atoms)


def call_far(number, list_batch, list_target, list_source, incoming, local_part, atoms, ops):
    cells, slots, _ = atoms.shape
    domains, _, channels = incoming.shape
    return pl.pallas_call(
        far_kernel,
        out_shape=Shape((cells, slots, channels), BF),
        in_specs=[SMEM] * 4 + [ANY] * 4,
        out_specs=ANY,
        scratch_shapes=[
            pltpu.VMEM((domains, ROWS, channels), BF),
            pltpu.VMEM((cells + 1, ROWS, channels), F32),
            pltpu.VMEM((cells, slots, 128), BF),
            pltpu.VMEM(ops.shape, BF),
            pltpu.VMEM((cells, slots, channels), BF),
            pltpu.SemaphoreType.DMA((4,)),
            pltpu.SemaphoreType.DMA((4,)),
        ],
        compiler_params=params(LIMIT),
        name="far_pairs_atoms",
    )(number, list_batch, list_target, list_source, incoming, local_part, atoms, ops)


def choose(batch_class, m2l_ops):
    hot = (batch_class[:, None] == lax.broadcasted_iota(I32, (1, m2l_ops.shape[0]), 1)).astype(BF)
    return jnp.einsum("bn,nkl->bkl", hot, m2l_ops, preferred_element_type=F32).astype(BF)


def local(
    charges,
    basis,
    leaf_count,
    cotangent,
    m2l_ops,
    fetch_cells,
    pair_target,
    pair_source,
    batch_class,
    batch_fill,
):
    basis_major = basis.transpose(1, 0, 2)
    wishes = fetch_cells.reshape(1, -1)
    targets, sources, fill = pair_target[0], pair_source[0], batch_fill[0]
    chosen = choose(batch_class[0], m2l_ops)
    back, own, ops = call_back(leaf_count, targets, sources, fill, wishes, cotangent, basis_major, chosen)
    returned = lax.all_to_all(back, ("dx", "dy"), split_axis=0, concat_axis=0, tiled=True)
    mult, local_part, atoms, number, list_batch, list_target, list_source = call_beside(
        leaf_count, targets, sources, fill, charges, basis_major, ops
    )
    outgoing, asked = call_pack(mult, returned)
    incoming = lax.all_to_all(outgoing, ("dx", "dy"), split_axis=0, concat_axis=0, tiled=True)
    charge_grad = call_charge(asked, returned, own, atoms)
    potential = call_far(number, list_batch, list_target, list_source, incoming, local_part, atoms, ops)
    return potential, charge_grad


def solution(mesh):
    in_specs = (
        P(("dx", "dy"), None, None),
        P(("dx", "dy"), None, None),
        P(("dx", "dy")),
        P(("dx", "dy"), None, None),
        P(),
        P(("dx", "dy"), None, None),
        P(("dx", "dy"), None, None),
        P(("dx", "dy"), None, None),
        P(("dx", "dy"), None),
        P(("dx", "dy"), None),
    )
    out_specs = (P(("dx", "dy"), None, None), P(("dx", "dy"), None, None))
    return jax.shard_map(local, mesh=mesh, in_specs=in_specs, out_specs=out_specs, check_vma=False)
```

time: 351 us -> 130 us (0.37)
  matrix products: 156 us -> 5 us
  local copies, waits for them, and re-layouts: 112 us -> 0.84 us
  Pallas kernels: 0 us -> 45.7 us
  waiting for transfers between devices: 39.7 us -> 55 us
  other arithmetic: 12.3 us -> 0 us
  starting transfers between devices: 27.2 us -> 20.7 us
    dot_general x22 -> x1, matrix products: 156 us -> 5 us  [choose(): jnp.einsum('bn,nkl->bkl', hot, m2l_ops, preferred_element_type=F32)]
    reshape x9 -> x0, local copies, waits for them, and re-layouts: 48.1 us -> none  [the longest x2 16.5 us: backward_group(): picked = picked.reshape(group_size, batch_size, coeffs, channels)]
    pallas_call x0 -> x5, Pallas kernels: none -> 45.7 us  [the longest x1 13.1 us: call_beside(): pl.pallas_call(beside_kernel, out_shape=(Shape((cells, ROWS, channels), B...]
    unnamed x16 -> x0, local copies, waits for them, and re-layouts: 24.5 us -> none
    gather x4 -> x0, local copies, waits for them, and re-layouts: 14.4 us -> none  [group_slices(): return (source_rows, target_rows, active, m2l_ops[classes])]
    all_to_all x3 -> x0, local copies, waits for them, and re-layouts: 11.1 us -> none  [the longest x1 4.79 us: local(): lax.all_to_all(outgoing, ('dx', 'dy'), split_axis=0, concat_axis=0, tiled...]
    all_to_all x1, waiting for transfers between devices: 20.1 us -> 29.7 us  [local(): lax.all_to_all(outgoing, ('dx', 'dy'), split_axis=0, concat_axis=0, tiled...]
    slice x2 -> x0, local copies, waits for them, and re-layouts: 8.7 us -> none  [local(): source_grad[cells_dev:].astype(jnp.bfloat16)]
  transfers between devices with their start and end apart: 3 -> 2, of which waited for: 2 -> 2; matrix products, arithmetic and copies ran while one was open for 47% -> 0% of each run, Pallas kernels for 0% -> 17%
where the time goes in v2:
time: 130 us; the launch traced here: 128 us
  waiting for transfers between devices  55 us (42%)
  Pallas kernels  45.7 us (35%)
  starting transfers between devices  20.7 us (16%)
  matrix products  5 us (4%)
    all_to_all x1, waiting for transfers between devices, local(): lax.all_to_all(outgoing, ('dx', 'dy'), split_axis=0, concat_axis=0, tiled...  29.7 us
    all_to_all x1, waiting for transfers between devices, local(): lax.all_to_all(back, ('dx', 'dy'), split_axis=0, concat_axis=0, tiled=True)  25.3 us
    all_to_all x1, starting transfers between devices, local(): lax.all_to_all(back, ('dx', 'dy'), split_axis=0, concat_axis=0, tiled=True)  15.1 us
    pallas_call x1, Pallas kernels, call_beside(): pl.pallas_call(beside_kernel, out_shape=(Shape((cells, ROWS, channels), B...  13.1 us
    pallas_call x1, Pallas kernels, call_back(): pl.pallas_call(back_kernel, out_shape=(Shape((domains, ROWS, channels), B...  11 us
    pallas_call x1, Pallas kernels, call_charge(): pl.pallas_call(charge_kernel, out_shape=Shape((cells, slots, channels), B...  8.88 us
    pallas_call x1, Pallas kernels, call_far(): pl.pallas_call(far_kernel, out_shape=Shape((cells, slots, channels), BF),...  8.02 us
    all_to_all x1, starting transfers between devices, local(): lax.all_to_all(outgoing, ('dx', 'dy'), split_axis=0, concat_axis=0, tiled...  5.62 us
  transfers between devices with their start and end apart: 2, of which 2 were waited for; matrix products, arithmetic and copies ran while one was open for 0% of the time, Pallas kernels for 17%

profile of v2, /device:TPU:1, one launch (start us, length us, event | category | flops | bytes accessed | tf_op | source)
XLA Modules:
  0.0 128.0 jit_solution(278376709574816628)
XLA Ops:
  0.6 5.0 %convolution_convert_fusion = bf16[16,81,81]{2,0,1:T(8,128)(2,1)S(1)} fusion(bf16[316,81,81]{0,2,1:T(8,128)(2,1)} %param.14, s32[16]{0:T(128)} %bitcast.18), kind=kOutput, calls=%fused_computation | convolution fusion | flops 66454864 | bytes 4356568 | tf_op jit(solution)/shard_map/bn,nkl->bkl/dot_general | solution.py:541
  5.6 0.8 copy.13.chosen_ref
  6.5 11.0 %back_pairs.1 = (bf16[128,88,128]{2,1,0:T(8,128)(2,1)}, f32[64,88,128]{2,1,0:T(8,128)}, bf16[16,88,128]{2,1,0:T(8,128)(2,1)}) custom-call(s32[64]{0:T(128)} %count_ref.3, s32[16,32]{1,0:T(8,128)} %bitcast.12, s32[16,32]{1,0:T(8,128)} %bitcast.14, s32[16]{0:T(128)} %bitcast.16, s32[1,128]{1,0:T(1,128)} %bitcast.19, bf16[64,128,128]{2,1,0:T(8,128)(2,1)} %cotangent_hbm.1, ...), custom_call_target="tpu_custom_call" | custom-call | tf_op jit(solution)/shard_map/back_pairs/pallas_call | solution.py:417
  17.5 15.1 %all-to-all-start = ((bf16[128,88,128]{2,1,0:T(8,128)(2,1)}), bf16[128,88,128]{2,1,0:T(8,128)(2,1)}, u32[]{:S(2)}, u32[]{:S(2)}) async-start(bf16[128,88,128]{2,1,0:T(8,128)(2,1)} %get-tuple-element.20), calls=%async_computation | async-start | bytes 5767168 | tf_op jit(solution)/shard_map/all_to_all | solution.py:561
  32.7 13.1 %own_pairs.1 = (bf16[64,88,128]{2,1,0:T(8,128)(2,1)}, f32[65,88,128]{2,1,0:T(8,128)}, bf16[64,128,128]{2,1,0:T(8,128)(2,1)}, s32[1]{0:T(128)}, s32[272]{0:T(512)}, /*index=5*/s32[544]{0:T(1024)}, s32[544]{0:T(1024)}) custom-call(s32[64]{0:T(128)} %count_ref.3, s32[16,32]{1,0:T(8,128)} %bitcast.13, s32[16,32]{1,0:T(8,128)} %bitcast.15, s32[16]{0:T(128)} %bitcast.17, ...), custom_call_target="tpu_custom_call" | custom-call | flops 400000000 | bytes 8000000 | tf_op jit(solution)/shard_map/own_pairs/pallas_call | solution.py:448
  45.8 25.3 %all-to-all-done.back_hbm.returned_hbm = bf16[128,88,128]{2,1,0:T(8,128)(2,1)} async-done(((bf16[128,88,128]{2,1,0:T(8,128)(2,1)}), bf16[128,88,128]{2,1,0:T(8,128)(2,1)}, u32[]{:S(2)}, u32[]{:S(2)}) %all-to-all-start) | async-done | bytes 2883616 | tf_op jit(solution)/shard_map/all_to_all | solution.py:561
  71.1 4.7 %pack_blocks.1 = (bf16[128,88,128]{2,1,0:T(8,128)(2,1)}, s32[1,128]{1,0:T(1,128)}) custom-call(bf16[64,88,128]{2,1,0:T(8,128)(2,1)} %get-tuple-element.19.mult_hbm, bf16[128,88,128]{2,1,0:T(8,128)(2,1)} %all-to-all-done.back_hbm.returned_hbm), custom_call_target="tpu_custom_call" | custom-call | tf_op jit(solution)/shard_map/pack_blocks/pallas_call | solution.py:478
  75.8 5.6 %all-to-all-start.1 = ((bf16[128,88,128]{2,1,0:T(8,128)(2,1)}), bf16[128,88,128]{2,1,0:T(8,128)(2,1)}, u32[]{:S(2)}, u32[]{:S(2)}) async-start(bf16[128,88,128]{2,1,0:T(8,128)(2,1)} %get-tuple-element.21), calls=%async_computation.1 | async-start | bytes 5767168 | tf_op jit(solution)/shard_map/all_to_all | solution.py:566
  81.4 8.9 %charge_atoms.1 = bf16[64,128,128]{2,1,0:T(8,128)(2,1)} custom-call(s32[1,128]{1,0:T(1,128)} %get-tuple-element.24.asked_ref, bf16[128,88,128]{2,1,0:T(8,128)(2,1)} %all-to-all-done.back_hbm.returned_hbm, f32[64,88,128]{2,1,0:T(8,128)} %get-tuple-element.25.own_hbm, bf16[64,128,128]{2,1,0:T(8,128)(2,1)} %get-tuple-element.23.atoms_hbm), custom_call_target="tpu_custom_call" | custom-call | flops 200000000 | bytes 8000000 | tf_op jit(solution)/shard_map/charge_atoms/pallas_call | solution.py:499
  90.3 29.7 %all-to-all-done.1.incoming_hbm = bf16[128,88,128]{2,1,0:T(8,128)(2,1)} async-done(((bf16[128,88,128]{2,1,0:T(8,128)(2,1)}), bf16[128,88,128]{2,1,0:T(8,128)(2,1)}, u32[]{:S(2)}, u32[]{:S(2)}) %all-to-all-start.1) | async-done | bytes 2883616 | tf_op jit(solution)/shard_map/all_to_all | solution.py:566
  120.0 8.0 %far_pairs_atoms.1 = bf16[64,128,128]{2,1,0:T(8,128)(2,1)} custom-call(s32[1]{0:T(128)} %get-tuple-element.15.number_ref, s32[272]{0:T(512)} %get-tuple-element.16.list_batch_ref, s32[544]{0:T(1024)} %get-tuple-element.17.list_target_ref, s32[544]{0:T(1024)} %get-tuple-element.18.list_source_ref, bf16[128,88,128]{2,1,0:T(8,128)(2,1)} %all-to-all-done.1.incoming_hbm, ...), custom_call_target="tpu_custom_call" | custom-call | tf_op jit(solution)/shard_map/far_pairs_atoms/pallas_call | solution.py:520
Async XLA Ops:
  17.5 53.6 %all-to-all-start = ((bf16[128,88,128]{2,1,0:T(8,128)(2,1)}), bf16[128,88,128]{2,1,0:T(8,128)(2,1)}, u32[]{:S(2)}, u32[]{:S(2)}) async-start(bf16[128,88,128]{2,1,0:T(8,128)(2,1)} %get-tuple-element.20), calls=%async_computation | async-start | bytes 5767168 | tf_op jit(solution)/shard_map/all_to_all | solution.py:561
  75.8 44.2 %all-to-all-start.1 = ((bf16[128,88,128]{2,1,0:T(8,128)(2,1)}), bf16[128,88,128]{2,1,0:T(8,128)(2,1)}, u32[]{:S(2)}, u32[]{:S(2)}) async-start(bf16[128,88,128]{2,1,0:T(8,128)(2,1)} %get-tuple-element.21), calls=%async_computation.1 | async-start | bytes 5767168 | tf_op jit(solution)/shard_map/all_to_all | solution.py:566

commit v3 on v2

v3 whole, which is shorter than its diff:
```python
import jax
import jax.numpy as jnp
from jax import lax
from jax.experimental import pallas as pl
from jax.experimental.pallas import tpu as pltpu
from jax.sharding import PartitionSpec as P

BF = jnp.bfloat16
F32 = jnp.float32
I32 = jnp.int32
ROWS = 88
MAIN = 80
KEEP = 82
STRIDE = 72
UNROLL = 16
LIMIT = 62


def dot(a, b):
    return lax.dot_general(a, b, (((1,), (0,)), ((), ())), preferred_element_type=F32)


def params():
    return pltpu.CompilerParams(vmem_limit_bytes=LIMIT << 20)


def flat(ref):
    return ref.reshape(ref.shape[0] * KEEP, ref.shape[-1])


def block(index):
    return pl.ds(pl.multiple_of(index * KEEP, 2), KEEP)


def spread_basis(basis_ref, wide_ref):
    coeffs, cells, slots = basis_ref.shape

    def put(k, carry):
        wide_ref[pl.ds(pl.multiple_of(k * STRIDE, 8), cells), :] = basis_ref[k].astype(F32)
        return carry

    lax.fori_loop(0, coeffs, put, 0, unroll=9)
    wide_ref[coeffs * STRIDE :, :] = jnp.zeros(((ROWS - coeffs) * STRIDE, slots), F32)


def masked_basis(wide_ref, count_ref, cell):
    tile = wide_ref[pl.ds(cell, ROWS, stride=STRIDE), :]
    lane = lax.broadcasted_iota(I32, tile.shape, 1)
    return jnp.where(lane < count_ref[cell], tile, 0.0)


def clear(ref, count):
    def one(e, carry):
        ref[e] = jnp.zeros(ref.shape[1:], ref.dtype)
        return carry

    lax.fori_loop(0, count, one, 0, unroll=8)


def encode(batch, entry, target):
    return batch * 65536 + entry * 256 + target


def decode(code):
    return code >> 16, (code >> 8) & 255, code & 255


def back_kernel(
    count_ref,
    target_ref,
    source_ref,
    fill_ref,
    fetch_ref,
    cotangent_hbm,
    basis_hbm,
    chosen_hbm,
    back_hbm,
    cotangent_ref,
    basis_ref,
    chosen_ref,
    wide_ref,
    grad_ref,
    total_ref,
    back_ref,
    back_op_ref,
    list_ref,
    sems,
    out_sems,
):
    cells = cotangent_ref.shape[0]
    coeffs = basis_ref.shape[0]
    batches, batch_size = target_ref.shape
    remote = back_ref.shape[0]
    parts = 4
    step = cells // parts
    basis_copy = pltpu.make_async_copy(basis_hbm, basis_ref, sems.at[0])
    basis_copy.start()
    copies = []
    for part in range(parts):
        rows = pl.ds(part * step, step)
        copy = pltpu.make_async_copy(cotangent_hbm.at[rows], cotangent_ref.at[rows], sems.at[2 + part])
        copy.start()
        copies.append(copy)
    chosen_copy = pltpu.make_async_copy(chosen_hbm, chosen_ref, sems.at[1])
    chosen_copy.start()
    clear(total_ref, remote)
    basis_copy.wait()
    spread_basis(basis_ref, wide_ref)

    share = cells // batches
    slots = batch_size // share
    dummy = encode(0, remote, 0)

    def moments(b, place):
        fill = fill_ref[b]
        for q in range(share):
            i = b * share + q
            tile = masked_basis(wide_ref, count_ref, i).astype(BF)
            grad_ref[i] = dot(tile, cotangent_ref[i]).astype(BF)
            for p in range(q * slots, (q + 1) * slots):
                entry = source_ref[b, p] - cells
                list_ref[place] = encode(b, entry, target_ref[b, p])
                place += jnp.where((p < fill) & (entry >= 0), 1, 0)
        list_ref[place] = dummy
        return ((place + 1) // 2) * 2

    place = 0
    for part in range(parts):
        copies[part].wait()
        place = lax.fori_loop(part * batches // parts, (part + 1) * batches // parts, moments, place)
    for q in range(2 * UNROLL):
        list_ref[place + q] = dummy
    turns = (place + 2 * UNROLL - 1) // (2 * UNROLL)
    chosen_copy.wait()

    def prepare(b, carry):
        wide = jnp.pad(chosen_ref[b].astype(F32), ((0, 128 - coeffs), (0, 128 - coeffs)))
        back_op_ref[b] = wide.T[:ROWS].astype(BF)
        return carry

    lax.fori_loop(0, batches, prepare, 0, unroll=4)

    def turn(j, carry):
        for q in range(UNROLL):
            d = 2 * (j * UNROLL + q)
            b, e0, t0 = decode(list_ref[d])
            _, e1, t1 = decode(list_ref[d + 1])
            result = dot(back_op_ref[b][:, :ROWS], jnp.concatenate([grad_ref[t0], grad_ref[t1]], axis=1))
            total_ref[e0] += result[:, :128]
            total_ref[e1] += result[:, 128:]
        return carry

    lax.fori_loop(0, turns, turn, 0)
    row = lax.broadcasted_iota(I32, (ROWS - MAIN, 128), 0)
    packed = flat(back_ref)

    def narrow(s, carry):
        tail = jnp.where(row == 1, fetch_ref[0, s].astype(F32), total_ref[s, MAIN:, :])
        tile = jnp.concatenate([total_ref[s, :MAIN, :], tail], axis=0).astype(BF)
        packed[block(s), :] = tile[:KEEP]
        return carry

    outs = []
    width = remote // parts
    for part in range(parts):
        lax.fori_loop(part * width, (part + 1) * width, narrow, 0, unroll=8)
        rows = pl.ds(part * width, width)
        copy = pltpu.make_async_copy(back_ref.at[rows], back_hbm.at[rows], out_sems.at[part])
        copy.start()
        outs.append(copy)
    for copy in outs:
        copy.wait()


def beside_kernel(
    count_ref,
    target_ref,
    source_ref,
    fill_ref,
    charges_hbm,
    cotangent_hbm,
    basis_hbm,
    chosen_ref,
    mult_hbm,
    local_ref,
    own_ref,
    atoms_ref,
    op_ref,
    list_ref,
    charges_ref,
    cotangent_ref,
    basis_ref,
    wide_ref,
    mult_ref,
    packed_ref,
    grad_ref,
    back_op_ref,
    own_target,
    own_source,
    sems,
):
    cells = mult_ref.shape[0]
    coeffs = basis_ref.shape[0]
    batches, _, _ = chosen_ref.shape
    copies = [
        pltpu.make_async_copy(src, dst, sems.at[k])
        for k, (src, dst) in enumerate(
            ((basis_hbm, basis_ref), (charges_hbm, charges_ref), (cotangent_hbm, cotangent_ref))
        )
    ]
    for copy in copies:
        copy.start()
    clear(local_ref, cells)
    clear(own_ref, cells)
    for copy in copies:
        copy.wait()
    spread_basis(basis_ref, wide_ref)
    packed = flat(packed_ref)

    def turn(i, carry):
        tile = masked_basis(wide_ref, count_ref, i)
        both = jnp.concatenate([charges_ref[i], cotangent_ref[i]], axis=1)
        result = dot(tile.astype(BF), both).astype(BF)
        mult_ref[i] = result[:, :128]
        packed[block(i), :] = result[:KEEP, :128]
        grad_ref[i] = result[:, 128:]
        atoms_ref[i] = jnp.pad(tile, ((0, 128 - ROWS), (0, 0))).T.astype(BF)
        return carry

    lax.fori_loop(0, cells, turn, 0, unroll=4)
    mult_copy = pltpu.make_async_copy(packed_ref, mult_hbm, sems.at[0])
    mult_copy.start()

    def prepare(b, carry):
        wide = jnp.pad(chosen_ref[b].astype(F32), ((0, 128 - coeffs), (0, 128 - coeffs)))
        back_op_ref[b] = wide.T[:ROWS].astype(BF)
        op_ref[b] = wide[:ROWS].astype(BF)
        return carry

    lax.fori_loop(0, batches, prepare, 0, unroll=2)
    dummy = encode(0, 0, cells)

    def batch(b, place):
        fill = fill_ref[b]

        def sort(p, places):
            own, far = places
            entry = source_ref[b, p] - cells
            target = target_ref[b, p]
            is_far = entry >= 0

            @pl.when(is_far)
            def _():
                list_ref[far] = encode(b, entry, target)

            @pl.when(jnp.logical_not(is_far))
            def _():
                own_target[own] = target
                own_source[own] = entry + cells

            step = is_far.astype(I32)
            return own + 1 - step, far + step

        own, far = lax.fori_loop(0, fill, sort, (0, place))
        list_ref[far] = dummy
        for q in range(8):
            own_target[own + q] = cells
            own_source[own + q] = cells
        op = op_ref[b][:, :ROWS]
        back_op = back_op_ref[b][:, :ROWS]

        def chunk(j, carry):
            for q in range(0, 8, 2):
                t0, t1 = own_target[j * 8 + q], own_target[j * 8 + q + 1]
                e0, e1 = own_source[j * 8 + q], own_source[j * 8 + q + 1]
                result = dot(op, jnp.concatenate([mult_ref[jnp.minimum(e0, cells - 1)], mult_ref[jnp.minimum(e1, cells - 1)]], axis=1))
                local_ref[t0] += result[:, :128]
                local_ref[t1] += result[:, 128:]
                result = dot(back_op, jnp.concatenate([grad_ref[jnp.minimum(t0, cells - 1)], grad_ref[jnp.minimum(t1, cells - 1)]], axis=1))
                own_ref[e0] += result[:, :128]
                own_ref[e1] += result[:, 128:]
            return carry

        lax.fori_loop(0, (own + 7) // 8, chunk, 0)
        return ((far + 1) // 2) * 2

    place = lax.fori_loop(0, batches, batch, 2)
    for q in range(2 * UNROLL):
        list_ref[place + q] = dummy
    list_ref[0] = (place - 2 + 2 * UNROLL - 1) // (2 * UNROLL)
    list_ref[1] = 0
    mult_copy.wait()


def pack_kernel(mult_hbm, back_hbm, out_hbm, asked_ref, mult_ref, tail_ref, wish_ref, sems):
    remote = back_hbm.shape[0]
    tail_copy = pltpu.make_async_copy(back_hbm.at[:, pl.ds(MAIN // 2, 1)], tail_ref, sems.at[0])
    tail_copy.start()
    mult_copy = pltpu.make_async_copy(mult_hbm, mult_ref, sems.at[1])
    mult_copy.start()
    row = lax.broadcasted_iota(I32, (16, 128), 0)
    lane = lax.broadcasted_iota(I32, (16, 128), 1)
    tails = tail_ref.reshape(2 * remote, 128)
    tail_copy.wait()
    wish = jnp.zeros((16, 128), F32)
    for g in range(remote // 8):
        tile = tails[16 * g : 16 * g + 16, :].astype(F32)
        wish = jnp.where(row == 2 * (lane - 8 * g) + 1, tile, wish)
    wish_ref[...] = jnp.sum(wish, axis=0, keepdims=True).astype(I32)
    wish_copy = pltpu.make_async_copy(wish_ref, asked_ref, sems.at[2])
    wish_copy.start()
    mult_copy.wait()
    wish_copy.wait()

    def one(s, carry):
        pltpu.make_async_copy(mult_ref.at[asked_ref[0, s]], out_hbm.at[s], sems.at[3]).start()
        return carry

    lax.fori_loop(0, remote, one, 0, unroll=8)
    pltpu.make_async_copy(back_hbm, out_hbm, sems.at[3]).wait()


def charge_kernel(asked_ref, returned_hbm, own_hbm, atoms_hbm, charge_hbm, returned_ref, own_ref, atoms_ref, charge_ref, sems):
    cells = charge_ref.shape[0]
    remote = returned_ref.shape[0]
    copies = [
        pltpu.make_async_copy(src, dst, sems.at[k])
        for k, (src, dst) in enumerate(((own_hbm, own_ref), (returned_hbm, returned_ref), (atoms_hbm, atoms_ref)))
    ]
    for copy in copies:
        copy.start()
    for copy in copies:
        copy.wait()
    packed = flat(returned_ref)

    def collect(s, carry):
        own_ref[asked_ref[0, s], :KEEP, :] += packed[block(s), :].astype(F32)
        return carry

    lax.fori_loop(0, remote, collect, 0, unroll=4)
    row = lax.broadcasted_iota(I32, (ROWS, 128), 0)

    def atoms(i, carry):
        grads = jnp.where(row > MAIN, 0.0, own_ref[i]).astype(BF)
        charge_ref[i] = dot(atoms_ref[i][:, :ROWS], grads).astype(BF)
        return carry

    lax.fori_loop(0, cells, atoms, 0, unroll=4)
    out = pltpu.make_async_copy(charge_ref, charge_hbm, sems.at[0])
    out.start()
    out.wait()


def far_kernel(
    list_ref,
    incoming_hbm,
    local_hbm,
    atoms_hbm,
    op_hbm,
    potential_hbm,
    incoming_ref,
    local_ref,
    atoms_ref,
    op_ref,
    sum_ref,
    potential_ref,
    sems,
    out_sems,
):
    cells = atoms_ref.shape[0]
    copies = [
        pltpu.make_async_copy(src, dst, sems.at[k])
        for k, (src, dst) in enumerate(
            ((op_hbm, op_ref), (incoming_hbm, incoming_ref), (local_hbm, local_ref), (atoms_hbm, atoms_ref))
        )
    ]
    for copy in copies:
        copy.start()
    clear(sum_ref, cells)
    packed = flat(incoming_ref)
    for copy in copies[:2]:
        copy.wait()

    def turn(j, carry):
        for q in range(UNROLL):
            d = 2 * (j * UNROLL + q + 1)
            b, e0, t0 = decode(list_ref[d])
            _, e1, t1 = decode(list_ref[d + 1])
            both = jnp.concatenate([packed[block(e0), :], packed[block(e1), :]], axis=1)
            result = dot(op_ref[b][:, :KEEP], both)
            sum_ref[t0] += result[:, :128]
            sum_ref[t1] += result[:, 128:]
        return carry

    lax.fori_loop(0, list_ref[0], turn, 0)
    for copy in copies[2:]:
        copy.wait()

    def atoms(i, carry):
        whole = (sum_ref[i] + local_ref[i]).astype(BF)
        potential_ref[i] = dot(atoms_ref[i][:, :ROWS], whole).astype(BF)
        return carry

    outs = []
    parts = 4
    width = cells // parts
    for part in range(parts):
        lax.fori_loop(part * width, (part + 1) * width, atoms, 0, unroll=8)
        rows = pl.ds(part * width, width)
        copy = pltpu.make_async_copy(potential_ref.at[rows], potential_hbm.at[rows], out_sems.at[part])
        copy.start()
        outs.append(copy)
    for copy in outs:
        copy.wait()


SMEM = pl.BlockSpec(memory_space=pltpu.SMEM)
VMEM = pl.BlockSpec(memory_space=pltpu.VMEM)
ANY = pl.BlockSpec(memory_space=pl.ANY)
Shape = jax.ShapeDtypeStruct


def call_back(leaf_count, targets, sources, fill, wishes, cotangent, basis_major, chosen):
    coeffs, cells, slots = basis_major.shape
    domains = wishes.shape[1]
    batches, batch_size = targets.shape
    channels = cotangent.shape[2]
    return pl.pallas_call(
        back_kernel,
        out_shape=Shape((domains, KEEP // 2, 2, channels), BF),
        in_specs=[SMEM] * 5 + [ANY] * 3,
        out_specs=ANY,
        scratch_shapes=[
            pltpu.VMEM((cells, slots, channels), BF),
            pltpu.VMEM((coeffs, cells, slots), BF),
            pltpu.VMEM(chosen.shape, BF),
            pltpu.VMEM((ROWS * STRIDE, slots), F32),
            pltpu.VMEM((cells, ROWS, channels), BF),
            pltpu.VMEM((domains + 1, ROWS, channels), F32),
            pltpu.VMEM((domains, KEEP // 2, 2, channels), BF),
            pltpu.VMEM((batches, ROWS, 128), BF),
            pltpu.SMEM((batches * batch_size + 2 * UNROLL + 2,), I32),
            pltpu.SemaphoreType.DMA((6,)),
            pltpu.SemaphoreType.DMA((4,)),
        ],
        compiler_params=params(),
        name="back_pairs",
    )(leaf_count, targets, sources, fill, wishes, cotangent, basis_major, chosen)


def call_beside(leaf_count, targets, sources, fill, charges, cotangent, basis_major, chosen):
    coeffs, cells, slots = basis_major.shape
    batches, batch_size = targets.shape
    channels = charges.shape[2]
    return pl.pallas_call(
        beside_kernel,
        out_shape=(
            Shape((cells, KEEP // 2, 2, channels), BF),
            Shape((cells + 1, ROWS, channels), F32),
            Shape((cells + 1, ROWS, channels), F32),
            Shape((cells, slots, 128), BF),
            Shape((batches, ROWS, 128), BF),
            Shape((batches * batch_size + 2 * UNROLL + 4,), I32),
        ),
        in_specs=[SMEM] * 4 + [ANY] * 3 + [VMEM],
        out_specs=(ANY, VMEM, VMEM, VMEM, VMEM, SMEM),
        scratch_shapes=[
            pltpu.VMEM((cells, slots, channels), BF),
            pltpu.VMEM((cells, slots, channels), BF),
            pltpu.VMEM((coeffs, cells, slots), BF),
            pltpu.VMEM((ROWS * STRIDE, slots), F32),
            pltpu.VMEM((cells, ROWS, channels), BF),
            pltpu.VMEM((cells, KEEP // 2, 2, channels), BF),
            pltpu.VMEM((cells, ROWS, channels), BF),
            pltpu.VMEM((batches, ROWS, 128), BF),
            pltpu.SMEM((batch_size + 8,), I32),
            pltpu.SMEM((batch_size + 8,), I32),
            pltpu.SemaphoreType.DMA((3,)),
        ],
        compiler_params=params(),
        cost_estimate=pl.CostEstimate(flops=400_000_000, bytes_accessed=8_000_000, transcendentals=0),
        name="own_pairs",
    )(leaf_count, targets, sources, fill, charges, cotangent, basis_major, chosen)


def call_pack(mult, returned):
    cells, _, _, channels = mult.shape
    domains = returned.shape[0]
    return pl.pallas_call(
        pack_kernel,
        out_shape=(Shape(returned.shape, BF), Shape((1, domains), I32)),
        in_specs=[ANY] * 2,
        out_specs=(ANY, SMEM),
        scratch_shapes=[
            pltpu.VMEM(mult.shape, BF),
            pltpu.VMEM((domains, 1, 2, channels), BF),
            pltpu.VMEM((1, domains), I32),
            pltpu.SemaphoreType.DMA((4,)),
        ],
        compiler_params=params(),
        name="pack_blocks",
    )(mult, returned)


def call_charge(asked, returned, own, atoms):
    cells, slots, _ = atoms.shape
    channels = returned.shape[3]
    return pl.pallas_call(
        charge_kernel,
        out_shape=Shape((cells, slots, channels), BF),
        in_specs=[SMEM] + [ANY] * 3,
        out_specs=ANY,
        scratch_shapes=[
            pltpu.VMEM(returned.shape, BF),
            pltpu.VMEM(own.shape, F32),
            pltpu.VMEM((cells, slots, 128), BF),
            pltpu.VMEM((cells, slots, channels), BF),
            pltpu.SemaphoreType.DMA((3,)),
        ],
        compiler_params=params(),
        cost_estimate=pl.CostEstimate(flops=200_000_000, bytes_accessed=8_000_000, transcendentals=0),
        name="charge_atoms",
    )(asked, returned, own, atoms)


def call_far(pairs, incoming, local_part, atoms, ops):
    cells, slots, _ = atoms.shape
    channels = incoming.shape[3]
    return pl.pallas_call(
        far_kernel,
        out_shape=Shape((cells, slots, channels), BF),
        in_specs=[SMEM] + [ANY] * 4,
        out_specs=ANY,
        scratch_shapes=[
            pltpu.VMEM(incoming.shape, BF),
            pltpu.VMEM(local_part.shape, F32),
            pltpu.VMEM((cells, slots, 128), BF),
            pltpu.VMEM(ops.shape, BF),
            pltpu.VMEM((cells + 1, ROWS, channels), F32),
            pltpu.VMEM((cells, slots, channels), BF),
            pltpu.SemaphoreType.DMA((4,)),
            pltpu.SemaphoreType.DMA((4,)),
        ],
        compiler_params=params(),
        name="far_pairs_atoms",
    )(pairs, incoming, local_part, atoms, ops)


def choose(batch_class, m2l_ops):
    hot = (batch_class[:, None] == lax.broadcasted_iota(I32, (1, m2l_ops.shape[0]), 1)).astype(BF)
    return jnp.einsum("bn,nkl->bkl", hot, m2l_ops, preferred_element_type=F32).astype(BF)


def local(
    charges,
    basis,
    leaf_count,
    cotangent,
    m2l_ops,
    fetch_cells,
    pair_target,
    pair_source,
    batch_class,
    batch_fill,
):
    basis_major = basis.transpose(1, 0, 2)
    wishes = fetch_cells.reshape(1, -1)
    targets, sources, fill = pair_target[0], pair_source[0], batch_fill[0]
    chosen = choose(batch_class[0], m2l_ops)
    back = call_back(leaf_count, targets, sources, fill, wishes, cotangent, basis_major, chosen)
    returned = lax.all_to_all(back, ("dx", "dy"), split_axis=0, concat_axis=0, tiled=True)
    mult, local_part, own, atoms, ops, pairs = call_beside(
        leaf_count, targets, sources, fill, charges, cotangent, basis_major, chosen
    )
    outgoing, asked = call_pack(mult, returned)
    incoming = lax.all_to_all(outgoing, ("dx", "dy"), split_axis=0, concat_axis=0, tiled=True)
    charge_grad = call_charge(asked, returned, own, atoms)
    potential = call_far(pairs, incoming, local_part, atoms, ops)
    return potential, charge_grad


def solution(mesh):
    in_specs = (
        P(("dx", "dy"), None, None),
        P(("dx", "dy"), None, None),
        P(("dx", "dy")),
        P(("dx", "dy"), None, None),
        P(),
        P(("dx", "dy"), None, None),
        P(("dx", "dy"), None, None),
        P(("dx", "dy"), None, None),
        P(("dx", "dy"), None),
        P(("dx", "dy"), None),
    )
    out_specs = (P(("dx", "dy"), None, None), P(("dx", "dy"), None, None))
    return jax.shard_map(local, mesh=mesh, in_specs=in_specs, out_specs=out_specs, check_vma=False)
```

time: 130 us -> 121 us (0.931); the launches traced: 128 us -> 121 us
  waiting for transfers between devices: 55 us -> 45.6 us
  Pallas kernels: 45.7 us -> 49.7 us
  starting transfers between devices: 20.7 us -> 18.7 us
    all_to_all x1, waiting for transfers between devices: 25.3 us -> 19.2 us  [local(): lax.all_to_all(back, ('dx', 'dy'), split_axis=0, concat_axis=0, tiled=True)]
    pallas_call x3, Pallas kernels: 28.8 us -> 32.4 us  [the longest x1 17.2 us: call_beside(): pl.pallas_call(beside_kernel, out_shape=(Shape((cells, KEEP // 2, 2, chan...]
    all_to_all x1, waiting for transfers between devices: 29.7 us -> 26.4 us  [local(): lax.all_to_all(outgoing, ('dx', 'dy'), split_axis=0, concat_axis=0, tiled...]
    all_to_all x1, starting transfers between devices: 15.1 us -> 13.2 us  [local(): lax.all_to_all(back, ('dx', 'dy'), split_axis=0, concat_axis=0, tiled=True)]
  transfers between devices with their start and end apart: 2 -> 2, of which waited for: 2 -> 2; matrix products, arithmetic and copies ran while one was open for 0% -> 0% of each run, Pallas kernels for 17% -> 23%
where the time goes in v3:
time: 121 us
  Pallas kernels  49.7 us (41%)
  waiting for transfers between devices  45.6 us (38%)
  starting transfers between devices  18.7 us (15%)
  matrix products  5 us (4%)
    all_to_all x1, waiting for transfers between devices, local(): lax.all_to_all(outgoing, ('dx', 'dy'), split_axis=0, concat_axis=0, tiled...  26.4 us
    all_to_all x1, waiting for transfers between devices, local(): lax.all_to_all(back, ('dx', 'dy'), split_axis=0, concat_axis=0, tiled=True)  19.2 us
    pallas_call x1, Pallas kernels, call_beside(): pl.pallas_call(beside_kernel, out_shape=(Shape((cells, KEEP // 2, 2, chan...  17.2 us
    all_to_all x1, starting transfers between devices, local(): lax.all_to_all(back, ('dx', 'dy'), split_axis=0, concat_axis=0, tiled=True)  13.2 us
    pallas_call x1, Pallas kernels, call_back(): pl.pallas_call(back_kernel, out_shape=Shape((domains, KEEP // 2, 2, chann...  11.6 us
    pallas_call x1, Pallas kernels, call_charge(): pl.pallas_call(charge_kernel, out_shape=Shape((cells, slots, channels), B...  10.1 us
    pallas_call x1, Pallas kernels, call_far(): pl.pallas_call(far_kernel, out_shape=Shape((cells, slots, channels), BF),...  7.31 us
    all_to_all x1, starting transfers between devices, local(): lax.all_to_all(outgoing, ('dx', 'dy'), split_axis=0, concat_axis=0, tiled...  5.57 us
  transfers between devices with their start and end apart: 2, of which 2 were waited for; matrix products, arithmetic and copies ran while one was open for 0% of the time, Pallas kernels for 23%

profile of v3, /device:TPU:1, one launch (start us, length us, event | category | flops | bytes accessed | tf_op | source)
XLA Modules:
  0.0 120.6 jit_solution(9117632985062509353)
XLA Ops:
  0.6 5.0 %fusion.1 = bf16[16,81,81]{2,0,1:T(8,128)(2,1)S(1)} fusion(bf16[316,81,81]{0,2,1:T(8,128)(2,1)} %param.14, s32[16]{0:T(128)} %bitcast.18), kind=kOutput, calls=%fused_computation.3 | convolution fusion | flops 66349888 | bytes 4356568 | tf_op jit(solution)/shard_map/bn,nkl->bkl/dot_general | solution.py:551
  5.6 0.8 copy.14.chosen_ref.chosen_hbm
  6.5 11.6 %back_pairs.1 = bf16[128,41,2,128]{3,2,1,0:T(2,128)(2,1)} custom-call(s32[64]{0:T(128)} %count_ref.3, s32[16,32]{1,0:T(8,128)} %bitcast.12, s32[16,32]{1,0:T(8,128)} %bitcast.14, s32[16]{0:T(128)} %bitcast.16, s32[1,128]{1,0:T(1,128)} %bitcast.19, bf16[64,128,128]{2,1,0:T(8,128)(2,1)} %cotangent_hbm.3, bf16[81,64,128]{2,1,0:T(8,128)(2,1)} %bitcast.10, ...), custom_call_target="tpu_custom_call" | custom-call | tf_op jit(solution)/shard_map/back_pairs/pallas_call | solution.py:428
  18.1 13.2 %all-to-all-start = ((bf16[128,41,2,128]{3,2,1,0:T(2,128)(2,1)}), bf16[128,41,2,128]{3,2,1,0:T(2,128)(2,1)}, u32[]{:S(2)}, u32[]{:S(2)}) async-start(bf16[128,41,2,128]{3,2,1,0:T(2,128)(2,1)} %back_pairs.1), calls=%async_computation | async-start | bytes 5373952 | tf_op jit(solution)/shard_map/all_to_all | solution.py:571
  31.2 17.2 %own_pairs.1 = (bf16[64,41,2,128]{3,2,1,0:T(2,128)(2,1)}, f32[65,88,128]{2,1,0:T(8,128)}, f32[65,88,128]{2,1,0:T(8,128)}, bf16[64,128,128]{2,1,0:T(8,128)(2,1)},...) custom-call(s32[64]{0:T(128)} %count_ref.3, s32[16,32]{1,0:T(8,128)} %bitcast.13, s32[16,32]{1,0:T(8,128)} %bitcast.15, ...), custom_call_target="tpu_custom_call" | custom-call | flops 400000000 | bytes 8000000 | tf_op jit(solution)/shard_map/own_pairs/pallas_call | solution.py:455
  48.4 19.2 %all-to-all-done.back_hbm.returned_hbm = bf16[128,41,2,128]{3,2,1,0:T(2,128)(2,1)} async-done(((bf16[128,41,2,128]{3,2,1,0:T(2,128)(2,1)}), bf16[128,41,2,128]{3,2,1,0:T(2,128)(2,1)}, u32[]{:S(2)}, u32[]{:S(2)}) %all-to-all-start) | async-done | bytes 2687008 | tf_op jit(solution)/shard_map/all_to_all | solution.py:571
  67.6 3.6 %pack_blocks.1 = (bf16[128,41,2,128]{3,2,1,0:T(2,128)(2,1)}, s32[1,128]{1,0:T(1,128)}) custom-call(bf16[64,41,2,128]{3,2,1,0:T(2,128)(2,1)} %get-tuple-element.11.mult_hbm, bf16[128,41,2,128]{3,2,1,0:T(2,128)(2,1)} %all-to-all-done.back_hbm.returned_hbm), custom_call_target="tpu_custom_call" | custom-call | tf_op jit(solution)/shard_map/pack_blocks/pallas_call | solution.py:489
  71.2 5.6 %all-to-all-start.1 = ((bf16[128,41,2,128]{3,2,1,0:T(2,128)(2,1)}), bf16[128,41,2,128]{3,2,1,0:T(2,128)(2,1)}, u32[]{:S(2)}, u32[]{:S(2)}) async-start(bf16[128,41,2,128]{3,2,1,0:T(2,128)(2,1)} %get-tuple-element.12), calls=%async_computation.1 | async-start | bytes 5373952 | tf_op jit(solution)/shard_map/all_to_all | solution.py:576
  76.8 10.1 %charge_atoms.1 = bf16[64,128,128]{2,1,0:T(8,128)(2,1)} custom-call(s32[1,128]{1,0:T(1,128)} %get-tuple-element.16.asked_ref, bf16[128,41,2,128]{3,2,1,0:T(2,128)(2,1)} %all-to-all-done.back_hbm.returned_hbm, f32[65,88,128]{2,1,0:T(8,128)} %get-tuple-element.17.own_hbm, bf16[64,128,128]{2,1,0:T(8,128)(2,1)} %get-tuple-element.14.atoms_hbm), custom_call_target="tpu_custom_call" | custom-call | flops 200000000 | bytes 8000000 | tf_op jit(solution)/shard_map/charge_atoms/pallas_call | solution.py:508
  86.9 26.4 %all-to-all-done.1.incoming_hbm = bf16[128,41,2,128]{3,2,1,0:T(2,128)(2,1)} async-done(((bf16[128,41,2,128]{3,2,1,0:T(2,128)(2,1)}), bf16[128,41,2,128]{3,2,1,0:T(2,128)(2,1)}, u32[]{:S(2)}, u32[]{:S(2)}) %all-to-all-start.1) | async-done | bytes 2687008 | tf_op jit(solution)/shard_map/all_to_all | solution.py:576
  113.3 7.3 %far_pairs_atoms.1 = bf16[64,128,128]{2,1,0:T(8,128)(2,1)} custom-call(s32[548]{0:T(1024)} %get-tuple-element.10.list_ref, bf16[128,41,2,128]{3,2,1,0:T(2,128)(2,1)} %all-to-all-done.1.incoming_hbm, f32[65,88,128]{2,1,0:T(8,128)} %get-tuple-element.13.local_hbm, bf16[64,128,128]{2,1,0:T(8,128)(2,1)} %get-tuple-element.14.atoms_hbm, ...), custom_call_target="tpu_custom_call" | custom-call | tf_op jit(solution)/shard_map/far_pairs_atoms/pallas_call | solution.py:529
Async XLA Ops:
  18.1 49.6 %all-to-all-start = ((bf16[128,41,2,128]{3,2,1,0:T(2,128)(2,1)}), bf16[128,41,2,128]{3,2,1,0:T(2,128)(2,1)}, u32[]{:S(2)}, u32[]{:S(2)}) async-start(bf16[128,41,2,128]{3,2,1,0:T(2,128)(2,1)} %back_pairs.1), calls=%async_computation | async-start | bytes 5373952 | tf_op jit(solution)/shard_map/all_to_all | solution.py:571
  71.2 42.1 %all-to-all-start.1 = ((bf16[128,41,2,128]{3,2,1,0:T(2,128)(2,1)}), bf16[128,41,2,128]{3,2,1,0:T(2,128)(2,1)}, u32[]{:S(2)}, u32[]{:S(2)}) async-start(bf16[128,41,2,128]{3,2,1,0:T(2,128)(2,1)} %get-tuple-element.12), calls=%async_computation.1 | async-start | bytes 5373952 | tf_op jit(solution)/shard_map/all_to_all | solution.py:576

commit v4 on v3

--- a/solution.py
+++ b/solution.py
@@ -65,26 +65,51 @@
     return code >> 16, (code >> 8) & 255, code & 255
 
 
+def choose_operators(class_ref, ops_ref, rows_ref):
+    coeffs, _, classes = ops_ref.shape
+    batches = rows_ref.shape[0] // ROWS
+    rows_ref[...] = jnp.zeros(rows_ref.shape, F32)
+    row = lax.broadcasted_iota(I32, (batches, classes), 0)
+    wanted = jnp.zeros((batches, classes), I32)
+    for b in range(batches):
+        wanted = jnp.where(row == b, class_ref[b], wanted)
+    hot = (wanted == lax.broadcasted_iota(I32, (batches, classes), 1)).astype(F32).astype(BF)
+
+    def one(k, carry):
+        picked = lax.dot_general(hot, ops_ref[k], (((1,), (1,)), ((), ())), preferred_element_type=F32)
+        rows_ref[pl.ds(pl.multiple_of(k * batches, batches), batches), :coeffs] = picked
+        return carry
+
+    return one
+
+
 def back_kernel(
     count_ref,
+    fill_ref,
+    fetch_ref,
+    class_ref,
     target_ref,
     source_ref,
-    fill_ref,
-    fetch_ref,
     cotangent_hbm,
     basis_hbm,
-    chosen_hbm,
+    ops_hbm,
     back_hbm,
+    op_hbm,
     cotangent_ref,
     basis_ref,
-    chosen_ref,
+    ops_ref,
     wide_ref,
+    rows_ref,
     grad_ref,
     total_ref,
     back_ref,
+    op_ref,
     back_op_ref,
+    found_ref,
+    code_ref,
     list_ref,
     sems,
+    ops_sems,
     out_sems,
 ):
     cells = cotangent_ref.shape[0]
@@ -93,52 +118,81 @@
     remote = back_ref.shape[0]
     parts = 4
     step = cells // parts
-    basis_copy = pltpu.make_async_copy(basis_hbm, basis_ref, sems.at[0])
+    span = coeffs // parts
+    basis_copy = pltpu.make_async_copy(basis_hbm, basis_ref, sems.at[parts])
     basis_copy.start()
-    copies = []
+
+    def cotangent_copy(part):
+        rows = pl.ds(part * step, step)
+        return pltpu.make_async_copy(cotangent_hbm.at[rows], cotangent_ref.at[rows], sems.at[part])
+
+    def ops_copy(part):
+        rows = pl.ds(part * span, span)
+        return pltpu.make_async_copy(ops_hbm.at[rows], ops_ref.at[rows], ops_sems.at[part])
+
     for part in range(parts):
-        rows = pl.ds(part * step, step)
-        copy = pltpu.make_async_copy(cotangent_hbm.at[rows], cotangent_ref.at[rows], sems.at[2 + part])
-        copy.start()
-        copies.append(copy)
-    chosen_copy = pltpu.make_async_copy(chosen_hbm, chosen_ref, sems.at[1])
-    chosen_copy.start()
+        cotangent_copy(part).start()
+        ops_copy(part).start()
+    rows = pl.ds(parts * span, coeffs - parts * span)
+    rest_copy = pltpu.make_async_copy(ops_hbm.at[rows], ops_ref.at[rows], ops_sems.at[parts])
+    rest_copy.start()
+
+    batch = lax.broadcasted_iota(I32, (batches, batch_size), 0)
+    slot = lax.broadcasted_iota(I32, (batches, batch_size), 1)
+    fill = jnp.zeros((batches, batch_size), I32)
+    for b in range(batches):
+        fill = jnp.where(batch == b, fill_ref[b], fill)
+    entry = source_ref[...] - cells
+    far = (slot < fill) & (entry >= 0)
+    found_ref[...] = jnp.where(far, encode(batch, entry, target_ref[...]), -1)
+    code_copy = pltpu.make_async_copy(found_ref, code_ref, sems.at[parts + 1])
+    code_copy.start()
     clear(total_ref, remote)
+    choose = choose_operators(class_ref, ops_ref, rows_ref)
     basis_copy.wait()
     spread_basis(basis_ref, wide_ref)
+    code_copy.wait()
 
     share = cells // batches
     slots = batch_size // share
     dummy = encode(0, remote, 0)
-
-    def moments(b, place):
-        fill = fill_ref[b]
-        for q in range(share):
-            i = b * share + q
-            tile = masked_basis(wide_ref, count_ref, i).astype(BF)
-            grad_ref[i] = dot(tile, cotangent_ref[i]).astype(BF)
-            for p in range(q * slots, (q + 1) * slots):
-                entry = source_ref[b, p] - cells
-                list_ref[place] = encode(b, entry, target_ref[b, p])
-                place += jnp.where((p < fill) & (entry >= 0), 1, 0)
-        list_ref[place] = dummy
-        return ((place + 1) // 2) * 2
-
-    place = 0
-    for part in range(parts):
-        copies[part].wait()
-        place = lax.fori_loop(part * batches // parts, (part + 1) * batches // parts, moments, place)
+    group = batches // parts
+
+    def moments(part, place):
+        cotangent_copy(part).wait()
+        ops_copy(part).wait()
+        for b in range(group):
+            for k in range(b * span // group, (b + 1) * span // group):
+                choose(part * span + k, 0)
+            for q in range(share):
+                i = (part * group + b) * share + q
+                tile = masked_basis(wide_ref, count_ref, i).astype(BF)
+                grad_ref[i] = dot(tile, cotangent_ref[i]).astype(BF)
+                for p in range(q * slots, (q + 1) * slots):
+                    code = code_ref[part * group + b, p]
+                    list_ref[place] = code
+                    place += 1 + (code >> 31)
+            list_ref[place] = dummy
+            place = ((place + 1) >> 1) << 1
+        return place
+
+    place = lax.fori_loop(0, parts, moments, 0)
     for q in range(2 * UNROLL):
         list_ref[place + q] = dummy
     turns = (place + 2 * UNROLL - 1) // (2 * UNROLL)
-    chosen_copy.wait()
+    rest_copy.wait()
+    for k in range(parts * span, coeffs):
+        choose(k, 0)
 
     def prepare(b, carry):
-        wide = jnp.pad(chosen_ref[b].astype(F32), ((0, 128 - coeffs), (0, 128 - coeffs)))
-        back_op_ref[b] = wide.T[:ROWS].astype(BF)
+        wide = rows_ref[pl.ds(b, ROWS, stride=batches), :]
+        op_ref[b] = wide.astype(BF)
+        back_op_ref[b] = jnp.pad(wide, ((0, 128 - ROWS), (0, 0))).T[:ROWS].astype(BF)
         return carry
 
     lax.fori_loop(0, batches, prepare, 0, unroll=4)
+    op_copy = pltpu.make_async_copy(op_ref, op_hbm, sems.at[parts])
+    op_copy.start()
 
     def turn(j, carry):
         for q in range(UNROLL):
@@ -160,16 +214,23 @@
         packed[block(s), :] = tile[:KEEP]
         return carry
 
-    outs = []
-    width = remote // parts
-    for part in range(parts):
-        lax.fori_loop(part * width, (part + 1) * width, narrow, 0, unroll=8)
+    pieces = 8
+    width = remote // pieces
+
+    def send(part):
         rows = pl.ds(part * width, width)
-        copy = pltpu.make_async_copy(back_ref.at[rows], back_hbm.at[rows], out_sems.at[part])
-        copy.start()
-        outs.append(copy)
-    for copy in outs:
-        copy.wait()
+        return pltpu.make_async_copy(back_ref.at[rows], back_hbm.at[rows], out_sems.at[part])
+
+    def ship(part, carry):
+        for q in range(width):
+            narrow(part * width + q, 0)
+        send(part).start()
+        return carry
+
+    lax.fori_loop(0, pieces, ship, 0)
+    op_copy.wait()
+    for part in range(pieces):
+        send(part).wait()
 
 
 def beside_kernel(
@@ -180,12 +241,11 @@
     charges_hbm,
     cotangent_hbm,
     basis_hbm,
-    chosen_ref,
+    op_ref,
     mult_hbm,
     local_ref,
     own_ref,
     atoms_ref,
-    op_ref,
     list_ref,
     charges_ref,
     cotangent_ref,
@@ -200,8 +260,7 @@
     sems,
 ):
     cells = mult_ref.shape[0]
-    coeffs = basis_ref.shape[0]
-    batches, _, _ = chosen_ref.shape
+    batches = op_ref.shape[0]
     copies = [
         pltpu.make_async_copy(src, dst, sems.at[k])
         for k, (src, dst) in enumerate(
@@ -232,9 +291,8 @@
     mult_copy.start()
 
     def prepare(b, carry):
-        wide = jnp.pad(chosen_ref[b].astype(F32), ((0, 128 - coeffs), (0, 128 - coeffs)))
+        wide = jnp.pad(op_ref[b].astype(F32), ((0, 128 - ROWS), (0, 0)))
         back_op_ref[b] = wide.T[:ROWS].astype(BF)
-        op_ref[b] = wide[:ROWS].astype(BF)
         return carry
 
     lax.fori_loop(0, batches, prepare, 0, unroll=2)
@@ -405,7 +463,7 @@
     parts = 4
     width = cells // parts
     for part in range(parts):
-        lax.fori_loop(part * width, (part + 1) * width, atoms, 0, unroll=8)
+        lax.fori_loop(part * width, (part + 1) * width, atoms, 0, unroll=16)
         rows = pl.ds(part * width, width)
         copy = pltpu.make_async_copy(potential_ref.at[rows], potential_hbm.at[rows], out_sems.at[part])
         copy.start()
@@ -420,35 +478,43 @@
 Shape = jax.ShapeDtypeStruct
 
 
-def call_back(leaf_count, targets, sources, fill, wishes, cotangent, basis_major, chosen):
+def call_back(leaf_count, fill, wishes, batch_class, targets, sources, cotangent, basis_major, ops_major):
     coeffs, cells, slots = basis_major.shape
     domains = wishes.shape[1]
     batches, batch_size = targets.shape
     channels = cotangent.shape[2]
     return pl.pallas_call(
         back_kernel,
-        out_shape=Shape((domains, KEEP // 2, 2, channels), BF),
-        in_specs=[SMEM] * 5 + [ANY] * 3,
-        out_specs=ANY,
+        out_shape=(
+            Shape((domains, KEEP // 2, 2, channels), BF),
+            Shape((batches, ROWS, 128), BF),
+        ),
+        in_specs=[SMEM] * 4 + [VMEM] * 2 + [ANY] * 3,
+        out_specs=(ANY, ANY),
         scratch_shapes=[
             pltpu.VMEM((cells, slots, channels), BF),
             pltpu.VMEM((coeffs, cells, slots), BF),
-            pltpu.VMEM(chosen.shape, BF),
+            pltpu.VMEM(ops_major.shape, BF),
             pltpu.VMEM((ROWS * STRIDE, slots), F32),
+            pltpu.VMEM((ROWS * batches, 128), F32),
             pltpu.VMEM((cells, ROWS, channels), BF),
             pltpu.VMEM((domains + 1, ROWS, channels), F32),
             pltpu.VMEM((domains, KEEP // 2, 2, channels), BF),
             pltpu.VMEM((batches, ROWS, 128), BF),
+            pltpu.VMEM((batches, ROWS, 128), BF),
+            pltpu.VMEM((batches, batch_size), I32),
+            pltpu.SMEM((batches, batch_size), I32),
             pltpu.SMEM((batches * batch_size + 2 * UNROLL + 2,), I32),
             pltpu.SemaphoreType.DMA((6,)),
-            pltpu.SemaphoreType.DMA((4,)),
+            pltpu.SemaphoreType.DMA((5,)),
+            pltpu.SemaphoreType.DMA((8,)),
         ],
         compiler_params=params(),
         name="back_pairs",
-    )(leaf_count, targets, sources, fill, wishes, cotangent, basis_major, chosen)
-
-
-def call_beside(leaf_count, targets, sources, fill, charges, cotangent, basis_major, chosen):
+    )(leaf_count, fill, wishes, batch_class, targets, sources, cotangent, basis_major, ops_major)
+
+
+def call_beside(leaf_count, targets, sources, fill, charges, cotangent, basis_major, ops):
     coeffs, cells, slots = basis_major.shape
     batches, batch_size = targets.shape
     channels = charges.shape[2]
@@ -459,11 +525,10 @@
             Shape((cells + 1, ROWS, channels), F32),
             Shape((cells + 1, ROWS, channels), F32),
             Shape((cells, slots, 128), BF),
-            Shape((batches, ROWS, 128), BF),
             Shape((batches * batch_size + 2 * UNROLL + 4,), I32),
         ),
         in_specs=[SMEM] * 4 + [ANY] * 3 + [VMEM],
-        out_specs=(ANY, VMEM, VMEM, VMEM, VMEM, SMEM),
+        out_specs=(ANY, VMEM, VMEM, VMEM, SMEM),
         scratch_shapes=[
             pltpu.VMEM((cells, slots, channels), BF),
             pltpu.VMEM((cells, slots, channels), BF),
@@ -480,7 +545,7 @@
         compiler_params=params(),
         cost_estimate=pl.CostEstimate(flops=400_000_000, bytes_accessed=8_000_000, transcendentals=0),
         name="own_pairs",
-    )(leaf_count, targets, sources, fill, charges, cotangent, basis_major, chosen)
+    )(leaf_count, targets, sources, fill, charges, cotangent, basis_major, ops)
 
 
 def call_pack(mult, returned):
@@ -546,11 +611,6 @@
     )(pairs, incoming, local_part, atoms, ops)
 
 
-def choose(batch_class, m2l_ops):
-    hot = (batch_class[:, None] == lax.broadcasted_iota(I32, (1, m2l_ops.shape[0]), 1)).astype(BF)
-    return jnp.einsum("bn,nkl->bkl", hot, m2l_ops, preferred_element_type=F32).astype(BF)
-
-
 def local(
     charges,
     basis,
@@ -566,11 +626,12 @@
     basis_major = basis.transpose(1, 0, 2)
     wishes = fetch_cells.reshape(1, -1)
     targets, sources, fill = pair_target[0], pair_source[0], batch_fill[0]
-    chosen = choose(batch_class[0], m2l_ops)
-    back = call_back(leaf_count, targets, sources, fill, wishes, cotangent, basis_major, chosen)
+    back, ops = call_back(
+        leaf_count, fill, wishes, batch_class[0], targets, sources, cotangent, basis_major, m2l_ops.transpose(1, 2, 0)
+    )
     returned = lax.all_to_all(back, ("dx", "dy"), split_axis=0, concat_axis=0, tiled=True)
-    mult, local_part, own, atoms, ops, pairs = call_beside(
-        leaf_count, targets, sources, fill, charges, cotangent, basis_major, chosen
+    mult, local_part, own, atoms, pairs = call_beside(
+        leaf_count, targets, sources, fill, charges, cotangent, basis_major, ops
     )
     outgoing, asked = call_pack(mult, returned)
     incoming = lax.all_to_all(outgoing, ("dx", "dy"), split_axis=0, concat_axis=0, tiled=True)

time: 121 us -> 114 us (0.942)
  matrix products: 5 us -> 0 us
  Pallas kernels: 49.7 us -> 52.4 us
  waiting for transfers between devices: 45.6 us -> 43.6 us
    dot_general x1 -> x0, matrix products: 5 us -> none  [choose(): jnp.einsum('bn,nkl->bkl', hot, m2l_ops, preferred_element_type=F32)]
    all_to_all x1, waiting for transfers between devices: 19.2 us -> 17.2 us  [local(): lax.all_to_all(back, ('dx', 'dy'), split_axis=0, concat_axis=0, tiled=True)]
    pallas_call x1, Pallas kernels: 17.2 us -> 19.2 us  [call_beside(): pl.pallas_call(beside_kernel, out_shape=(Shape((cells, KEEP // 2, 2, chan...]
    all_to_all x1, starting transfers between devices: 13.2 us -> 11.9 us  [local(): lax.all_to_all(back, ('dx', 'dy'), split_axis=0, concat_axis=0, tiled=True)]
  transfers between devices with their start and end apart: 2 -> 2, of which waited for: 2 -> 2; matrix products, arithmetic and copies ran while one was open for 0% -> 0% of each run, Pallas kernels for 23% -> 26%
where the time goes in v4:
time: 114 us
  Pallas kernels  52.4 us (46%)
  waiting for transfers between devices  43.6 us (38%)
  starting transfers between devices  17.5 us (15%)
    all_to_all x1, waiting for transfers between devices, local(): lax.all_to_all(outgoing, ('dx', 'dy'), split_axis=0, concat_axis=0, tiled...  26.4 us
    pallas_call x1, Pallas kernels, call_beside(): pl.pallas_call(beside_kernel, out_shape=(Shape((cells, KEEP // 2, 2, chan...  19.2 us
    all_to_all x1, waiting for transfers between devices, local(): lax.all_to_all(back, ('dx', 'dy'), split_axis=0, concat_axis=0, tiled=True)  17.2 us
    pallas_call x1, Pallas kernels, call_back(): pl.pallas_call(back_kernel, out_shape=(Shape((domains, KEEP // 2, 2, chan...  12.3 us
    all_to_all x1, starting transfers between devices, local(): lax.all_to_all(back, ('dx', 'dy'), split_axis=0, concat_axis=0, tiled=True)  11.9 us
    pallas_call x1, Pallas kernels, call_charge(): pl.pallas_call(charge_kernel, out_shape=Shape((cells, slots, channels), B...  10.1 us
    pallas_call x1, Pallas kernels, call_far(): pl.pallas_call(far_kernel, out_shape=Shape((cells, slots, channels), BF),...  7.29 us
    all_to_all x1, starting transfers between devices, local(): lax.all_to_all(outgoing, ('dx', 'dy'), split_axis=0, concat_axis=0, tiled...  5.57 us
  transfers between devices with their start and end apart: 2, of which 2 were waited for; matrix products, arithmetic and copies ran while one was open for 0% of the time, Pallas kernels for 26%

profile of v4, /device:TPU:1, one launch (start us, length us, event | category | flops | bytes accessed | tf_op | source)
XLA Modules:
  0.0 114.2 jit_solution(12641776782423170175)
XLA Ops:
  0.6 12.3 %back_pairs.1 = (bf16[128,41,2,128]{3,2,1,0:T(2,128)(2,1)}, bf16[16,88,128]{2,1,0:T(8,128)(2,1)}) custom-call(s32[64]{0:T(128)} %count_ref.3, s32[16]{0:T(128)} %bitcast.14, s32[1,128]{1,0:T(1,128)} %bitcast.16, s32[16]{0:T(128)} %bitcast.17, s32[16,32]{1,0:T(8,128)} %bitcast.10, s32[16,32]{1,0:T(8,128)} %bitcast.12, bf16[64,128,128]{2,1,0:T(8,128)(2,1)} %cotangent_hbm.3, ...), custom_call_target="tpu_custom_call" | custom-call | tf_op jit(solution)/shard_map/back_pairs/pallas_call | solution.py:486
  12.9 11.9 %all-to-all-start = ((bf16[128,41,2,128]{3,2,1,0:T(2,128)(2,1)}), bf16[128,41,2,128]{3,2,1,0:T(2,128)(2,1)}, u32[]{:S(2)}, u32[]{:S(2)}) async-start(bf16[128,41,2,128]{3,2,1,0:T(2,128)(2,1)} %get-tuple-element.14), calls=%async_computation | async-start | bytes 5373952 | tf_op jit(solution)/shard_map/all_to_all | solution.py:632
  24.8 19.2 %own_pairs.1 = (bf16[64,41,2,128]{3,2,1,0:T(2,128)(2,1)}, f32[65,88,128]{2,1,0:T(8,128)}, f32[65,88,128]{2,1,0:T(8,128)}, bf16[64,128,128]{2,1,0:T(8,128)(2,1)}, s32[548]{0:T(1024)}) custom-call(s32[64]{0:T(128)} %count_ref.3, s32[16,32]{1,0:T(8,128)} %bitcast.11, s32[16,32]{1,0:T(8,128)} %bitcast.13, s32[16]{0:T(128)} %bitcast.15, ...), custom_call_target="tpu_custom_call" | custom-call | flops 400000000 | bytes 8000000 | tf_op jit(solution)/shard_map/own_pairs/pallas_call | solution.py:521
  44.0 17.2 %all-to-all-done.back_hbm.returned_hbm = bf16[128,41,2,128]{3,2,1,0:T(2,128)(2,1)} async-done(((bf16[128,41,2,128]{3,2,1,0:T(2,128)(2,1)}), bf16[128,41,2,128]{3,2,1,0:T(2,128)(2,1)}, u32[]{:S(2)}, u32[]{:S(2)}) %all-to-all-start) | async-done | bytes 2687008 | tf_op jit(solution)/shard_map/all_to_all | solution.py:632
  61.2 3.6 %pack_blocks.1 = (bf16[128,41,2,128]{3,2,1,0:T(2,128)(2,1)}, s32[1,128]{1,0:T(1,128)}) custom-call(bf16[64,41,2,128]{3,2,1,0:T(2,128)(2,1)} %get-tuple-element.13.mult_hbm, bf16[128,41,2,128]{3,2,1,0:T(2,128)(2,1)} %all-to-all-done.back_hbm.returned_hbm), custom_call_target="tpu_custom_call" | custom-call | tf_op jit(solution)/shard_map/pack_blocks/pallas_call | solution.py:554
  64.9 5.6 %all-to-all-start.1 = ((bf16[128,41,2,128]{3,2,1,0:T(2,128)(2,1)}), bf16[128,41,2,128]{3,2,1,0:T(2,128)(2,1)}, u32[]{:S(2)}, u32[]{:S(2)}) async-start(bf16[128,41,2,128]{3,2,1,0:T(2,128)(2,1)} %get-tuple-element.15), calls=%async_computation.1 | async-start | bytes 5373952 | tf_op jit(solution)/shard_map/all_to_all | solution.py:637
  70.4 10.1 %charge_atoms.1 = bf16[64,128,128]{2,1,0:T(8,128)(2,1)} custom-call(s32[1,128]{1,0:T(1,128)} %get-tuple-element.18.asked_ref, bf16[128,41,2,128]{3,2,1,0:T(2,128)(2,1)} %all-to-all-done.back_hbm.returned_hbm, f32[65,88,128]{2,1,0:T(8,128)} %get-tuple-element.19.own_hbm, bf16[64,128,128]{2,1,0:T(8,128)(2,1)} %get-tuple-element.17.atoms_hbm), custom_call_target="tpu_custom_call" | custom-call | flops 200000000 | bytes 8000000 | tf_op jit(solution)/shard_map/charge_atoms/pallas_call | solution.py:573
  80.5 26.4 %all-to-all-done.1.incoming_hbm = bf16[128,41,2,128]{3,2,1,0:T(2,128)(2,1)} async-done(((bf16[128,41,2,128]{3,2,1,0:T(2,128)(2,1)}), bf16[128,41,2,128]{3,2,1,0:T(2,128)(2,1)}, u32[]{:S(2)}, u32[]{:S(2)}) %all-to-all-start.1) | async-done | bytes 2687008 | tf_op jit(solution)/shard_map/all_to_all | solution.py:637
  107.0 7.3 %far_pairs_atoms.1 = bf16[64,128,128]{2,1,0:T(8,128)(2,1)} custom-call(s32[548]{0:T(1024)} %get-tuple-element.12.list_ref, bf16[128,41,2,128]{3,2,1,0:T(2,128)(2,1)} %all-to-all-done.1.incoming_hbm, f32[65,88,128]{2,1,0:T(8,128)} %get-tuple-element.16.local_hbm, bf16[64,128,128]{2,1,0:T(8,128)(2,1)} %get-tuple-element.17.atoms_hbm, ...), custom_call_target="tpu_custom_call" | custom-call | tf_op jit(solution)/shard_map/far_pairs_atoms/pallas_call | solution.py:594
Async XLA Ops:
  12.9 48.3 %all-to-all-start = ((bf16[128,41,2,128]{3,2,1,0:T(2,128)(2,1)}), bf16[128,41,2,128]{3,2,1,0:T(2,128)(2,1)}, u32[]{:S(2)}, u32[]{:S(2)}) async-start(bf16[128,41,2,128]{3,2,1,0:T(2,128)(2,1)} %get-tuple-element.14), calls=%async_computation | async-start | bytes 5373952 | tf_op jit(solution)/shard_map/all_to_all | solution.py:632
  64.9 42.1 %all-to-all-start.1 = ((bf16[128,41,2,128]{3,2,1,0:T(2,128)(2,1)}), bf16[128,41,2,128]{3,2,1,0:T(2,128)(2,1)}, u32[]{:S(2)}, u32[]{:S(2)}) async-start(bf16[128,41,2,128]{3,2,1,0:T(2,128)(2,1)} %get-tuple-element.15), calls=%async_computation.1 | async-start | bytes 5373952 | tf_op jit(solution)/shard_map/all_to_all | solution.py:637

commit v5 on v4

--- a/solution.py
+++ b/solution.py
@@ -20,8 +20,8 @@
     return lax.dot_general(a, b, (((1,), (0,)), ((), ())), preferred_element_type=F32)
 
 
-def params():
-    return pltpu.CompilerParams(vmem_limit_bytes=LIMIT << 20)
+def params(mib=LIMIT):
+    return pltpu.CompilerParams(vmem_limit_bytes=mib << 20)
 
 
 def flat(ref):
@@ -47,6 +47,21 @@
     tile = wide_ref[pl.ds(cell, ROWS, stride=STRIDE), :]
     lane = lax.broadcasted_iota(I32, tile.shape, 1)
     return jnp.where(lane < count_ref[cell], tile, 0.0)
+
+
+class Split:
+    def __init__(self, src, dst, sem, pieces):
+        self.src, self.dst, self.sem, self.pieces = src, dst, sem, pieces
+
+    def start(self):
+        size = self.src.shape[0]
+        edges = [size * k // self.pieces for k in range(self.pieces + 1)]
+        for low, high in zip(edges, edges[1:]):
+            rows = pl.ds(low, high - low)
+            pltpu.make_async_copy(self.src.at[rows], self.dst.at[rows], self.sem).start()
+
+    def wait(self):
+        pltpu.make_async_copy(self.src, self.dst, self.sem).wait()
 
 
 def clear(ref, count):
@@ -84,17 +99,23 @@
 
 
 def back_kernel(
+    count_hbm,
+    fill_hbm,
+    fetch_hbm,
+    class_hbm,
+    target_hbm,
+    source_hbm,
+    cotangent_hbm,
+    basis_hbm,
+    ops_hbm,
+    back_hbm,
+    op_hbm,
     count_ref,
     fill_ref,
     fetch_ref,
     class_ref,
     target_ref,
     source_ref,
-    cotangent_hbm,
-    basis_hbm,
-    ops_hbm,
-    back_hbm,
-    op_hbm,
     cotangent_ref,
     basis_ref,
     ops_ref,
@@ -108,6 +129,7 @@
     found_ref,
     code_ref,
     list_ref,
+    small_sems,
     sems,
     ops_sems,
     out_sems,
@@ -115,12 +137,27 @@
     cells = cotangent_ref.shape[0]
     coeffs = basis_ref.shape[0]
     batches, batch_size = target_ref.shape
+    small_copies = [
+        pltpu.make_async_copy(src, dst, small_sems.at[k])
+        for k, (src, dst) in enumerate(
+            (
+                (fill_hbm, fill_ref),
+                (target_hbm, target_ref),
+                (source_hbm, source_ref),
+                (class_hbm, class_ref),
+                (count_hbm, count_ref),
+                (fetch_hbm, fetch_ref),
+            )
+        )
+    ]
     remote = back_ref.shape[0]
     parts = 4
     step = cells // parts
     span = coeffs // parts
-    basis_copy = pltpu.make_async_copy(basis_hbm, basis_ref, sems.at[parts])
+    basis_copy = Split(basis_hbm, basis_ref, sems.at[parts], 9)
     basis_copy.start()
+    for copy in small_copies:
+        copy.start()
 
     def cotangent_copy(part):
         rows = pl.ds(part * step, step)
@@ -136,6 +173,9 @@
     rows = pl.ds(parts * span, coeffs - parts * span)
     rest_copy = pltpu.make_async_copy(ops_hbm.at[rows], ops_ref.at[rows], ops_sems.at[parts])
     rest_copy.start()
+    clear(total_ref, remote)
+    for copy in small_copies:
+        copy.wait()
 
     batch = lax.broadcasted_iota(I32, (batches, batch_size), 0)
     slot = lax.broadcasted_iota(I32, (batches, batch_size), 1)
@@ -147,7 +187,6 @@
     found_ref[...] = jnp.where(far, encode(batch, entry, target_ref[...]), -1)
     code_copy = pltpu.make_async_copy(found_ref, code_ref, sems.at[parts + 1])
     code_copy.start()
-    clear(total_ref, remote)
     choose = choose_operators(class_ref, ops_ref, rows_ref)
     basis_copy.wait()
     spread_basis(basis_ref, wide_ref)
@@ -354,7 +393,7 @@
     remote = back_hbm.shape[0]
     tail_copy = pltpu.make_async_copy(back_hbm.at[:, pl.ds(MAIN // 2, 1)], tail_ref, sems.at[0])
     tail_copy.start()
-    mult_copy = pltpu.make_async_copy(mult_hbm, mult_ref, sems.at[1])
+    mult_copy = Split(mult_hbm, mult_ref, sems.at[1], 8)
     mult_copy.start()
     row = lax.broadcasted_iota(I32, (16, 128), 0)
     lane = lax.broadcasted_iota(I32, (16, 128), 1)
@@ -410,13 +449,13 @@
 
 
 def far_kernel(
-    list_ref,
-    incoming_hbm,
+    list_hbm,
+    incoming_ref,
     local_hbm,
     atoms_hbm,
     op_hbm,
     potential_hbm,
-    incoming_ref,
+    list_ref,
     local_ref,
     atoms_ref,
     op_ref,
@@ -427,9 +466,14 @@
 ):
     cells = atoms_ref.shape[0]
     copies = [
-        pltpu.make_async_copy(src, dst, sems.at[k])
-        for k, (src, dst) in enumerate(
-            ((op_hbm, op_ref), (incoming_hbm, incoming_ref), (local_hbm, local_ref), (atoms_hbm, atoms_ref))
+        Split(src, dst, sems.at[k], pieces)
+        for k, (src, dst, pieces) in enumerate(
+            (
+                (list_hbm, list_ref, 1),
+                (op_hbm, op_ref, 2),
+                (atoms_hbm, atoms_ref, 4),
+                (local_hbm, local_ref, 5),
+            )
         )
     ]
     for copy in copies:
@@ -460,10 +504,10 @@
         return carry
 
     outs = []
-    parts = 4
+    parts = 8
     width = cells // parts
     for part in range(parts):
-        lax.fori_loop(part * width, (part + 1) * width, atoms, 0, unroll=16)
+        lax.fori_loop(part * width, (part + 1) * width, atoms, 0, unroll=8)
         rows = pl.ds(part * width, width)
         copy = pltpu.make_async_copy(potential_ref.at[rows], potential_hbm.at[rows], out_sems.at[part])
         copy.start()
@@ -489,9 +533,15 @@
             Shape((domains, KEEP // 2, 2, channels), BF),
             Shape((batches, ROWS, 128), BF),
         ),
-        in_specs=[SMEM] * 4 + [VMEM] * 2 + [ANY] * 3,
+        in_specs=[ANY] * 9,
         out_specs=(ANY, ANY),
         scratch_shapes=[
+            pltpu.SMEM(leaf_count.shape, I32),
+            pltpu.SMEM(fill.shape, I32),
+            pltpu.SMEM(wishes.shape, I32),
+            pltpu.SMEM(batch_class.shape, I32),
+            pltpu.VMEM(targets.shape, I32),
+            pltpu.VMEM(sources.shape, I32),
             pltpu.VMEM((cells, slots, channels), BF),
             pltpu.VMEM((coeffs, cells, slots), BF),
             pltpu.VMEM(ops_major.shape, BF),
@@ -505,6 +555,7 @@
             pltpu.VMEM((batches, batch_size), I32),
             pltpu.SMEM((batches, batch_size), I32),
             pltpu.SMEM((batches * batch_size + 2 * UNROLL + 2,), I32),
+            pltpu.SemaphoreType.DMA((6,)),
             pltpu.SemaphoreType.DMA((6,)),
             pltpu.SemaphoreType.DMA((5,)),
             pltpu.SemaphoreType.DMA((8,)),
@@ -582,7 +633,7 @@
             pltpu.VMEM((cells, slots, channels), BF),
             pltpu.SemaphoreType.DMA((3,)),
         ],
-        compiler_params=params(),
+        compiler_params=params(52),
         cost_estimate=pl.CostEstimate(flops=200_000_000, bytes_accessed=8_000_000, transcendentals=0),
         name="charge_atoms",
     )(asked, returned, own, atoms)
@@ -594,19 +645,19 @@
     return pl.pallas_call(
         far_kernel,
         out_shape=Shape((cells, slots, channels), BF),
-        in_specs=[SMEM] + [ANY] * 4,
+        in_specs=[ANY, VMEM] + [ANY] * 3,
         out_specs=ANY,
         scratch_shapes=[
-            pltpu.VMEM(incoming.shape, BF),
+            pltpu.SMEM(pairs.shape, I32),
             pltpu.VMEM(local_part.shape, F32),
             pltpu.VMEM((cells, slots, 128), BF),
             pltpu.VMEM(ops.shape, BF),
             pltpu.VMEM((cells + 1, ROWS, channels), F32),
             pltpu.VMEM((cells, slots, channels), BF),
-            pltpu.SemaphoreType.DMA((4,)),
-            pltpu.SemaphoreType.DMA((4,)),
+            pltpu.SemaphoreType.DMA((5,)),
+            pltpu.SemaphoreType.DMA((8,)),
         ],
-        compiler_params=params(),
+        compiler_params=params(50),
         name="far_pairs_atoms",
     )(pairs, incoming, local_part, atoms, ops)
 

time: 114 us -> 115 us (level); the launches traced: 114 us -> 113 us
  Pallas kernels: 52.4 us -> 47.9 us
  waiting for transfers between devices: 43.6 us -> 46.3 us
    all_to_all x1, waiting for transfers between devices: 17.2 us -> 19.9 us  [local(): lax.all_to_all(back, ('dx', 'dy'), split_axis=0, concat_axis=0, tiled=True)]
    pallas_call x1, Pallas kernels: 19.2 us -> 16.4 us  [call_beside(): pl.pallas_call(beside_kernel, out_shape=(Shape((cells, KEEP // 2, 2, chan...]
  transfers between devices with their start and end apart: 2 -> 2, of which waited for: 2 -> 2; matrix products, arithmetic and copies ran while one was open for 0% -> 0% of each run, Pallas kernels for 26% -> 23%
where the time goes in v5:
time: 115 us; the launch traced here: 113 us
  Pallas kernels  47.9 us (42%)
  waiting for transfers between devices  46.3 us (40%)
  starting transfers between devices  18.5 us (16%)
    all_to_all x1, waiting for transfers between devices, local(): lax.all_to_all(outgoing, ('dx', 'dy'), split_axis=0, concat_axis=0, tiled...  26.4 us
    all_to_all x1, waiting for transfers between devices, local(): lax.all_to_all(back, ('dx', 'dy'), split_axis=0, concat_axis=0, tiled=True)  19.9 us
    pallas_call x1, Pallas kernels, call_beside(): pl.pallas_call(beside_kernel, out_shape=(Shape((cells, KEEP // 2, 2, chan...  16.4 us
    all_to_all x1, starting transfers between devices, local(): lax.all_to_all(back, ('dx', 'dy'), split_axis=0, concat_axis=0, tiled=True)  12.9 us
    pallas_call x1, Pallas kernels, call_back(): pl.pallas_call(back_kernel, out_shape=(Shape((domains, KEEP // 2, 2, chan...  11.5 us
    pallas_call x1, Pallas kernels, call_charge(): pl.pallas_call(charge_kernel, out_shape=Shape((cells, slots, channels), B...  10.1 us
    pallas_call x1, Pallas kernels, call_far(): pl.pallas_call(far_kernel, out_shape=Shape((cells, slots, channels), BF),...  6.24 us
    all_to_all x1, starting transfers between devices, local(): lax.all_to_all(outgoing, ('dx', 'dy'), split_axis=0, concat_axis=0, tiled...  5.58 us
  transfers between devices with their start and end apart: 2, of which 2 were waited for; matrix products, arithmetic and copies ran while one was open for 0% of the time, Pallas kernels for 23%

profile of v5, /device:TPU:1, one launch (start us, length us, event | category | flops | bytes accessed | tf_op | source)
XLA Modules:
  0.0 113.4 jit_solution(14064349596365904593)
XLA Ops:
  0.6 11.5 %back_pairs.1 = (bf16[128,41,2,128]{3,2,1,0:T(2,128)(2,1)}, bf16[16,88,128]{2,1,0:T(8,128)(2,1)}) custom-call(s32[64]{0:T(128)} %count_ref.1, s32[16]{0:T(128)} %bitcast.14, s32[1,128]{1,0:T(1,128)} %bitcast.16, s32[16]{0:T(128)} %bitcast.17, s32[16,32]{1,0:T(8,128)} %bitcast.10, s32[16,32]{1,0:T(8,128)} %bitcast.12, bf16[64,128,128]{2,1,0:T(8,128)(2,1)} %cotangent_hbm.3, ...), custom_call_target="tpu_custom_call" | custom-call | tf_op jit(solution)/shard_map/back_pairs/pallas_call | solution.py:530
  12.2 12.9 %all-to-all-start = ((bf16[128,41,2,128]{3,2,1,0:T(2,128)(2,1)}), bf16[128,41,2,128]{3,2,1,0:T(2,128)(2,1)}, u32[]{:S(2)}, u32[]{:S(2)}) async-start(bf16[128,41,2,128]{3,2,1,0:T(2,128)(2,1)} %get-tuple-element.14), calls=%async_computation | async-start | bytes 5373952 | tf_op jit(solution)/shard_map/all_to_all | solution.py:683
  25.1 16.4 %own_pairs.1 = (bf16[64,41,2,128]{3,2,1,0:T(2,128)(2,1)}, f32[65,88,128]{2,1,0:T(8,128)}, f32[65,88,128]{2,1,0:T(8,128)}, bf16[64,128,128]{2,1,0:T(8,128)(2,1)}, s32[548]{0:T(1024)}) custom-call(s32[64]{0:T(128)} %count_ref.1, s32[16,32]{1,0:T(8,128)} %bitcast.11, s32[16,32]{1,0:T(8,128)} %bitcast.13, s32[16]{0:T(128)} %bitcast.15, ...), custom_call_target="tpu_custom_call" | custom-call | flops 400000000 | bytes 8000000 | tf_op jit(solution)/shard_map/own_pairs/pallas_call | solution.py:572
  41.5 19.9 %all-to-all-done.back_hbm.returned_hbm = bf16[128,41,2,128]{3,2,1,0:T(2,128)(2,1)} async-done(((bf16[128,41,2,128]{3,2,1,0:T(2,128)(2,1)}), bf16[128,41,2,128]{3,2,1,0:T(2,128)(2,1)}, u32[]{:S(2)}, u32[]{:S(2)}) %all-to-all-start) | async-done | bytes 2687008 | tf_op jit(solution)/shard_map/all_to_all | solution.py:683
  61.4 3.6 %pack_blocks.1 = (bf16[128,41,2,128]{3,2,1,0:T(2,128)(2,1)}, s32[1,128]{1,0:T(1,128)}) custom-call(bf16[64,41,2,128]{3,2,1,0:T(2,128)(2,1)} %get-tuple-element.13.mult_hbm, bf16[128,41,2,128]{3,2,1,0:T(2,128)(2,1)} %all-to-all-done.back_hbm.returned_hbm), custom_call_target="tpu_custom_call" | custom-call | tf_op jit(solution)/shard_map/pack_blocks/pallas_call | solution.py:605
  65.1 0.0 copy-start.3
  65.1 5.6 %all-to-all-start.1 = ((bf16[128,41,2,128]{3,2,1,0:T(2,128)(2,1)}), bf16[128,41,2,128]{3,2,1,0:T(2,128)(2,1)}, u32[]{:S(2)}, u32[]{:S(2)}) async-start(bf16[128,41,2,128]{3,2,1,0:T(2,128)(2,1)} %get-tuple-element.15), calls=%async_computation.1 | async-start | bytes 5373952 | tf_op jit(solution)/shard_map/all_to_all | solution.py:688
  70.7 0.0 copy-done.3
  70.7 0.0 copy-start
  70.7 0.0 copy-start.1
  70.7 0.0 copy-start.2
  70.7 10.1 %charge_atoms.1 = bf16[64,128,128]{2,1,0:T(8,128)(2,1)} custom-call(s32[1,128]{1,0:T(1,128)S(1)} %copy-done.3, bf16[128,41,2,128]{3,2,1,0:T(2,128)(2,1)} %all-to-all-done.back_hbm.returned_hbm, f32[65,88,128]{2,1,0:T(8,128)} %get-tuple-element.19.own_hbm, bf16[64,128,128]{2,1,0:T(8,128)(2,1)} %get-tuple-element.17.atoms_hbm), custom_call_target="tpu_custom_call" | custom-call | flops 200000000 | bytes 8000000 | tf_op jit(solution)/shard_map/charge_atoms/pallas_call | solution.py:624
  80.8 26.4 %all-to-all-done.1.incoming_ref = bf16[128,41,2,128]{3,2,1,0:T(2,128)(2,1)} async-done(((bf16[128,41,2,128]{3,2,1,0:T(2,128)(2,1)}), bf16[128,41,2,128]{3,2,1,0:T(2,128)(2,1)}, u32[]{:S(2)}, u32[]{:S(2)}) %all-to-all-start.1) | async-done | bytes 2687008 | tf_op jit(solution)/shard_map/all_to_all | solution.py:688
  107.2 0.0 copy-done
  107.2 0.0 copy-done.1
  107.2 0.0 copy-done.2
  107.2 6.2 %far_pairs_atoms.1 = bf16[64,128,128]{2,1,0:T(8,128)(2,1)} custom-call(s32[548]{0:T(1024)S(1)} %copy-done.2, bf16[128,41,2,128]{3,2,1,0:T(2,128)(2,1)} %all-to-all-done.1.incoming_ref, f32[65,88,128]{2,1,0:T(8,128)} %get-tuple-element.16.local_hbm, bf16[64,128,128]{2,1,0:T(8,128)(2,1)S(1)} %copy-done, bf16[16,88,128]{2,1,0:T(8,128)(2,1)S(1)} %copy-done.1), custom_call_target="tpu_custom_call" | custom-call | tf_op jit(solution)/shard_map/far_pairs_atoms/pallas_call | solution.py:645
Async XLA Ops:
  12.2 49.3 %all-to-all-start = ((bf16[128,41,2,128]{3,2,1,0:T(2,128)(2,1)}), bf16[128,41,2,128]{3,2,1,0:T(2,128)(2,1)}, u32[]{:S(2)}, u32[]{:S(2)}) async-start(bf16[128,41,2,128]{3,2,1,0:T(2,128)(2,1)} %get-tuple-element.14), calls=%async_computation | async-start | bytes 5373952 | tf_op jit(solution)/shard_map/all_to_all | solution.py:683
  65.1 5.6 %copy-start.3 = (s32[1,128]{1,0:T(1,128)S(1)}, s32[1,128]{1,0:T(1,128)}, u32[]{:S(2)}) copy-start(s32[1,128]{1,0:T(1,128)} %get-tuple-element.18.asked_ref) | copy-start | bytes 1540
  65.1 42.1 %all-to-all-start.1 = ((bf16[128,41,2,128]{3,2,1,0:T(2,128)(2,1)}), bf16[128,41,2,128]{3,2,1,0:T(2,128)(2,1)}, u32[]{:S(2)}, u32[]{:S(2)}) async-start(bf16[128,41,2,128]{3,2,1,0:T(2,128)(2,1)} %get-tuple-element.15), calls=%async_computation.1 | async-start | bytes 5373952 | tf_op jit(solution)/shard_map/all_to_all | solution.py:688
  70.7 36.5 %copy-start = (bf16[64,128,128]{2,1,0:T(8,128)(2,1)S(1)}, bf16[64,128,128]{2,1,0:T(8,128)(2,1)}, u32[]{:S(2)}) copy-start(bf16[64,128,128]{2,1,0:T(8,128)(2,1)} %get-tuple-element.17.atoms_hbm) | copy-start | bytes 6291460
  70.7 36.5 %copy-start.1 = (bf16[16,88,128]{2,1,0:T(8,128)(2,1)S(1)}, bf16[16,88,128]{2,1,0:T(8,128)(2,1)}, u32[]{:S(2)}) copy-start(bf16[16,88,128]{2,1,0:T(8,128)(2,1)} %get-tuple-element.11.op_ref.op_hbm) | copy-start | bytes 1081348
  70.7 36.5 %copy-start.2 = (s32[548]{0:T(1024)S(1)}, s32[548]{0:T(1024)}, u32[]{:S(2)}) copy-start(s32[548]{0:T(1024)} %get-tuple-element.12.list_hbm) | copy-start | bytes 6580

commit v6 on v5

--- a/solution.py
+++ b/solution.py
@@ -657,7 +657,7 @@
             pltpu.SemaphoreType.DMA((5,)),
             pltpu.SemaphoreType.DMA((8,)),
         ],
-        compiler_params=params(50),
+        compiler_params=params(49),
         name="far_pairs_atoms",
     )(pairs, incoming, local_part, atoms, ops)
 

time: 115 us -> 114 us (level); the launches traced: 113 us -> 115 us
  Pallas kernels: 47.9 us -> 55.3 us
  waiting for transfers between devices: 46.3 us -> 41.9 us
  starting transfers between devices: 18.5 us -> 16 us
  local copies, waits for them, and re-layouts: 0.02 us -> 1.6 us
    all_to_all x1, waiting for transfers between devices: 19.9 us -> 15.1 us  [local(): lax.all_to_all(back, ('dx', 'dy'), split_axis=0, concat_axis=0, tiled=True)]
    pallas_call x1, Pallas kernels: 16.4 us -> 21.3 us  [call_beside(): pl.pallas_call(beside_kernel, out_shape=(Shape((cells, KEEP // 2, 2, chan...]
    pallas_call x1, Pallas kernels: 11.5 us -> 13.5 us  [call_back(): pl.pallas_call(back_kernel, out_shape=(Shape((domains, KEEP // 2, 2, chan...]
    unnamed x8, local copies, waits for them, and re-layouts: 0.02 us -> 1.6 us
    all_to_all x1, starting transfers between devices: 12.9 us -> 11.4 us  [local(): lax.all_to_all(back, ('dx', 'dy'), split_axis=0, concat_axis=0, tiled=True)]
  transfers between devices with their start and end apart: 2 -> 2, of which waited for: 2 -> 2; matrix products, arithmetic and copies ran while one was open for 0% -> 0% of each run, Pallas kernels for 23% -> 27%
where the time goes in v6:
time: 114 us; the launch traced here: 115 us
  Pallas kernels  55.3 us (49%)
  waiting for transfers between devices  41.9 us (37%)
  starting transfers between devices  16 us (14%)
  local copies, waits for them, and re-layouts  1.6 us (1%)
    all_to_all x1, waiting for transfers between devices, local(): lax.all_to_all(outgoing, ('dx', 'dy'), split_axis=0, concat_axis=0, tiled...  26.8 us
    pallas_call x1, Pallas kernels, call_beside(): pl.pallas_call(beside_kernel, out_shape=(Shape((cells, KEEP // 2, 2, chan...  21.3 us
    all_to_all x1, waiting for transfers between devices, local(): lax.all_to_all(back, ('dx', 'dy'), split_axis=0, concat_axis=0, tiled=True)  15.1 us
    pallas_call x1, Pallas kernels, call_back(): pl.pallas_call(back_kernel, out_shape=(Shape((domains, KEEP // 2, 2, chan...  13.5 us
    all_to_all x1, starting transfers between devices, local(): lax.all_to_all(back, ('dx', 'dy'), split_axis=0, concat_axis=0, tiled=True)  11.4 us
    pallas_call x1, Pallas kernels, call_charge(): pl.pallas_call(charge_kernel, out_shape=Shape((cells, slots, channels), B...  9.94 us
    pallas_call x1, Pallas kernels, call_far(): pl.pallas_call(far_kernel, out_shape=Shape((cells, slots, channels), BF),...  6.95 us
    all_to_all x1, starting transfers between devices, local(): lax.all_to_all(outgoing, ('dx', 'dy'), split_axis=0, concat_axis=0, tiled...  4.57 us
  transfers between devices with their start and end apart: 2, of which 2 were waited for; matrix products, arithmetic and copies ran while one was open for 0% of the time, Pallas kernels for 27%

profile of v6, /device:TPU:1, one launch (start us, length us, event | category | flops | bytes accessed | tf_op | source)
XLA Modules:
  0.0 115.5 jit_solution(446861281218486696)
XLA Ops:
  0.6 13.5 %back_pairs.1 = (bf16[128,41,2,128]{3,2,1,0:T(2,128)(2,1)}, bf16[16,88,128]{2,1,0:T(8,128)(2,1)}) custom-call(s32[64]{0:T(128)} %count_ref.1, s32[16]{0:T(128)} %bitcast.14, s32[1,128]{1,0:T(1,128)} %bitcast.16, s32[16]{0:T(128)} %bitcast.17, s32[16,32]{1,0:T(8,128)} %bitcast.10, s32[16,32]{1,0:T(8,128)} %bitcast.12, bf16[64,128,128]{2,1,0:T(8,128)(2,1)} %cotangent_hbm.3, ...), custom_call_target="tpu_custom_call" | custom-call | tf_op jit(solution)/shard_map/back_pairs/pallas_call | solution.py:530
  14.2 11.4 %all-to-all-start = ((bf16[128,41,2,128]{3,2,1,0:T(2,128)(2,1)}), bf16[128,41,2,128]{3,2,1,0:T(2,128)(2,1)}, u32[]{:S(2)}, u32[]{:S(2)}) async-start(bf16[128,41,2,128]{3,2,1,0:T(2,128)(2,1)} %get-tuple-element.14), calls=%async_computation | async-start | bytes 5373952 | tf_op jit(solution)/shard_map/all_to_all | solution.py:683
  25.5 21.3 %own_pairs.1 = (bf16[64,41,2,128]{3,2,1,0:T(2,128)(2,1)}, f32[65,88,128]{2,1,0:T(8,128)}, f32[65,88,128]{2,1,0:T(8,128)}, bf16[64,128,128]{2,1,0:T(8,128)(2,1)}, s32[548]{0:T(1024)}) custom-call(s32[64]{0:T(128)} %count_ref.1, s32[16,32]{1,0:T(8,128)} %bitcast.11, s32[16,32]{1,0:T(8,128)} %bitcast.13, s32[16]{0:T(128)} %bitcast.15, ...), custom_call_target="tpu_custom_call" | custom-call | flops 400000000 | bytes 8000000 | tf_op jit(solution)/shard_map/own_pairs/pallas_call | solution.py:572
  46.9 15.1 %all-to-all-done.back_hbm.returned_hbm = bf16[128,41,2,128]{3,2,1,0:T(2,128)(2,1)} async-done(((bf16[128,41,2,128]{3,2,1,0:T(2,128)(2,1)}), bf16[128,41,2,128]{3,2,1,0:T(2,128)(2,1)}, u32[]{:S(2)}, u32[]{:S(2)}) %all-to-all-start) | async-done | bytes 2687008 | tf_op jit(solution)/shard_map/all_to_all | solution.py:683
  61.9 3.6 %pack_blocks.1 = (bf16[128,41,2,128]{3,2,1,0:T(2,128)(2,1)}, s32[1,128]{1,0:T(1,128)}) custom-call(bf16[64,41,2,128]{3,2,1,0:T(2,128)(2,1)} %get-tuple-element.13.mult_hbm, bf16[128,41,2,128]{3,2,1,0:T(2,128)(2,1)} %all-to-all-done.back_hbm.returned_hbm), custom_call_target="tpu_custom_call" | custom-call | tf_op jit(solution)/shard_map/pack_blocks/pallas_call | solution.py:605
  65.5 0.0 copy-start.3
  65.5 4.6 %all-to-all-start.1 = ((bf16[128,41,2,128]{3,2,1,0:T(2,128)(2,1)}), bf16[128,41,2,128]{3,2,1,0:T(2,128)(2,1)S(1)}, u32[]{:S(2)}, u32[]{:S(2)}) async-start(bf16[128,41,2,128]{3,2,1,0:T(2,128)(2,1)} %get-tuple-element.15), calls=%async_computation.1 | async-start | bytes 5373952 | tf_op jit(solution)/shard_map/all_to_all | solution.py:688
  70.1 0.0 copy-done.3
  70.1 0.0 copy-start.1
  70.1 0.0 copy-start.2
  70.1 9.9 %charge_atoms.1 = bf16[64,128,128]{2,1,0:T(8,128)(2,1)} custom-call(s32[1,128]{1,0:T(1,128)S(1)} %copy-done.3, bf16[128,41,2,128]{3,2,1,0:T(2,128)(2,1)} %all-to-all-done.back_hbm.returned_hbm, f32[65,88,128]{2,1,0:T(8,128)} %get-tuple-element.19.own_hbm, bf16[64,128,128]{2,1,0:T(8,128)(2,1)} %get-tuple-element.17.atoms_hbm), custom_call_target="tpu_custom_call" | custom-call | flops 200000000 | bytes 8000000 | tf_op jit(solution)/shard_map/charge_atoms/pallas_call | solution.py:624
  80.1 26.8 %all-to-all-done.1.incoming_ref = bf16[128,41,2,128]{3,2,1,0:T(2,128)(2,1)S(1)} async-done(((bf16[128,41,2,128]{3,2,1,0:T(2,128)(2,1)}), bf16[128,41,2,128]{3,2,1,0:T(2,128)(2,1)S(1)}, u32[]{:S(2)}, u32[]{:S(2)}) %all-to-all-start.1) | async-done | bytes 2687008 | tf_op jit(solution)/shard_map/all_to_all | solution.py:688
  106.9 0.0 copy-done.1
  106.9 0.0 copy-done.2
  106.9 0.0 copy-start
  106.9 1.6 %copy-done = bf16[64,128,128]{2,1,0:T(8,128)(2,1)S(1)} copy-done((bf16[64,128,128]{2,1,0:T(8,128)(2,1)S(1)}, bf16[64,128,128]{2,1,0:T(8,128)(2,1)}, u32[]{:S(2)}) %copy-start) | copy-done | bytes 2097176
  108.5 6.9 %far_pairs_atoms.1 = bf16[64,128,128]{2,1,0:T(8,128)(2,1)} custom-call(s32[548]{0:T(1024)S(1)} %copy-done.2, bf16[128,41,2,128]{3,2,1,0:T(2,128)(2,1)S(1)} %all-to-all-done.1.incoming_ref, f32[65,88,128]{2,1,0:T(8,128)} %get-tuple-element.16.local_hbm, bf16[64,128,128]{2,1,0:T(8,128)(2,1)S(1)} %copy-done, bf16[16,88,128]{2,1,0:T(8,128)(2,1)S(1)} %copy-done.1), custom_call_target="tpu_custom_call" | custom-call | tf_op jit(solution)/shard_map/far_pairs_atoms/pallas_call | solution.py:645
Async XLA Ops:
  14.2 47.8 %all-to-all-start = ((bf16[128,41,2,128]{3,2,1,0:T(2,128)(2,1)}), bf16[128,41,2,128]{3,2,1,0:T(2,128)(2,1)}, u32[]{:S(2)}, u32[]{:S(2)}) async-start(bf16[128,41,2,128]{3,2,1,0:T(2,128)(2,1)} %get-tuple-element.14), calls=%async_computation | async-start | bytes 5373952 | tf_op jit(solution)/shard_map/all_to_all | solution.py:683
  65.5 4.6 %copy-start.3 = (s32[1,128]{1,0:T(1,128)S(1)}, s32[1,128]{1,0:T(1,128)}, u32[]{:S(2)}) copy-start(s32[1,128]{1,0:T(1,128)} %get-tuple-element.18.asked_ref) | copy-start | bytes 1540
  65.5 41.4 %all-to-all-start.1 = ((bf16[128,41,2,128]{3,2,1,0:T(2,128)(2,1)}), bf16[128,41,2,128]{3,2,1,0:T(2,128)(2,1)S(1)}, u32[]{:S(2)}, u32[]{:S(2)}) async-start(bf16[128,41,2,128]{3,2,1,0:T(2,128)(2,1)} %get-tuple-element.15), calls=%async_computation.1 | async-start | bytes 5373952 | tf_op jit(solution)/shard_map/all_to_all | solution.py:688
  70.1 36.8 %copy-start.1 = (bf16[16,88,128]{2,1,0:T(8,128)(2,1)S(1)}, bf16[16,88,128]{2,1,0:T(8,128)(2,1)}, u32[]{:S(2)}) copy-start(bf16[16,88,128]{2,1,0:T(8,128)(2,1)} %get-tuple-element.11.op_ref.op_hbm) | copy-start | bytes 1081348
  70.1 36.8 %copy-start.2 = (s32[548]{0:T(1024)S(1)}, s32[548]{0:T(1024)}, u32[]{:S(2)}) copy-start(s32[548]{0:T(1024)} %get-tuple-element.12.list_hbm) | copy-start | bytes 6580
  106.9 1.6 %copy-start = (bf16[64,128,128]{2,1,0:T(8,128)(2,1)S(1)}, bf16[64,128,128]{2,1,0:T(8,128)(2,1)}, u32[]{:S(2)}) copy-start(bf16[64,128,128]{2,1,0:T(8,128)(2,1)} %get-tuple-element.17.atoms_hbm) | copy-start | bytes 6291460

commit v7 on v6

--- a/solution.py
+++ b/solution.py
@@ -422,7 +422,7 @@
     remote = returned_ref.shape[0]
     copies = [
         pltpu.make_async_copy(src, dst, sems.at[k])
-        for k, (src, dst) in enumerate(((own_hbm, own_ref), (returned_hbm, returned_ref), (atoms_hbm, atoms_ref)))
+        for k, (src, dst) in enumerate(((own_hbm, own_ref), (returned_hbm, returned_ref), (atoms_hbm.at[pl.ds(0, cells)], atoms_ref)))
     ]
     for copy in copies:
         copy.start()
@@ -471,8 +471,8 @@
             (
                 (list_hbm, list_ref, 1),
                 (op_hbm, op_ref, 2),
-                (atoms_hbm, atoms_ref, 4),
-                (local_hbm, local_ref, 5),
+                (atoms_hbm.at[pl.ds(0, cells)], atoms_ref, 4),
+                (local_hbm.at[pl.ds(0, cells)], local_ref, 4),
             )
         )
     ]
@@ -573,9 +573,9 @@
         beside_kernel,
         out_shape=(
             Shape((cells, KEEP // 2, 2, channels), BF),
+            Shape((2 * cells, ROWS, channels), F32),
             Shape((cells + 1, ROWS, channels), F32),
-            Shape((cells + 1, ROWS, channels), F32),
-            Shape((cells, slots, 128), BF),
+            Shape((2 * cells, slots, 128), BF),
             Shape((batches * batch_size + 2 * UNROLL + 4,), I32),
         ),
         in_specs=[SMEM] * 4 + [ANY] * 3 + [VMEM],
@@ -619,7 +619,7 @@
 
 
 def call_charge(asked, returned, own, atoms):
-    cells, slots, _ = atoms.shape
+    cells, slots = own.shape[0] - 1, atoms.shape[1]
     channels = returned.shape[3]
     return pl.pallas_call(
         charge_kernel,
@@ -640,7 +640,7 @@
 
 
 def call_far(pairs, incoming, local_part, atoms, ops):
-    cells, slots, _ = atoms.shape
+    cells, slots = atoms.shape[0] // 2, atoms.shape[1]
     channels = incoming.shape[3]
     return pl.pallas_call(
         far_kernel,
@@ -649,7 +649,7 @@
         out_specs=ANY,
         scratch_shapes=[
             pltpu.SMEM(pairs.shape, I32),
-            pltpu.VMEM(local_part.shape, F32),
+            pltpu.VMEM((cells, ROWS, channels), F32),
             pltpu.VMEM((cells, slots, 128), BF),
             pltpu.VMEM(ops.shape, BF),
             pltpu.VMEM((cells + 1, ROWS, channels), F32),

time: 114 us -> 112 us (0.982); the launches traced: 115 us -> 112 us
  Pallas kernels: 55.3 us -> 51.7 us
  local copies, waits for them, and re-layouts: 1.6 us -> 0.01 us
    unnamed x8 -> x6, local copies, waits for them, and re-layouts: 1.6 us -> 0.01 us
    pallas_call x1, Pallas kernels: 6.95 us -> 5.36 us  [call_far(): pl.pallas_call(far_kernel, out_shape=Shape((cells, slots, channels), BF),...]
where the time goes in v7:
time: 112 us
  Pallas kernels  51.7 us (46%)
  waiting for transfers between devices  42.7 us (38%)
  starting transfers between devices  16.9 us (15%)
    all_to_all x1, waiting for transfers between devices, local(): lax.all_to_all(outgoing, ('dx', 'dy'), split_axis=0, concat_axis=0, tiled...  26.8 us
    pallas_call x1, Pallas kernels, call_beside(): pl.pallas_call(beside_kernel, out_shape=(Shape((cells, KEEP // 2, 2, chan...  20.6 us
    all_to_all x1, waiting for transfers between devices, local(): lax.all_to_all(back, ('dx', 'dy'), split_axis=0, concat_axis=0, tiled=True)  15.8 us
    pallas_call x1, Pallas kernels, call_back(): pl.pallas_call(back_kernel, out_shape=(Shape((domains, KEEP // 2, 2, chan...  12.4 us
    all_to_all x1, starting transfers between devices, local(): lax.all_to_all(back, ('dx', 'dy'), split_axis=0, concat_axis=0, tiled=True)  12.3 us
    pallas_call x1, Pallas kernels, call_charge(): pl.pallas_call(charge_kernel, out_shape=Shape((cells, slots, channels), B...  9.94 us
    pallas_call x1, Pallas kernels, call_far(): pl.pallas_call(far_kernel, out_shape=Shape((cells, slots, channels), BF),...  5.36 us
    all_to_all x1, starting transfers between devices, local(): lax.all_to_all(outgoing, ('dx', 'dy'), split_axis=0, concat_axis=0, tiled...  4.57 us
  transfers between devices with their start and end apart: 2, of which 2 were waited for; matrix products, arithmetic and copies ran while one was open for 0% of the time, Pallas kernels for 27%

profile of v7, /device:TPU:1, one launch (start us, length us, event | category | flops | bytes accessed | tf_op | source)
XLA Modules:
  0.0 112.0 jit_solution(5658378631183336957)
XLA Ops:
  0.6 12.4 %back_pairs.1 = (bf16[128,41,2,128]{3,2,1,0:T(2,128)(2,1)}, bf16[16,88,128]{2,1,0:T(8,128)(2,1)}) custom-call(s32[64]{0:T(128)} %count_ref.1, s32[16]{0:T(128)} %bitcast.14, s32[1,128]{1,0:T(1,128)} %bitcast.16, s32[16]{0:T(128)} %bitcast.17, s32[16,32]{1,0:T(8,128)} %bitcast.10, s32[16,32]{1,0:T(8,128)} %bitcast.12, bf16[64,128,128]{2,1,0:T(8,128)(2,1)} %cotangent_hbm.3, ...), custom_call_target="tpu_custom_call" | custom-call | tf_op jit(solution)/shard_map/back_pairs/pallas_call | solution.py:530
  13.0 12.3 %all-to-all-start = ((bf16[128,41,2,128]{3,2,1,0:T(2,128)(2,1)}), bf16[128,41,2,128]{3,2,1,0:T(2,128)(2,1)}, u32[]{:S(2)}, u32[]{:S(2)}) async-start(bf16[128,41,2,128]{3,2,1,0:T(2,128)(2,1)} %get-tuple-element.14), calls=%async_computation | async-start | bytes 5373952 | tf_op jit(solution)/shard_map/all_to_all | solution.py:683
  25.4 20.6 %own_pairs.1 = (bf16[64,41,2,128]{3,2,1,0:T(2,128)(2,1)}, f32[128,88,128]{2,1,0:T(8,128)}, f32[65,88,128]{2,1,0:T(8,128)}, bf16[128,128,128]{2,1,0:T(8,128)(2,1)}, s32[548]{0:T(1024)}) custom-call(s32[64]{0:T(128)} %count_ref.1, s32[16,32]{1,0:T(8,128)} %bitcast.11, s32[16,32]{1,0:T(8,128)} %bitcast.13, s32[16]{0:T(128)} %bitcast.15, ...), custom_call_target="tpu_custom_call" | custom-call | flops 400000000 | bytes 8000000 | tf_op jit(solution)/shard_map/own_pairs/pallas_call | solution.py:572
  45.9 15.8 %all-to-all-done.back_hbm.returned_hbm = bf16[128,41,2,128]{3,2,1,0:T(2,128)(2,1)} async-done(((bf16[128,41,2,128]{3,2,1,0:T(2,128)(2,1)}), bf16[128,41,2,128]{3,2,1,0:T(2,128)(2,1)}, u32[]{:S(2)}, u32[]{:S(2)}) %all-to-all-start) | async-done | bytes 2687008 | tf_op jit(solution)/shard_map/all_to_all | solution.py:683
  61.7 3.5 %pack_blocks.1 = (bf16[128,41,2,128]{3,2,1,0:T(2,128)(2,1)}, s32[1,128]{1,0:T(1,128)}) custom-call(bf16[64,41,2,128]{3,2,1,0:T(2,128)(2,1)} %get-tuple-element.13.mult_hbm, bf16[128,41,2,128]{3,2,1,0:T(2,128)(2,1)} %all-to-all-done.back_hbm.returned_hbm), custom_call_target="tpu_custom_call" | custom-call | tf_op jit(solution)/shard_map/pack_blocks/pallas_call | solution.py:605
  65.3 0.0 copy-start.2
  65.3 4.6 %all-to-all-start.1 = ((bf16[128,41,2,128]{3,2,1,0:T(2,128)(2,1)}), bf16[128,41,2,128]{3,2,1,0:T(2,128)(2,1)S(1)}, u32[]{:S(2)}, u32[]{:S(2)}) async-start(bf16[128,41,2,128]{3,2,1,0:T(2,128)(2,1)} %get-tuple-element.15), calls=%async_computation.1 | async-start | bytes 5373952 | tf_op jit(solution)/shard_map/all_to_all | solution.py:688
  69.8 0.0 copy-done.2
  69.9 0.0 copy-start
  69.9 0.0 copy-start.1
  69.9 9.9 %charge_atoms.1 = bf16[64,128,128]{2,1,0:T(8,128)(2,1)} custom-call(s32[1,128]{1,0:T(1,128)S(1)} %copy-done.2, bf16[128,41,2,128]{3,2,1,0:T(2,128)(2,1)} %all-to-all-done.back_hbm.returned_hbm, f32[65,88,128]{2,1,0:T(8,128)} %get-tuple-element.19.own_hbm, bf16[128,128,128]{2,1,0:T(8,128)(2,1)} %get-tuple-element.17.atoms_hbm), custom_call_target="tpu_custom_call" | custom-call | flops 200000000 | bytes 8000000 | tf_op jit(solution)/shard_map/charge_atoms/pallas_call | solution.py:624
  79.8 26.8 %all-to-all-done.1.incoming_ref = bf16[128,41,2,128]{3,2,1,0:T(2,128)(2,1)S(1)} async-done(((bf16[128,41,2,128]{3,2,1,0:T(2,128)(2,1)}), bf16[128,41,2,128]{3,2,1,0:T(2,128)(2,1)S(1)}, u32[]{:S(2)}, u32[]{:S(2)}) %all-to-all-start.1) | async-done | bytes 2687008 | tf_op jit(solution)/shard_map/all_to_all | solution.py:688
  106.7 0.0 copy-done
  106.7 0.0 copy-done.1
  106.7 5.4 %far_pairs_atoms.1 = bf16[64,128,128]{2,1,0:T(8,128)(2,1)} custom-call(s32[548]{0:T(1024)S(1)} %copy-done.1, bf16[128,41,2,128]{3,2,1,0:T(2,128)(2,1)S(1)} %all-to-all-done.1.incoming_ref, f32[128,88,128]{2,1,0:T(8,128)} %get-tuple-element.16.local_hbm, bf16[128,128,128]{2,1,0:T(8,128)(2,1)} %get-tuple-element.17.atoms_hbm, bf16[16,88,128]{2,1,0:T(8,128)(2,1)S(1)} %copy-done), custom_call_target="tpu_custom_call" | custom-call | tf_op jit(solution)/shard_map/far_pairs_atoms/pallas_call | solution.py:645
Async XLA Ops:
  13.0 48.7 %all-to-all-start = ((bf16[128,41,2,128]{3,2,1,0:T(2,128)(2,1)}), bf16[128,41,2,128]{3,2,1,0:T(2,128)(2,1)}, u32[]{:S(2)}, u32[]{:S(2)}) async-start(bf16[128,41,2,128]{3,2,1,0:T(2,128)(2,1)} %get-tuple-element.14), calls=%async_computation | async-start | bytes 5373952 | tf_op jit(solution)/shard_map/all_to_all | solution.py:683
  65.3 4.6 %copy-start.2 = (s32[1,128]{1,0:T(1,128)S(1)}, s32[1,128]{1,0:T(1,128)}, u32[]{:S(2)}) copy-start(s32[1,128]{1,0:T(1,128)} %get-tuple-element.18.asked_ref) | copy-start | bytes 1540
  65.3 41.4 %all-to-all-start.1 = ((bf16[128,41,2,128]{3,2,1,0:T(2,128)(2,1)}), bf16[128,41,2,128]{3,2,1,0:T(2,128)(2,1)S(1)}, u32[]{:S(2)}, u32[]{:S(2)}) async-start(bf16[128,41,2,128]{3,2,1,0:T(2,128)(2,1)} %get-tuple-element.15), calls=%async_computation.1 | async-start | bytes 5373952 | tf_op jit(solution)/shard_map/all_to_all | solution.py:688
  69.9 36.8 %copy-start = (bf16[16,88,128]{2,1,0:T(8,128)(2,1)S(1)}, bf16[16,88,128]{2,1,0:T(8,128)(2,1)}, u32[]{:S(2)}) copy-start(bf16[16,88,128]{2,1,0:T(8,128)(2,1)} %get-tuple-element.11.op_ref.op_hbm) | copy-start | bytes 1081348
  69.9 36.8 %copy-start.1 = (s32[548]{0:T(1024)S(1)}, s32[548]{0:T(1024)}, u32[]{:S(2)}) copy-start(s32[548]{0:T(1024)} %get-tuple-element.12.list_hbm) | copy-start | bytes 6580
